TPU v7x, 256 devices: a whole 4x4x8 slice. The times are simulated.
256 devices in a mesh: gx: 8 (over x, core), gy: 32 (over y, z).
Axes of the slice: x: 4, y: 4, z: 8, core: 2. Of those that a mesh axis runs over, the one named last changes fastest.
Arguments:
- state: float32 [4, 2, 256, 4096], P(None, None, 'gx', 'gy'), may hold values from -3.5 to 3.5
- diffusivity: float32 [2, 256, 4096], P(None, 'gx', 'gy'), may hold values from 1 to 4
- sea_mask: int32 [256, 4096], P('gx', 'gy'), may hold values 0 or 1
- depth_index: int32 [256, 4096], P('gx', 'gy'), may hold values from 1 to 2
- closure_in: float32 [64, 9], replicated, may hold values from -2.5 to 2.5
- closure_out: float32 [64], replicated, may hold values from -0.75 to 0.75
- cotangent: float32 [4, 2, 256, 4096], P(None, None, 'gx', 'gy'), may hold values from -6 to 6
Outputs:
- final_state: float32 [4, 2, 256, 4096], P(None, None, 'gx', 'gy')
- state_grad: float32 [4, 2, 256, 4096], P(None, None, 'gx', 'gy')
- closure_grad: float32 [64, 10], replicated
All inputs are finite; a program needn't handle non-finite values. No bound on the sum of `sea_mask` on one device may be relied on, other than what follows from the above.
Results may differ from a plain program's by a relative error of at most 0.0005.
Values sent between devices are 32-bit elements; how exact they have to be, the bound alone decides.
No kernel may reach another device: no remote copies, remote signals or barrier semaphores. Data moves between devices by JAX's collectives and lax.ppermute only.
A program may use at most 64 MiB of HBM per device.

v0:
```python
from functools import partial
import math

import jax
import jax.numpy as jnp
from jax import lax
from jax.sharding import PartitionSpec as P

FEAT = 8
DIFFUSE = 2048


def extended(block, sides, width):
    for axis, dim in sides:
        count = lax.axis_size(axis)
        forward = [(i, i + 1) for i in range(count - 1)]
        backward = [(target, source) for source, target in forward]
        low = lax.ppermute(
            lax.slice_in_dim(block, block.shape[dim] - width, None, axis=dim), axis, forward
        )
        high = lax.ppermute(lax.slice_in_dim(block, 0, width, axis=dim), axis, backward)
        block = jnp.concatenate([low, block, high], axis=dim)
    return block


def closure_level(grads, closure_in, closure_out):
    preact = jnp.einsum("hc,cxy->hxy", closure_in[:, :FEAT], grads, precision=lax.Precision.HIGHEST)
    hidden = jnp.tanh(preact + closure_in[:, FEAT][:, None, None])
    mixed = jnp.einsum("h,hxy->xy", closure_out, hidden, precision=lax.Precision.HIGHEST)
    return 0.24 * jax.nn.sigmoid(mixed)


def explicit(padded, closure_in, closure_out, wet, coriolis):
    center = padded[:, :, 1:-1, 1:-1]
    east = padded[:, :, 2:, 1:-1]
    west = padded[:, :, :-2, 1:-1]
    north = padded[:, :, 1:-1, 2:]
    south = padded[:, :, 1:-1, :-2]
    slope_x = 0.5 * (east - west)
    slope_y = 0.5 * (north - south)
    curve_x = east - 2.0 * center + west
    curve_y = north - 2.0 * center + south
    speed_u = center[0]
    speed_v = center[1]
    upwind = (
        speed_u * slope_x
        + speed_v * slope_y
        - 0.5
        * (
            jnp.sqrt(speed_u * speed_u + 0.01) * curve_x
            + jnp.sqrt(speed_v * speed_v + 0.01) * curve_y
        )
    )
    features = jnp.moveaxis(jnp.concatenate([slope_x, slope_y], 0), 1, 0)

    def level_viscosity(grads):
        return closure_level(grads, closure_in, closure_out)

    viscosity = lax.map(jax.checkpoint(level_viscosity), features)
    mixing = curve_x + curve_y
    moment_u = speed_u - 0.3 * upwind[0] + viscosity * mixing[0] + 0.3 * coriolis * speed_v
    moment_v = speed_v - 0.3 * upwind[1] + viscosity * mixing[1] - 0.3 * coriolis * speed_u
    tracers = center[2:] - 0.3 * upwind[2:]
    return wet[None] * jnp.concatenate([moment_u[None], moment_v[None], tracers], 0)


def lower(values, stride, fill, axis):
    length = values.shape[axis]
    kept = lax.slice_in_dim(values, 0, length - stride, axis=axis)
    widths = [(0, 0)] * values.ndim
    widths[axis] = (stride, 0)
    return jnp.pad(kept, widths, constant_values=fill)


def higher(values, stride, fill, axis):
    length = values.shape[axis]
    kept = lax.slice_in_dim(values, stride, length, axis=axis)
    widths = [(0, 0)] * values.ndim
    widths[axis] = (0, stride)
    return jnp.pad(kept, widths, constant_values=fill)


def line_reduce(sub_diag, main_diag, super_diag, rhs_stack):
    length = main_diag.shape[2]
    stride = 1
    while stride < length:
        sub_below = lower(sub_diag, stride, 0.0, 2)
        main_below = lower(main_diag, stride, 1.0, 2)
        super_below = lower(super_diag, stride, 0.0, 2)
        rhs_below = lower(rhs_stack, stride, 0.0, 3)
        sub_above = higher(sub_diag, stride, 0.0, 2)
        main_above = higher(main_diag, stride, 1.0, 2)
        super_above = higher(super_diag, stride, 0.0, 2)
        rhs_above = higher(rhs_stack, stride, 0.0, 3)
        left_mult = -sub_diag / main_below
        right_mult = -super_diag / main_above
        main_diag = main_diag + left_mult * super_below + right_mult * sub_above
        sub_diag = left_mult * sub_below
        super_diag = right_mult * super_above
        rhs_stack = rhs_stack + left_mult * rhs_below + right_mult * rhs_above
        stride = stride * 2
    return rhs_stack / main_diag


def block_product(left_block, right_block):
    return (
        left_block[:, 0][:, None] * right_block[0][None]
        + left_block[:, 1][:, None] * right_block[1][None]
    )


def block_apply(matrix, vector):
    return matrix[:, 0] * vector[0] + matrix[:, 1] * vector[1]


def block_inverse(matrix):
    determinant = matrix[0, 0] * matrix[1, 1] - matrix[0, 1] * matrix[1, 0]
    first_row = jnp.stack([matrix[1, 1], -matrix[0, 1]])
    second_row = jnp.stack([-matrix[1, 0], matrix[0, 0]])
    return jnp.stack([first_row, second_row]) / determinant


def block_steps(lower_blk, upper_blk, right_side, count, neighbors):
    tail = lower_blk.shape[2:]
    unit_block = jnp.eye(2, dtype=jnp.float32).reshape((2, 2) + (1,) * len(tail))
    main_blk = jnp.broadcast_to(unit_block, lower_blk.shape)
    stride = 1
    while stride < count:
        packed = jnp.concatenate(
            [
                lower_blk.reshape((4,) + tail),
                (main_blk - unit_block).reshape((4,) + tail),
                upper_blk.reshape((4,) + tail),
                right_side,
            ],
            0,
        )
        below, above = neighbors(packed, stride)
        below_lower = below[0:4].reshape((2, 2) + tail)
        below_main = below[4:8].reshape((2, 2) + tail) + unit_block
        below_upper = below[8:12].reshape((2, 2) + tail)
        above_lower = above[0:4].reshape((2, 2) + tail)
        above_main = above[4:8].reshape((2, 2) + tail) + unit_block
        above_upper = above[8:12].reshape((2, 2) + tail)
        left_mult = -block_product(lower_blk, block_inverse(below_main))
        right_mult = -block_product(upper_blk, block_inverse(above_main))
        main_blk = (
            main_blk
            + block_product(left_mult, below_upper)
            + block_product(right_mult, above_lower)
        )
        lower_blk = block_product(left_mult, below_lower)
        upper_blk = block_product(right_mult, above_upper)
        right_side = (
            right_side
            + block_apply(left_mult, below[12:14])
            + block_apply(right_mult, above[12:14])
        )
        stride = stride * 2
    return block_apply(block_inverse(main_blk), right_side)


def local_pair(packed, stride):
    return (lower(packed, stride, 0.0, 1), higher(packed, stride, 0.0, 1))


def solve_lines(cond, rhs):
    length = rhs.shape[2]
    left_face = cond[:, :, :-1]
    right_face = cond[:, :, 1:]
    cells = jnp.arange(length, dtype=jnp.int32)[:, None]
    sub_diag = jnp.where(cells > 0, -left_face, 0.0)
    super_diag = jnp.where(cells < length - 1, -right_face, 0.0)
    main_diag = 1.0 + left_face + right_face
    first_unit = jnp.broadcast_to(jnp.where(cells == 0, 1.0, 0.0), rhs.shape).astype(jnp.float32)
    last_unit = jnp.broadcast_to(jnp.where(cells == length - 1, 1.0, 0.0), rhs.shape).astype(
        jnp.float32
    )
    solved = line_reduce(sub_diag, main_diag, super_diag, jnp.stack([rhs, first_unit, last_unit]))
    local_part = solved[0]
    from_left = solved[1]
    from_right = solved[2]
    left_cond = cond[:, :, 0]
    right_cond = cond[:, :, length]
    coupled_prev_first = -left_cond * from_left[:, :, 0]
    coupled_prev_last = -left_cond * from_left[:, :, length - 1]
    coupled_next_first = -right_cond * from_right[:, :, 0]
    coupled_next_last = -right_cond * from_right[:, :, length - 1]
    rows = jnp.stack(
        [
            coupled_prev_first,
            coupled_prev_last,
            coupled_next_first,
            coupled_next_last,
            local_part[:, :, 0],
            local_part[:, :, length - 1],
        ]
    )
    every = jnp.moveaxis(lax.all_gather(rows[None], "gx", axis=0, tiled=True), 0, 1)
    blank = jnp.zeros_like(every[0])
    lower_all = jnp.stack([jnp.stack([blank, every[0]]), jnp.stack([blank, every[1]])])
    upper_all = jnp.stack([jnp.stack([every[2], blank]), jnp.stack([every[3], blank])])
    solution = block_steps(lower_all, upper_all, every[4:6], every.shape[1], local_pair)
    own_index = lax.axis_index("gx")
    before = lax.dynamic_index_in_dim(lower(solution, 1, 0.0, 1), own_index, 1, keepdims=False)
    after = lax.dynamic_index_in_dim(higher(solution, 1, 0.0, 1), own_index, 1, keepdims=False)
    previous_last = before[1]
    next_first = after[0]
    return (
        local_part
        + left_cond[:, :, None] * previous_last[:, :, None] * from_left
        + right_cond[:, :, None] * next_first[:, :, None] * from_right
    )


def return_rims(adjoint_pad):
    length = adjoint_pad.shape[2] - 2
    width = adjoint_pad.shape[3] - 2
    inner = adjoint_pad[:, :, 1:-1, 1:-1]
    middle_x = jnp.zeros_like(inner[:, :, : length - 2])
    middle_y = jnp.zeros_like(inner[:, :, :, : width - 2])
    along_x = jnp.concatenate(
        [adjoint_pad[:, :, 0:1, 1:-1], middle_x, adjoint_pad[:, :, length + 1 :, 1:-1]], 2
    )
    along_y = jnp.concatenate(
        [adjoint_pad[:, :, 1:-1, 0:1], middle_y, adjoint_pad[:, :, 1:-1, width + 1 :]], 3
    )
    from_x = extended(along_x, (("gx", 2),), 1)
    from_y = extended(along_y, (("gy", 3),), 1)
    edge_x = jnp.concatenate([from_x[:, :, 0:1], middle_x, from_x[:, :, length + 1 :]], 2)
    edge_y = jnp.concatenate([from_y[:, :, :, 0:1], middle_y, from_y[:, :, :, width + 1 :]], 3)
    return inner + edge_x + edge_y


def per_device(state, diffusivity, sea_mask, depth_index, closure_in, closure_out, cotangent):
    levels = state.shape[1]
    cells_x = state.shape[2]
    cells_y = state.shape[3]
    level_ids = jnp.arange(levels, dtype=jnp.int32)[:, None, None]
    wet = jnp.where((level_ids < depth_index[None]) & (sea_mask[None] > 0), 1.0, 0.0).astype(
        jnp.float32
    )
    total_y = cells_y * lax.axis_size("gy")
    total_x = cells_x * lax.axis_size("gx")
    places = lax.axis_index("gy") * cells_y + jnp.arange(cells_y, dtype=jnp.int32)
    coriolis = 0.5 + 0.5 * places.astype(jnp.float32) / total_y
    rates = jnp.array([DIFFUSE, DIFFUSE, 0.5, 0.5], dtype=jnp.float32)
    local_step = partial(explicit, wet=wet, coriolis=coriolis)
    fields = state
    stacked = jnp.concatenate([fields, wet[None], diffusivity[None]], 0)
    padded = extended(stacked, (("gx", 2), ("gy", 3)), 1)
    wet_pad = padded[4]
    face_terms = padded[5][:, :-1, 1:-1] * wet_pad[:, :-1, 1:-1] * wet_pad[:, 1:, 1:-1]
    cond = rates[:, None, None, None] * face_terms[None]
    updated, backward = jax.vjp(local_step, padded[:4], closure_in, closure_out)
    saved = (cond, backward)
    fields = solve_lines(cond, updated)
    adjoint = cotangent
    cond, stored = saved
    adjoint_explicit = solve_lines(cond, adjoint)
    adjoint_pad, grad_in, grad_out = stored(adjoint_explicit)
    adjoint = return_rims(adjoint_pad)
    summed_in, summed_out = lax.psum((grad_in, grad_out), ("gx", "gy"))
    factor = 1.0 / math.sqrt(levels * total_x * total_y)
    closure_grad = jnp.concatenate([summed_in, summed_out[:, None]], 1) * factor
    return (fields, adjoint, closure_grad)


def solution(mesh):
    return jax.shard_map(
        per_device,
        mesh=mesh,
        in_specs=(
            P(None, None, "gx", "gy"),
            P(None, "gx", "gy"),
            P("gx", "gy"),
            P("gx", "gy"),
            P(),
            P(),
            P(None, None, "gx", "gy"),
        ),
        out_specs=(P(None, None, "gx", "gy"), P(None, None, "gx", "gy"), P()),
        check_vma=False,
    )
```

profile of v0, /device:TPU:32, one launch (start us, length us, event | category | flops | bytes accessed | tf_op | source)
XLA Modules:
  0.0 206.3 jit_solution(14337797914564062561)
XLA Ops:
  0.6 0.8 copy.900
  1.5 1.0 copy.568
  2.6 1.4 collective-permute-start
  4.0 3.0 %collective-permute-start.1 = (f32[6,2,1,128]{3,1,0,2:T(2,128)S(1)}, f32[6,2,1,128]{3,1,0,2:T(2,128)S(1)}, u32[]{:S(2)}, u32[]{:S(2)}) collective-permute-start(f32[6,2,1,128]{3,1,0,2:T(2,128)S(1)} %get-tuple-element.508), channel_id=1, source_target_pairs={{0,32},{32,64},{64,96},{96,128},{128,160},{160,192},{192,224},{1,3... | collective-permute-start | bytes 18440 | tf_op jit(solution)/shard_map/ppermute | solution.py:18
  13.9 3.8 %collective-permute-start.2 = (f32[6,2,34,1]{3,1,0,2:T(2,128)S(1)}, f32[6,2,34,1]{3,1,0,2:T(2,128)S(1)}, u32[]{:S(2)}, u32[]{:S(2)}) collective-permute-start(f32[6,2,34,1]{3,1,0,2:T(2,128)S(1)} %get-tuple-element.497), channel_id=1, source_target_pairs={{1,0},{2,1},{3,2},{4,3},{5,4},{6,5},{7,6},{8,7},{9,8},{10,9},{11,1... | collective-permute-start | bytes 4904 | tf_op jit(solution)/shard_map/ppermute | solution.py:21
  17.6 2.1 %collective-permute-start.3 = (f32[6,2,34,1]{3,1,0,2:T(2,128)S(1)}, f32[6,2,34,1]{3,1,0,2:T(2,128)S(1)}, u32[]{:S(2)}, u32[]{:S(2)}) collective-permute-start(f32[6,2,34,1]{3,1,0,2:T(2,128)S(1)} %get-tuple-element.496), channel_id=1, source_target_pairs={{0,1},{1,2},{2,3},{3,4},{4,5},{5,6},{6,7},{7,8},{8,9},{9,10},{10,1... | collective-permute-start | bytes 4904 | tf_op jit(solution)/shard_map/ppermute | solution.py:18
  19.8 3.7 %collective-permute-done.2 = f32[6,2,34,1]{3,1,0,2:T(2,128)S(1)} collective-permute-done((f32[6,2,34,1]{3,1,0,2:T(2,128)S(1)}, f32[6,2,34,1]{3,1,0,2:T(2,128)S(1)}, u32[]{:S(2)}, u32[]{:S(2)}) %collective-permute-start.2) | collective-permute-done | bytes 1664 | tf_op jit(solution)/shard_map/ppermute | solution.py:21
  23.5 2.9 %collective-permute-done.3 = f32[6,2,34,1]{3,1,0,2:T(2,128)S(1)} collective-permute-done((f32[6,2,34,1]{3,1,0,2:T(2,128)S(1)}, f32[6,2,34,1]{3,1,0,2:T(2,128)S(1)}, u32[]{:S(2)}, u32[]{:S(2)}) %collective-permute-start.3) | collective-permute-done | bytes 1664 | tf_op jit(solution)/shard_map/ppermute | solution.py:18
  32.9 13.0 %all-gather.1 = f32[48,4,2,128]{3,1,2,0:T(4,128)S(1)} all-gather(f32[6,4,2,128]{3,1,2,0:T(4,128)S(1)} %copy.643), channel_id=3, replica_groups=mesh['gx'=8,'gy'=32] {'gx'}, dimensions={0}, use_global_device_ids=true | all-gather | bytes 221184 | tf_op jit(solution)/shard_map/all_gather | solution.py:199
  60.0 3.6 %while.31 = (s32[]{:T(128)}, f32[2,32,128]{2,1,0:T(8,128)S(1)}, f32[2,8,32,128]{3,1,2,0:T(8,128)S(1)}, f32[64,8]{0,1:T(8,128)S(1)}, f32[64,1,1]{0,2,1:T(1,128)S(1)}, /*index=5*/f32[64]{0:T(128)S(1)}) while((s32[]{:T(128)}, f32[2,32,128]{2,1,0:T(8,128)S(1)}, f32[2,8,32,128]{3,1,2,0:T(8,128)S(1)}, f32[64,8]{0,1:T(8,128)S(1)}, ...), condition=%wide.region_1.2_spmd.clone, body=%wide.region_0.1_spmd.sunk.clone | while | flops 28590080 | bytes 2282325 | solution.py:59
  60.2 1.0 fusion.218
  61.9 1.0 fusion.218
  67.5 12.8 %all-gather = f32[48,4,2,128]{3,1,2,0:T(4,128)S(1)} all-gather(f32[6,4,2,128]{3,1,2,0:T(4,128)S(1)} %copy.593), channel_id=2, replica_groups=mesh['gx'=8,'gy'=32] {'gx'}, dimensions={0}, use_global_device_ids=true | all-gather | bytes 221184 | tf_op jit(solution)/shard_map/all_gather | solution.py:199
  91.8 9.9 %while.32 = (s32[]{:T(128)}, f32[64,9]{0,1:T(8,128)S(1)}, f32[64]{0:T(128)S(1)}, f32[2,8,32,128]{3,2,0,1:T(8,128)S(1)}, f32[2,8,32,128]{3,1,2,0:T(8,128)S(1)}, /...) while((s32[]{:T(128)}, f32[64,9]{0,1:T(8,128)S(1)}, ...), condition=%wide.region_4.5_spmd.clone.clone, body=%wide.region_2.4_spmd.clone.sunk.clone | while | flops 86275840 | bytes 7393152 | solution.py:59
  91.8 1.0 fusion.228
  93.5 1.1 convolution_bitcast_fusion.7
  94.9 0.9 fusion.232
  95.9 0.8 convolution_bitcast_fusion.8
  96.8 1.0 fusion.228
  98.5 1.1 convolution_bitcast_fusion.7
  99.9 0.9 fusion.232
  100.9 0.8 convolution_bitcast_fusion.8
  103.0 0.8 copy-done.2
  104.3 0.9 copy-done.1
  105.6 0.8 copy-done.5
  106.8 0.8 copy-done.3
  110.2 1.3 collective-permute-start.5
  111.5 3.0 %collective-permute-start.4 = (f32[4,2,1,128]{3,2,1,0:T(1,128)S(1)}, f32[4,2,1,128]{3,2,1,0:T(1,128)S(1)}, u32[]{:S(2)}, u32[]{:S(2)}) collective-permute-start(f32[4,2,1,128]{3,2,1,0:T(1,128)S(1)} %get-tuple-element.379), channel_id=1, source_target_pairs={{0,32},{32,64},{64,96},{96,128},{128,160},{160,192},{192,224},{1,3... | collective-permute-start | bytes 12296 | tf_op jit(solution)/shard_map/ppermute | solution.py:18
  114.7 1.9 collective-permute-start.7
  116.6 3.9 %collective-permute-start.6 = (f32[4,2,32,1]{3,2,1,0:T(8,128)S(1)}, f32[4,2,32,1]{3,2,1,0:T(8,128)S(1)}, u32[]{:S(2)}, u32[]{:S(2)}) collective-permute-start(f32[4,2,32,1]{3,2,1,0:T(8,128)S(1)} %get-tuple-element.474), channel_id=1, source_target_pairs={{0,1},{1,2},{2,3},{3,4},{4,5},{5,6},{6,7},{7,8},{8,9},{9,10},{10,1... | collective-permute-start | bytes 3080 | tf_op jit(solution)/shard_map/ppermute | solution.py:18
  121.3 82.8 %all-reduce.87 = (f32[64,1]{0,1:T(1,128)S(1)}, f32[64,9]{0,1:T(8,128)S(1)}) all-reduce(f32[64,1]{0,1:T(1,128)S(1)} %bitcast.1001, f32[64,9]{0,1:T(8,128)S(1)} %get-tuple-element.203), channel_id=1, replica_groups=mesh['gx'=8,'gy'=32] {'gx','gy'}, use_global_device_ids=true, to_apply=%region_10.11 | all-reduce | flops 640 | bytes 5120 | tf_op jit(solution)/shard_map/psum | solution.py:263
  205.5 0.8 fusion.18
  (527 shorter events, 51.0 us)
Async XLA Ops:
  0.6 0.8 copy-start.37
  1.5 1.0 copy-start.30
  2.5 4.6 %copy-start = (f32[4,2,32,128]{3,2,1,0:T(8,128)S(1)}, f32[4,2,32,128]{3,2,1,0:T(8,128)}, u32[]{:S(2)}) copy-start(f32[4,2,32,128]{3,2,1,0:T(8,128)} %param.12) | copy-start | bytes 393220
  2.6 4.6 %copy-start.24 = (f32[4,2,32,128]{3,2,1,0:T(8,128)S(1)}, f32[4,2,32,128]{3,2,1,0:T(8,128)}, u32[]{:S(2)}) copy-start(f32[4,2,32,128]{3,2,1,0:T(8,128)} %param.18) | copy-start | bytes 393220
  2.6 10.9 %collective-permute-start = (f32[6,2,1,128]{3,1,0,2:T(2,128)S(1)}, f32[6,2,1,128]{3,1,0,2:T(2,128)S(1)}, u32[]{:S(2)}, u32[]{:S(2)}) collective-permute-start(f32[6,2,1,128]{3,1,0,2:T(2,128)S(1)} %get-tuple-element.509), channel_id=1, source_target_pairs={{32,0},{64,32},{96,64},{128,96},{160,128},{192,160},{224,192},{33,... | collective-permute-start | bytes 18440 | tf_op jit(solution)/shard_map/ppermute | solution.py:21
  4.0 9.5 %collective-permute-start.1 = (f32[6,2,1,128]{3,1,0,2:T(2,128)S(1)}, f32[6,2,1,128]{3,1,0,2:T(2,128)S(1)}, u32[]{:S(2)}, u32[]{:S(2)}) collective-permute-start(f32[6,2,1,128]{3,1,0,2:T(2,128)S(1)} %get-tuple-element.508), channel_id=1, source_target_pairs={{0,32},{32,64},{64,96},{96,128},{128,160},{160,192},{192,224},{1,3... | collective-permute-start | bytes 18440 | tf_op jit(solution)/shard_map/ppermute | solution.py:18
  7.1 39.5 %copy-start.31 = (f32[2,2]{1,0:T(2,128)}, f32[2,2]{1,0:T(2,128)S(1)}, u32[]{:S(2)}) copy-start(f32[2,2]{1,0:T(2,128)S(1)} %compare_convert_fusion.1) | copy-start | bytes 52
  12.2 33.8 %copy-start.41 = (f32[14]{0:T(128)}, f32[14]{0:T(128)S(1)}, u32[]{:S(2)}) copy-start(f32[14]{0:T(128)S(1)} %pad.512.clone) | copy-start | bytes 172
  13.5 12.9 %copy-start.26 = (f32[6,2,1,128]{3,1,0,2:T(2,128)}, f32[6,2,1,128]{3,1,0,2:T(2,128)S(1)}, u32[]{:S(2)}) copy-start(f32[6,2,1,128]{3,1,0,2:T(2,128)S(1)} %collective-permute-done) | copy-start | bytes 18436
  13.5 12.9 %copy-start.28 = (f32[6,2,1,128]{3,1,0,2:T(2,128)}, f32[6,2,1,128]{3,1,0,2:T(2,128)S(1)}, u32[]{:S(2)}) copy-start(f32[6,2,1,128]{3,1,0,2:T(2,128)S(1)} %collective-permute-done.1) | copy-start | bytes 18436
  13.9 9.6 %collective-permute-start.2 = (f32[6,2,34,1]{3,1,0,2:T(2,128)S(1)}, f32[6,2,34,1]{3,1,0,2:T(2,128)S(1)}, u32[]{:S(2)}, u32[]{:S(2)}) collective-permute-start(f32[6,2,34,1]{3,1,0,2:T(2,128)S(1)} %get-tuple-element.497), channel_id=1, source_target_pairs={{1,0},{2,1},{3,2},{4,3},{5,4},{6,5},{7,6},{8,7},{9,8},{10,9},{11,1... | collective-permute-start | bytes 4904 | tf_op jit(solution)/shard_map/ppermute | solution.py:21
  17.6 8.7 %collective-permute-start.3 = (f32[6,2,34,1]{3,1,0,2:T(2,128)S(1)}, f32[6,2,34,1]{3,1,0,2:T(2,128)S(1)}, u32[]{:S(2)}, u32[]{:S(2)}) collective-permute-start(f32[6,2,34,1]{3,1,0,2:T(2,128)S(1)} %get-tuple-element.496), channel_id=1, source_target_pairs={{0,1},{1,2},{2,3},{3,4},{4,5},{5,6},{6,7},{7,8},{8,9},{9,10},{10,1... | collective-permute-start | bytes 4904 | tf_op jit(solution)/shard_map/ppermute | solution.py:18
  59.3 0.8 copy-start.33
  91.8 10.4 %copy-start.16 = (f32[2,32,128]{2,1,0:T(8,128)S(1)}, f32[2,32,128]{2,1,0:T(8,128)}, u32[]{:S(2)}) copy-start(f32[2,32,128]{2,1,0:T(8,128)} %get-tuple-element.524) | copy-start | bytes 98308
  103.0 0.8 copy-start.2
  103.0 0.8 copy-start.13
  103.0 0.8 copy-start.14
  104.3 0.9 copy-start.1
  105.6 0.8 copy-start.5
  105.6 0.9 copy-start.6
  106.8 0.8 copy-start.3
  106.8 0.9 copy-start.4
  107.8 0.8 copy-start.7
  107.8 0.9 copy-start.8
  107.8 0.9 copy-start.9
  107.8 0.9 copy-start.10
  109.0 0.8 copy-start.19
  109.1 0.8 copy-start.20
  110.2 95.2 %collective-permute-start.5 = (f32[4,2,1,128]{3,2,1,0:T(1,128)S(1)}, f32[4,2,1,128]{3,2,1,0:T(1,128)S(1)}, u32[]{:S(2)}, u32[]{:S(2)}) collective-permute-start(f32[4,2,1,128]{3,2,1,0:T(1,128)S(1)} %get-tuple-element.380), channel_id=1, source_target_pairs={{32,0},{64,32},{96,64},{128,96},{160,128},{192,160},{224,192},{33,... | collective-permute-start | bytes 12296 | tf_op jit(solution)/shard_map/ppermute | solution.py:21
  111.5 93.9 %collective-permute-start.4 = (f32[4,2,1,128]{3,2,1,0:T(1,128)S(1)}, f32[4,2,1,128]{3,2,1,0:T(1,128)S(1)}, u32[]{:S(2)}, u32[]{:S(2)}) collective-permute-start(f32[4,2,1,128]{3,2,1,0:T(1,128)S(1)} %get-tuple-element.379), channel_id=1, source_target_pairs={{0,32},{32,64},{64,96},{96,128},{128,160},{160,192},{192,224},{1,3... | collective-permute-start | bytes 12296 | tf_op jit(solution)/shard_map/ppermute | solution.py:18
  114.7 90.7 %collective-permute-start.7 = (f32[4,2,32,1]{3,2,1,0:T(8,128)S(1)}, f32[4,2,32,1]{3,2,1,0:T(8,128)S(1)}, u32[]{:S(2)}, u32[]{:S(2)}) collective-permute-start(f32[4,2,32,1]{3,2,1,0:T(8,128)S(1)} %get-tuple-element.475), channel_id=1, source_target_pairs={{1,0},{2,1},{3,2},{4,3},{5,4},{6,5},{7,6},{8,7},{9,8},{10,9},{11,1... | collective-permute-start | bytes 3080 | tf_op jit(solution)/shard_map/ppermute | solution.py:21
  116.6 88.8 %collective-permute-start.6 = (f32[4,2,32,1]{3,2,1,0:T(8,128)S(1)}, f32[4,2,32,1]{3,2,1,0:T(8,128)S(1)}, u32[]{:S(2)}, u32[]{:S(2)}) collective-permute-start(f32[4,2,32,1]{3,2,1,0:T(8,128)S(1)} %get-tuple-element.474), channel_id=1, source_target_pairs={{0,1},{1,2},{2,3},{3,4},{4,5},{5,6},{6,7},{7,8},{8,9},{9,10},{10,1... | collective-permute-start | bytes 3080 | tf_op jit(solution)/shard_map/ppermute | solution.py:18
  (23 other events, 16.1 us)
where the time goes:
time: 209 us; the launch traced here: 206 us
  blocking collectives  109 us (52%)
  local copies, waits for them, and re-layouts  32.7 us (16%)
  other arithmetic  21.6 us (10%)
  starting transfers between devices  20.5 us (10%)
  matrix products  12.3 us (6%)
  waiting for transfers between devices  6.52 us (3%)
  between operations  3.76 us (2%)
    psum x1, blocking collectives, per_device(): summed_in, summed_out = lax.psum((grad_in, grad_out), ('gx', 'gy'))  82.8 us
    all_gather x2, blocking collectives, solve_lines(): lax.all_gather(rows[None], 'gx', axis=0, tiled=True)  25.8 us
    unnamed x99, local copies, waits for them, and re-layouts  16 us
    ppermute x4, starting transfers between devices, extended(): lax.ppermute(lax.slice_in_dim(block, block.shape[dim] - width, None, axis...  12.1 us
    ppermute x4, starting transfers between devices, extended(): lax.ppermute(lax.slice_in_dim(block, 0, width, axis=dim), axis, backward)  8.39 us
    dot_general x8, matrix products, closure_level(): jnp.einsum('hc,cxy->hxy', closure_in[:, :FEAT], grads, precision=lax.Prec...  7.9 us
    dot_general x6, matrix products, closure_level(): jnp.einsum('h,hxy->xy', closure_out, hidden, precision=lax.Precision.HIGH...  4.42 us
  transfers between devices with their start and end apart: 8, of which 2 were waited for; matrix products, arithmetic and copies ran while one was open for 4% of the time, Pallas kernels for 0%

commit v1 on v0

v1 whole, which is shorter than its diff:
```python
import math

import jax
import jax.numpy as jnp
from jax import lax
from jax.experimental import pallas as pl
from jax.experimental.pallas import tpu as pltpu
from jax.sharding import PartitionSpec as P

F32 = jnp.float32
BF16 = jnp.bfloat16
DIFFUSE = 2048.0
FEAT = 8
HID = 64
NX = 32
NY = 128
ROWS = 8
XS = 4
RIM = 80


def iota(shape, dim):
    return lax.broadcasted_iota(jnp.int32, shape, dim)


def rows8():
    return iota((ROWS, NY), 0)


def lanes8():
    return iota((ROWS, NY), 1)


def wide(row):
    return jnp.broadcast_to(row, (ROWS, NY))


def by_level(first, second):
    return jnp.where((rows8() & 1) == 0, wide(first), wide(second))


def line(ref, x):
    return ref[pl.ds(x, ROWS, stride=NX), :]


def wet_line(sea_ref, depth_ref, x):
    sea = wide(sea_ref[x : x + 1, :])
    depth = wide(depth_ref[x : x + 1, :])
    return jnp.where(((rows8() & 1) < depth) & (sea > 0), 1.0, 0.0).astype(F32)


def rates8():
    return jnp.where(rows8() < 4, DIFFUSE, 0.5).astype(F32)


def split(values):
    high = values.astype(BF16)
    return high, (values - high.astype(F32)).astype(BF16)


def columns_kernel(state_ref, first_ref, last_ref):
    lanes = lanes8()
    first = jnp.zeros((ROWS, NY), F32)
    last = jnp.zeros((ROWS, NY), F32)
    for x in range(NX):
        here = line(state_ref, x)
        first = jnp.where(lanes == x, pltpu.roll(here, x, 1) if x else here, first)
        last = jnp.where(lanes == x, pltpu.roll(here, x + 1, 1), last)
    first_ref[...] = first
    last_ref[...] = last


def factor_kernel(
    state_ref, diff_ref, sea_ref, depth_ref, cot_ref, send_ref, right_ref, recip_ref, left_ref
):
    me = lax.axis_index("gx")
    count = send_ref.shape[0]
    row = rows8()
    wet = [wet_line(sea_ref, depth_ref, x) for x in range(NX)]
    rates = rates8()
    bare = [
        by_level(diff_ref[x : x + 1, :], diff_ref[NX + x : NX + x + 1, :]) * wet[x]
        for x in range(NX)
    ]
    cond = [rates * bare[x] * wet[x + 1] for x in range(NX - 1)]
    mass = jnp.ones((ROWS, NY), F32)
    carry = jnp.ones((ROWS, NY), F32)
    load = line(cot_ref, 0)
    mass_back = jnp.ones((ROWS, NY), F32)
    load_back = line(cot_ref, NX - 1)
    for i in range(NX - 1):
        recip = 1.0 / (mass + cond[i])
        ratio = cond[i] * recip
        right_ref[i] = ratio
        recip_ref[i] = recip
        mass = 1.0 + mass * ratio
        load = line(cot_ref, i + 1) + ratio * load
        carry = carry * ratio
        j = NX - 2 - i
        ratio_back = cond[j] / (mass_back + cond[j])
        left_ref[j] = ratio_back
        mass_back = 1.0 + mass_back * ratio_back
        load_back = line(cot_ref, j) + ratio_back * load_back
    last_self = 1.0 / mass
    first_self = 1.0 / mass_back
    right_ref[NX - 1] = jnp.zeros((ROWS, NY), F32)
    left_ref[NX - 1] = jnp.zeros((ROWS, NY), F32)
    recip_ref[NX - 1] = last_self
    across = carry * last_self
    upper = (row & 2) == 0
    tiles = [
        load_back * first_self,
        load * last_self,
        jnp.where(upper, first_self, across),
        jnp.where(upper, last_self, jnp.where(row < 4, bare[NX - 1], wet[0])),
    ]
    own_last = line(state_ref, NX - 1)
    own_first = line(state_ref, 0)
    for j in range(count):
        for n, tile in enumerate(tiles):
            send_ref[j, ROWS * n : ROWS * (n + 1), :] = tile
        send_ref[j, ROWS * 4 :, :] = jnp.where(j > me, own_last, own_first)


def reduced(got_ref):
    count = got_ref.shape[0]
    upper = (rows8() & 2) == 0
    first_self, across, last_self, bare, wet = [], [], [], [], []
    for j in range(count):
        tile = got_ref[j, 16:24, :]
        first_self.append(jnp.where(upper, tile, pltpu.roll(tile, 2, 0)))
        across.append(jnp.where(upper, pltpu.roll(tile, 6, 0), tile))
        tile = got_ref[j, 24:32, :]
        last_self.append(jnp.where(upper, tile, pltpu.roll(tile, 2, 0)))
        bare.append(by_level(got_ref[j, 26:27, :], got_ref[j, 27:28, :]))
        wet.append(by_level(got_ref[j, 30:31, :], got_ref[j, 31:32, :]))
    face = [rates8() * bare[j] * wet[j + 1] for j in range(count - 1)]
    return first_self, across, last_self, face


def end_fluxes(system, first, last, me):
    first_self, across, last_self, face = system
    count = len(first_self)
    zero = jnp.zeros((ROWS, NY), F32)
    give, value = last_self[0], last[0]
    gives, values, links = [give], [value], [zero]
    for j in range(1, count):
        link = face[j - 1] / (1.0 + face[j - 1] * (give + first_self[j]))
        pull = across[j] * link
        value = last[j] + pull * (value - first[j])
        give = last_self[j] - pull * across[j]
        gives.append(give)
        values.append(value)
        links.append(link)
    back_give, back_value = first_self[count - 1], first[count - 1]
    right_flux = [None] * count
    right_flux[count - 1] = zero
    for j in range(count - 2, -1, -1):
        right_flux[j] = (
            face[j] * (back_value - values[j]) / (1.0 + face[j] * (back_give + gives[j]))
        )
        link = face[j] / (1.0 + face[j] * (back_give + last_self[j]))
        pull = across[j] * link
        back_value = first[j] + pull * (back_value - last[j])
        back_give = first_self[j] - pull * across[j]
    left, right = zero, right_flux[0]
    for j in range(1, count):
        here = links[j] * (values[j - 1] - first[j] - across[j] * right_flux[j])
        left = jnp.where(me == j, here, left)
        right = jnp.where(me == j, right_flux[j], right)
    return left, right


def own_lines(read, right_ref, recip_ref, fluxes, write):
    left, right = fluxes
    load = read(0) + left
    loads = [load]
    for i in range(1, NX):
        load = read(i) + right_ref[i - 1] * load
        loads.append(load)
    value = (loads[NX - 1] + right) * recip_ref[NX - 1]
    write(NX - 1, value)
    for i in range(NX - 2, -1, -1):
        value = right_ref[i] * value + recip_ref[i] * loads[i]
        write(i, value)


def network(weights_ref, out_ref):
    weights = weights_ref[...]
    where_to = []
    for level in range(2):
        spread = (iota((FEAT + 1, 128), 1) == 2 * iota((FEAT + 1, 128), 0) + level) & (
            iota((FEAT + 1, 128), 0) < FEAT
        )
        where_to.append(
            jnp.dot(
                weights,
                spread.astype(F32),
                precision=lax.Precision.HIGHEST,
                preferred_element_type=F32,
            )
        )
    both = jnp.concatenate(where_to, 0)
    high = both.astype(BF16).astype(F32)
    low = both - high
    bias = weights[:, FEAT : FEAT + 1]
    bias = jnp.broadcast_to(jnp.concatenate([bias, bias], 0), (2 * HID, 128))
    bias_high = bias.astype(BF16).astype(F32)
    bias_mid = (bias - bias_high).astype(BF16).astype(F32)
    bias_low = bias - bias_high - bias_mid
    lane = iota((2 * HID, 128), 1)
    forward = high + pltpu.roll(high, 16, 1) + pltpu.roll(low, 48, 1) + pltpu.roll(low, 64, 1)
    forward = jnp.where(lane == 32, bias_high, forward)
    forward = jnp.where(lane == 33, bias_mid, forward)
    forward = jnp.where(lane == 34, bias_low, forward)
    turned = jnp.transpose(high + pltpu.roll(low, 16, 1))[:32]
    back = jnp.concatenate([turned, turned], 1)
    out = out_ref[...]
    out = jnp.broadcast_to(jnp.concatenate([out, out], 0), (2 * HID, 128))
    return forward.astype(BF16), back.astype(BF16), out


def main_kernel(
    got_ref,
    low_ref,
    high_ref,
    state_ref,
    sea_ref,
    depth_ref,
    cot_ref,
    right_ref,
    recip_ref,
    left_ref,
    weights_ref,
    out_ref,
    send_ref,
    grad_ref,
    rims_ref,
    rhs_ref,
    fields,
    wets,
    adj,
    slope_x,
    slope_y,
    curve_x,
    curve_y,
    feats,
    forward_ref,
    back_ref,
    outw_ref,
    sums_ref,
    out_sums_ref,
):
    me = lax.axis_index("gx")
    here_y = lax.axis_index("gy")
    count = got_ref.shape[0]
    total_y = NY * lax.axis_size("gy")
    lanes = lanes8()
    row = rows8()
    zero = jnp.zeros((ROWS, NY), F32)

    for x in range(NX):
        wets[x] = wet_line(sea_ref, depth_ref, x)
        fields[x + 1] = line(state_ref, x)
    below = got_ref[jnp.maximum(me - 1, 0), 32:40, :]
    above = got_ref[jnp.minimum(me + 1, count - 1), 32:40, :]
    fields[0] = jnp.where(me > 0, below, zero)
    fields[NX + 1] = jnp.where(me < count - 1, above, zero)

    system = reduced(got_ref)
    first = [got_ref[j, 0:8, :] for j in range(count)]
    last = [got_ref[j, 8:16, :] for j in range(count)]
    fluxes = end_fluxes(system, first, last, me)

    def keep(x, value):
        adj[x] = wets[x] * value

    own_lines(lambda x: line(cot_ref, x), right_ref, recip_ref, fluxes, keep)

    low = low_ref[...]
    high = high_ref[...]
    feats[32:48, :] = jnp.ones((16, NX * NY), BF16)
    for x in range(NX):
        center = fields[x + 1]
        east = fields[x + 2]
        west = fields[x]
        south = jnp.where(lanes == 0, pltpu.roll(low, (-x) % NY, 1) if x else low, pltpu.roll(center, 1, 1))
        north = jnp.where(
            lanes == NY - 1, pltpu.roll(high, NY - 1 - x, 1), pltpu.roll(center, NY - 1, 1)
        )
        sx = 0.5 * (east - west)
        sy = 0.5 * (north - south)
        slope_x[x] = sx
        slope_y[x] = sy
        curve_x[x] = east - 2.0 * center + west
        curve_y[x] = north - 2.0 * center + south
        part_high, part_low = split(jnp.concatenate([sx, sy], 0))
        place = slice(x * NY, (x + 1) * NY)
        feats[0:16, place] = part_high
        feats[16:32, place] = part_low
        feats[48:64, place] = part_high
        feats[64:80, place] = part_low

    forward, back, outw = network(weights_ref, out_ref)
    forward_ref[...] = forward
    back_ref[...] = back
    outw_ref[...] = outw
    sums_ref[...] = jnp.zeros(sums_ref.shape, F32)
    out_sums_ref[...] = jnp.zeros(out_sums_ref.shape, F32)
    grad_ref[...] = jnp.zeros(grad_ref.shape, F32)
    rims_ref[...] = jnp.zeros(rims_ref.shape, F32)
    places = (here_y * NY + lanes).astype(F32)
    turn = 0.3 * (0.5 + 0.5 * places / total_y)
    moment = row < 4

    @pl.loop(0, NX // XS)
    def _(step):
        base = step * XS
        place = pl.ds(pl.multiple_of(base * NY, XS * NY), XS * NY)
        hidden = jnp.tanh(
            jnp.dot(forward_ref[:, 0:80], feats[0:80, place], preferred_element_type=F32)
        )
        outw = outw_ref[...]
        sharp, keepers = [], []
        for i in range(XS):
            x = base + i
            unit = hidden[:, i * NY : (i + 1) * NY]
            weighed = unit * outw
            mixed = by_level(
                jnp.sum(weighed[:HID], 0, keepdims=True), jnp.sum(weighed[HID:], 0, keepdims=True)
            )
            gate = 1.0 / (1.0 + jnp.exp(-mixed))
            nu = jnp.where(moment, 0.24 * gate, 0.0)
            center = fields[x + 1]
            sx, sy, cx, cy = slope_x[x], slope_y[x], curve_x[x], curve_y[x]
            u = by_level(center[0:1], center[1:2])
            v = by_level(center[2:3], center[3:4])
            speed_u = jnp.sqrt(u * u + 0.01)
            speed_v = jnp.sqrt(v * v + 0.01)
            upwind = u * sx + v * sy - 0.5 * (speed_u * cx + speed_v * cy)
            twist = jnp.where(
                row < 2, pltpu.roll(center, 6, 0), jnp.where(moment, -pltpu.roll(center, 2, 0), 0.0)
            )
            rhs_ref[x] = wets[x] * (center - 0.3 * upwind + nu * (cx + cy) + turn * twist)
            g = adj[x]
            to_gate = jnp.where(moment, g * (cx + cy) * (0.24 * gate * (1.0 - gate)), 0.0)
            to_gate = to_gate + pltpu.roll(to_gate, 6, 0)
            gate_level = jnp.concatenate(
                [
                    jnp.broadcast_to(to_gate[0:1], (HID, NY)),
                    jnp.broadcast_to(to_gate[1:2], (HID, NY)),
                ],
                0,
            )
            out_sums_ref[...] += unit * gate_level
            sharp.append((1.0 - unit * unit) * (outw * gate_level))
            along_u = g * (-0.3 * sx + 0.15 * (u / speed_u) * cx)
            along_v = g * (-0.3 * sy + 0.15 * (v / speed_v) * cy)
            along_u = along_u + pltpu.roll(along_u, 4, 0)
            along_u = along_u + pltpu.roll(along_u, 2, 0)
            along_v = along_v + pltpu.roll(along_v, 4, 0)
            along_v = along_v + pltpu.roll(along_v, 2, 0)
            untwist = jnp.where(
                row < 2, along_u - turn * pltpu.roll(g, 6, 0), along_v + turn * pltpu.roll(g, 2, 0)
            )
            bend_x = g * (0.15 * speed_u + nu)
            bend_y = g * (0.15 * speed_v + nu)
            middle = g + jnp.where(moment, untwist, 0.0) - 2.0 * (bend_x + bend_y)
            keepers.append((-0.3 * u * g, -0.3 * v * g, bend_x, bend_y, middle))
        parts = split(jnp.concatenate(sharp, 1))
        stacked = jnp.concatenate(parts, 0)
        sums_ref[...] += lax.dot_general(
            stacked, feats[0:48, place], (((1,), (1,)), ((), ())), preferred_element_type=F32
        )
        to_feats = jnp.dot(back_ref[...], stacked, preferred_element_type=F32)
        to_feats = to_feats[0:16] + to_feats[16:32]
        for i in range(XS):
            x = base + i
            to_sx, to_sy, bend_x, bend_y, middle = keepers[i]
            mine = to_feats[:, i * NY : (i + 1) * NY]
            half_x = 0.5 * (to_sx + mine[0:8])
            half_y = 0.5 * (to_sy + mine[8:16])
            to_north = bend_y + half_y
            to_south = bend_y - half_y
            north = pltpu.roll(to_north, 1, 1)
            south = pltpu.roll(to_south, NY - 1, 1)
            rims_ref[0] = jnp.where(lanes == RIM + x, pltpu.roll(north, RIM + x, 1), rims_ref[0])
            rims_ref[1] = jnp.where(
                lanes == RIM + x, pltpu.roll(south, RIM + x + 1, 1), rims_ref[1]
            )
            grad_ref[x] += bend_x - half_x
            grad_ref[x + 1] += (
                middle + jnp.where(lanes == 0, 0.0, north) + jnp.where(lanes == NY - 1, 0.0, south)
            )
            grad_ref[x + 2] += bend_x + half_x

    load = rhs_ref[0]
    load_back = rhs_ref[NX - 1]
    for i in range(NX - 1):
        load = rhs_ref[i + 1] + right_ref[i] * load
        j = NX - 2 - i
        load_back = rhs_ref[j] + left_ref[j] * load_back
    first_own = load_back * jnp.where(
        (row & 2) == 0, got_ref[me, 16:24, :], pltpu.roll(got_ref[me, 16:24, :], 2, 0)
    )
    last_own = load * recip_ref[NX - 1]

    sums = sums_ref[0:128] + sums_ref[128:256]
    total = jnp.zeros((HID, 128), F32)
    for level in range(2):
        source = iota((48, 128), 0)
        target = iota((48, 128), 1)
        feature = (source < 32) & ((source & 15) == 2 * target + level) & (target < FEAT)
        gather = feature | ((source == 32) & (target == FEAT))
        total += jnp.dot(
            sums[level * HID : (level + 1) * HID],
            gather.astype(F32),
            precision=lax.Precision.HIGHEST,
            preferred_element_type=F32,
        )
    out_total = jnp.sum(out_sums_ref[0:HID] + out_sums_ref[HID:], 1, keepdims=True)
    total = jnp.where(iota((HID, 128), 1) == FEAT + 1, out_total, total)
    packed = zero
    for a in range(HID // 8):
        piece = total[8 * a : 8 * (a + 1)]
        piece = pltpu.roll(piece, 10 * a, 1) if a else piece
        packed = jnp.where((lanes >= 10 * a) & (lanes < 10 * a + 10), piece, packed)
    to_last = grad_ref[NX + 1]
    to_first = grad_ref[0]
    for j in range(count):
        send_ref[j, 0:8, :] = first_own
        send_ref[j, 8:16, :] = last_own
        send_ref[j, 16:24, :] = packed
        send_ref[j, 24:32, :] = jnp.where(j > me, to_last, to_first)


def share_kernel(second_ref, rims_ref, send_ref):
    me = lax.axis_index("gy")
    lanes = lanes8()
    total = second_ref[0, 16:24, :]
    for j in range(1, second_ref.shape[0]):
        total = total + second_ref[j, 16:24, :]
    upward = jnp.where(lanes < RIM, total, rims_ref[0])
    downward = jnp.where(lanes < RIM, total, rims_ref[1])
    for j in range(send_ref.shape[0]):
        send_ref[j] = jnp.where(j > me, upward, downward)


def final_kernel(got_ref, second_ref, rhs_ref, right_ref, recip_ref, final_ref):
    me = lax.axis_index("gx")
    count = got_ref.shape[0]
    system = reduced(got_ref)
    first = [second_ref[j, 0:8, :] for j in range(count)]
    last = [second_ref[j, 8:16, :] for j in range(count)]
    fluxes = end_fluxes(system, first, last, me)

    def keep(x, value):
        final_ref[pl.ds(x, ROWS, stride=NX), :] = value

    own_lines(lambda x: rhs_ref[x], right_ref, recip_ref, fluxes, keep)


def finish_kernel(factor, third_ref, second_ref, grad_ref, out_ref, closure_ref):
    me_x = lax.axis_index("gx")
    me_y = lax.axis_index("gy")
    count_x = second_ref.shape[0]
    count_y = third_ref.shape[0]
    lanes = lanes8()
    zero = jnp.zeros((ROWS, NY), F32)
    parts = [third_ref[j] for j in range(count_y)]
    while len(parts) > 1:
        parts = [a + b for a, b in zip(parts[::2], parts[1::2])]
    total = parts[0] * factor
    for a in range(HID // 8):
        piece = pltpu.roll(total, NY - 10 * a, 1) if a else total
        closure_ref[8 * a : 8 * (a + 1), :] = piece[:, 0:10]
    before = jnp.where(me_x > 0, second_ref[jnp.maximum(me_x - 1, 0), 24:32, :], zero)
    after = jnp.where(
        me_x < count_x - 1, second_ref[jnp.minimum(me_x + 1, count_x - 1), 24:32, :], zero
    )
    south = jnp.where(me_y > 0, third_ref[jnp.maximum(me_y - 1, 0)], zero)
    north = jnp.where(me_y < count_y - 1, third_ref[jnp.minimum(me_y + 1, count_y - 1)], zero)
    for x in range(NX):
        value = grad_ref[x + 1]
        if x == 0:
            value = value + before
        if x == NX - 1:
            value = value + after
        value = value + jnp.where(lanes == 0, pltpu.roll(south, NY - RIM - x, 1), 0.0)
        value = value + jnp.where(lanes == NY - 1, pltpu.roll(north, NY - 1 - RIM - x, 1), 0.0)
        out_ref[pl.ds(x, ROWS, stride=NX), :] = value


def tile(*shape):
    return jax.ShapeDtypeStruct(shape, F32)


def params():
    return pltpu.CompilerParams(vmem_limit_bytes=40 * 1024 * 1024)


def per_device(state, diffusivity, sea_mask, depth_index, closure_in, closure_out, cotangent):
    count_x = lax.axis_size("gx")
    count_y = lax.axis_size("gy")
    flat_state = state.reshape(ROWS * NX, NY)
    flat_cot = cotangent.reshape(ROWS * NX, NY)
    flat_diff = diffusivity.reshape(2 * NX, NY)
    first, last = pl.pallas_call(
        columns_kernel, out_shape=(tile(8, NY), tile(8, NY)), compiler_params=params()
    )(flat_state)
    upward = [(i, i + 1) for i in range(count_y - 1)]
    downward = [(i + 1, i) for i in range(count_y - 1)]
    low = lax.ppermute(last, "gy", upward)
    high = lax.ppermute(first, "gy", downward)
    lines = tile(NX, ROWS, NY)
    send, right, recip, left = pl.pallas_call(
        factor_kernel,
        out_shape=(tile(count_x, 40, NY), lines, lines, lines),
        compiler_params=params(),
    )(flat_state, flat_diff, sea_mask, depth_index, flat_cot)
    got = lax.all_to_all(send, "gx", 0, 0, tiled=True)
    scratch = (
        [pltpu.VMEM((NX + 2, ROWS, NY), F32)]
        + [pltpu.VMEM((NX, ROWS, NY), F32)] * 6
        + [
            pltpu.VMEM((80, NX * NY), BF16),
            pltpu.VMEM((2 * HID, 128), BF16),
            pltpu.VMEM((32, 256), BF16),
            pltpu.VMEM((2 * HID, 128), F32),
            pltpu.VMEM((4 * HID, 48), F32),
            pltpu.VMEM((2 * HID, 128), F32),
        ]
    )
    send, grad, rims, rhs = pl.pallas_call(
        main_kernel,
        out_shape=(tile(count_x, 32, NY), tile(NX + 2, ROWS, NY), tile(2, ROWS, NY), lines),
        scratch_shapes=scratch,
        compiler_params=params(),
    )(
        got,
        low,
        high,
        flat_state,
        sea_mask,
        depth_index,
        flat_cot,
        right,
        recip,
        left,
        closure_in,
        closure_out.reshape(HID, 1),
    )
    second = lax.all_to_all(send, "gx", 0, 0, tiled=True)
    send = pl.pallas_call(
        share_kernel, out_shape=tile(count_y, ROWS, NY), compiler_params=params()
    )(second, rims)
    third = lax.all_to_all(send, "gy", 0, 0, tiled=True)
    final = pl.pallas_call(
        final_kernel, out_shape=tile(ROWS * NX, NY), compiler_params=params()
    )(got, second, rhs, right, recip)
    factor = 1.0 / math.sqrt(2 * NX * count_x * NY * count_y)

    def finish(*refs):
        finish_kernel(factor, *refs)

    state_grad, closure_grad = pl.pallas_call(
        finish, out_shape=(tile(ROWS * NX, NY), tile(HID, 10)), compiler_params=params()
    )(third, second, grad)
    return (final.reshape(state.shape), state_grad.reshape(state.shape), closure_grad)


def solution(mesh):
    return jax.shard_map(
        per_device,
        mesh=mesh,
        in_specs=(
            P(None, None, "gx", "gy"),
            P(None, "gx", "gy"),
            P("gx", "gy"),
            P("gx", "gy"),
            P(),
            P(),
            P(None, None, "gx", "gy"),
        ),
        out_specs=(P(None, None, "gx", "gy"), P(None, None, "gx", "gy"), P()),
        check_vma=False,
    )
```

time: 209 us -> 59.8 us (0.29); the launches traced: 206 us -> 59.2 us
  blocking collectives: 109 us -> 10.7 us
  local copies, waits for them, and re-layouts: 32.7 us -> 5.53 us
  other arithmetic: 21.6 us -> 0 us
  matrix products: 12.3 us -> 0 us
  Pallas kernels: 0 us -> 9.33 us
  waiting for transfers between devices: 6.52 us -> 11.4 us
  between operations: 3.76 us -> 0.71 us
    psum x1 -> x0, blocking collectives: 82.8 us -> none  [per_device(): summed_in, summed_out = lax.psum((grad_in, grad_out), ('gx', 'gy'))]
    all_gather x2 -> x0, blocking collectives: 25.8 us -> none  [solve_lines(): lax.all_gather(rows[None], 'gx', axis=0, tiled=True)]
    all_to_all x0 -> x2, starting transfers between devices: none -> 15.6 us  [the longest x1 11.2 us: per_device(): third = lax.all_to_all(send, 'gy', 0, 0, tiled=True)]
    ppermute x8 -> x2, starting transfers between devices: 20.5 us -> 5.83 us  [the longest x1 3.82 us: per_device(): low = lax.ppermute(last, 'gy', upward)]
    dot_general x14 -> x0, matrix products: 12.3 us -> none  [the longest x8 7.9 us: closure_level(): jnp.einsum('hc,cxy->hxy', closure_in[:, :FEAT], grads, precision=lax.Prec...]
    all_to_all x0 -> x1, blocking collectives: none -> 10.7 us  [per_device(): second = lax.all_to_all(send, 'gx', 0, 0, tiled=True)]
    unnamed x99 -> x24, local copies, waits for them, and re-layouts: 16 us -> 5.44 us
    pallas_call x0 -> x6, Pallas kernels: none -> 9.33 us  [the longest x1 5.73 us: per_device(): pl.pallas_call(main_kernel, out_shape=(tile(count_x, 32, NY), tile(NX + 2...]
  transfers between devices with their start and end apart: 8 -> 4, of which waited for: 2 -> 2; matrix products, arithmetic and copies ran while one was open for 4% -> 0% of each run, Pallas kernels for 0% -> 2%
where the time goes in v1:
time: 59.8 us; the launch traced here: 59.2 us
  starting transfers between devices  21.5 us (36%)
  waiting for transfers between devices  11.4 us (19%)
  blocking collectives  10.7 us (18%)
  Pallas kernels  9.33 us (16%)
  local copies, waits for them, and re-layouts  5.53 us (9%)
  between operations  0.71 us (1%)
    all_to_all x1, starting transfers between devices, per_device(): third = lax.all_to_all(send, 'gy', 0, 0, tiled=True)  11.2 us
    all_to_all x1, blocking collectives, per_device(): second = lax.all_to_all(send, 'gx', 0, 0, tiled=True)  10.7 us
    all_to_all x1, waiting for transfers between devices, per_device(): third = lax.all_to_all(send, 'gy', 0, 0, tiled=True)  8.76 us
    pallas_call x1, Pallas kernels, per_device(): pl.pallas_call(main_kernel, out_shape=(tile(count_x, 32, NY), tile(NX + 2...  5.73 us
    unnamed x24, local copies, waits for them, and re-layouts  5.44 us
    all_to_all x1, starting transfers between devices, per_device(): got = lax.all_to_all(send, 'gx', 0, 0, tiled=True)  4.43 us
    ppermute x1, starting transfers between devices, per_device(): low = lax.ppermute(last, 'gy', upward)  3.82 us
    ppermute x1, waiting for transfers between devices, per_device(): high = lax.ppermute(first, 'gy', downward)  2.62 us
  transfers between devices with their start and end apart: 4, of which 2 were waited for; matrix products, arithmetic and copies ran while one was open for 0% of the time, Pallas kernels for 2%

profile of v1, /device:TPU:32, one launch (start us, length us, event | category | flops | bytes accessed | tf_op | source)
XLA Modules:
  0.0 59.2 jit_solution(17346551417086936321)
XLA Ops:
  0.6 0.0 copy-start
  0.6 0.9 %copy-done = f32[4,2,32,128]{3,2,1,0:T(8,128)S(1)} copy-done((f32[4,2,32,128]{3,2,1,0:T(8,128)S(1)}, f32[4,2,32,128]{3,2,1,0:T(8,128)}, u32[]{:S(2)}) %copy-start) | copy-done | bytes 131096
  1.5 0.0 copy-start.2
  1.5 0.9 %copy-done.2 = f32[4,2,32,128]{3,2,1,0:T(8,128)S(1)} copy-done((f32[4,2,32,128]{3,2,1,0:T(8,128)S(1)}, f32[4,2,32,128]{3,2,1,0:T(8,128)}, u32[]{:S(2)}) %copy-start.2) | copy-done | bytes 131096
  2.4 0.7 %copy-done.4 = s32[32,128]{1,0:T(8,128)S(1)} copy-done((s32[32,128]{1,0:T(8,128)S(1)}, s32[32,128]{1,0:T(8,128)}, u32[]{:S(2)}) %copy-start.4) | copy-done | bytes 16408
  3.2 0.7 %copy-done.6 = s32[32,128]{1,0:T(8,128)S(1)} copy-done((s32[32,128]{1,0:T(8,128)S(1)}, s32[32,128]{1,0:T(8,128)}, u32[]{:S(2)}) %copy-start.6) | copy-done | bytes 16408
  3.9 0.8 %copy-done.8 = f32[2,32,128]{2,1,0:T(8,128)S(1)} copy-done((f32[2,32,128]{2,1,0:T(8,128)S(1)}, f32[2,32,128]{2,1,0:T(8,128)}, u32[]{:S(2)}) %copy-start.8) | copy-done | bytes 32792
  4.6 1.0 %shard_map.94 = (f32[8,40,128]{2,1,0:T(8,128)}, f32[32,8,128]{2,1,0:T(8,128)S(1)}, f32[32,8,128]{2,1,0:T(8,128)S(1)}, f32[32,8,128]{2,1,0:T(8,128)S(1)}) custom-call(f32[256,128]{1,0:T(8,128)S(1)} %bitcast.6, f32[64,128]{1,0:T(8,128)S(1)} %bitcast.11, s32[32,128]{1,0:T(8,128)S(1)} %copy-done.4, s32[32,128]{1,0:T(8,128)S(1)} %copy-done.6, f32[256,128]{1,0:T(8,128)S(1)} %bitcast.9), custom_call_target="tpu_custom_call" | custom-call | tf_op jit(solution)/shard_map/pallas_call | solution.py:516
  5.7 4.4 %all-to-all-start = ((f32[8,40,128]{2,1,0:T(8,128)}), f32[8,40,128]{2,1,0:T(8,128)S(1)}, u32[]{:S(2)}, u32[]{:S(2)}) async-start(f32[8,40,128]{2,1,0:T(8,128)} %get-tuple-element.15), calls=%async_computation | async-start | bytes 327680 | tf_op jit(solution)/shard_map/all_to_all | solution.py:521
  10.1 0.0 copy-done.1
  10.1 0.0 copy-start.3
  10.1 0.1 shard_map.95
  10.3 3.8 %collective-permute-start = (f32[8,128]{1,0:T(8,128)S(1)}, f32[8,128]{1,0:T(8,128)S(1)}, u32[]{:S(2)}, u32[]{:S(2)}) collective-permute-start(f32[8,128]{1,0:T(8,128)S(1)} %get-tuple-element.16), channel_id=1, source_target_pairs={{0,1},{1,2},{2,3},{3,4},{4,5},{5,6},{6,7},{7,8},{8,9},{9,10},{10,1... | collective-permute-start | bytes 12296 | tf_op jit(solution)/shard_map/ppermute | solution.py:513
  14.1 2.0 %collective-permute-start.1 = (f32[8,128]{1,0:T(8,128)S(1)}, f32[8,128]{1,0:T(8,128)S(1)}, u32[]{:S(2)}, u32[]{:S(2)}) collective-permute-start(f32[8,128]{1,0:T(8,128)S(1)} %get-tuple-element.17), channel_id=1, source_target_pairs={{1,0},{2,1},{3,2},{4,3},{5,4},{6,5},{7,6},{8,7},{9,8},{10,9},{11,1... | collective-permute-start | bytes 12296 | tf_op jit(solution)/shard_map/ppermute | solution.py:514
  16.1 0.0 copy-done.9
  16.1 0.1 copy.10.weights_ref
  16.2 0.7 %copy-done.10 = f32[64]{0:T(128)S(1)} copy-done((f32[64]{0:T(128)S(1)}, f32[64]{0:T(128)}, u32[]{:S(2)}) %copy-start.10) | copy-done | bytes 280
  16.9 0.1 copy.11.out_ref
  17.0 0.0 collective-permute-done.low_ref
  17.0 2.6 %collective-permute-done.1.high_ref = f32[8,128]{1,0:T(8,128)S(1)} collective-permute-done((f32[8,128]{1,0:T(8,128)S(1)}, f32[8,128]{1,0:T(8,128)S(1)}, u32[]{:S(2)}, u32[]{:S(2)}) %collective-permute-start.1) | collective-permute-done | bytes 4128 | tf_op jit(solution)/shard_map/ppermute | solution.py:514
  19.6 0.0 all-to-all-done.got_ref
  19.6 0.0 copy-done.3
  19.6 0.0 copy-done.5
  19.6 0.0 copy-done.7
  19.6 5.7 %shard_map.96 = (f32[8,32,128]{2,1,0:T(8,128)S(1)}, f32[34,8,128]{2,1,0:T(8,128)S(1)}, f32[2,8,128]{2,1,0:T(8,128)S(1)}, f32[32,8,128]{2,1,0:T(8,128)S(1)}) custom-call(f32[8,40,128]{2,1,0:T(8,128)S(1)} %all-to-all-done.got_ref, f32[8,128]{1,0:T(8,128)S(1)} %collective-permute-done.low_ref, f32[8,128]{1,0:T(8,128)S(1)} %collective-permute-done.1.high_ref, ...), custom_call_target="tpu_custom_call" | custom-call | tf_op jit(solution)/shard_map/pallas_call | solution.py:534
  25.4 10.7 %all_to_all.15.second_ref.refs_1_ = f32[8,32,128]{2,1,0:T(8,128)S(1)} all-to-all(f32[8,32,128]{2,1,0:T(8,128)S(1)} %get-tuple-element.21), channel_id=1, replica_groups=mesh['gx'=8,'gy'=32] {'gx'}, dimensions={0} | all-to-all | bytes 262144 | tf_op jit(solution)/shard_map/all_to_all | solution.py:553
  36.1 0.7 %shard_map.98 = f32[32,8,128]{2,1,0:T(8,128)} custom-call(f32[8,32,128]{2,1,0:T(8,128)S(1)} %all_to_all.15.second_ref.refs_1_, f32[2,8,128]{2,1,0:T(8,128)S(1)} %get-tuple-element.23.rims_ref), custom_call_target="tpu_custom_call" | custom-call | tf_op jit(solution)/shard_map/pallas_call | solution.py:554
  36.8 11.2 %all-to-all-start.2 = ((f32[32,8,128]{2,1,0:T(8,128)}), f32[32,8,128]{2,1,0:T(8,128)S(1)}, u32[]{:S(2)}, u32[]{:S(2)}) async-start(f32[32,8,128]{2,1,0:T(8,128)} %shard_map.98), calls=%async_computation.2 | async-start | bytes 262144 | tf_op jit(solution)/shard_map/all_to_all | solution.py:557
  48.0 0.9 %shard_map.97 = f32[256,128]{1,0:T(8,128)} custom-call(f32[8,40,128]{2,1,0:T(8,128)S(1)} %all-to-all-done.got_ref, f32[8,32,128]{2,1,0:T(8,128)S(1)} %all_to_all.15.second_ref.refs_1_, f32[32,8,128]{2,1,0:T(8,128)S(1)} %get-tuple-element.22.rhs_ref, f32[32,8,128]{2,1,0:T(8,128)S(1)} %get-tuple-element.18.right_ref, f32[32,8,128]{2,1,0:T(8,128)S(1)} %get-tuple-element.19.recip_ref), custom_call_target="tpu_custom_call" | custom-call | tf_op jit(solution)/shard_map/pallas_call | solution.py:558
  48.9 8.8 %all-to-all-done.2.refs_0_ = f32[32,8,128]{2,1,0:T(8,128)S(1)} async-done(((f32[32,8,128]{2,1,0:T(8,128)}), f32[32,8,128]{2,1,0:T(8,128)S(1)}, u32[]{:S(2)}, u32[]{:S(2)}) %all-to-all-start.2) | async-done | bytes 131104 | tf_op jit(solution)/shard_map/all_to_all | solution.py:557
  57.6 0.8 %shard_map.99 = (f32[256,128]{1,0:T(8,128)}, f32[64,10]{1,0:T(8,128)S(1)}) custom-call(f32[32,8,128]{2,1,0:T(8,128)S(1)} %all-to-all-done.2.refs_0_, f32[8,32,128]{2,1,0:T(8,128)S(1)} %all_to_all.15.second_ref.refs_1_, f32[34,8,128]{2,1,0:T(8,128)S(1)} %get-tuple-element.24.refs_2_), custom_call_target="tpu_custom_call" | custom-call | tf_op jit(solution)/shard_map/pallas_call | solution.py:566
  58.5 0.7 %copy.12 = f32[64,10]{0,1:T(8,128)} copy(f32[64,10]{1,0:T(8,128)S(1)} %get-tuple-element.29) | data formatting | bytes 5120
  (8 shorter events, 0.0 us)
Async XLA Ops:
  0.6 0.9 %copy-start = (f32[4,2,32,128]{3,2,1,0:T(8,128)S(1)}, f32[4,2,32,128]{3,2,1,0:T(8,128)}, u32[]{:S(2)}) copy-start(f32[4,2,32,128]{3,2,1,0:T(8,128)} %param.7) | copy-start | bytes 393220
  1.5 0.9 %copy-start.2 = (f32[4,2,32,128]{3,2,1,0:T(8,128)S(1)}, f32[4,2,32,128]{3,2,1,0:T(8,128)}, u32[]{:S(2)}) copy-start(f32[4,2,32,128]{3,2,1,0:T(8,128)} %param.13) | copy-start | bytes 393220
  2.4 0.7 %copy-start.4 = (s32[32,128]{1,0:T(8,128)S(1)}, s32[32,128]{1,0:T(8,128)}, u32[]{:S(2)}) copy-start(s32[32,128]{1,0:T(8,128)} %sea_ref.3) | copy-start | bytes 49156
  3.2 0.7 %copy-start.6 = (s32[32,128]{1,0:T(8,128)S(1)}, s32[32,128]{1,0:T(8,128)}, u32[]{:S(2)}) copy-start(s32[32,128]{1,0:T(8,128)} %depth_ref.3) | copy-start | bytes 49156
  3.9 0.8 %copy-start.8 = (f32[2,32,128]{2,1,0:T(8,128)S(1)}, f32[2,32,128]{2,1,0:T(8,128)}, u32[]{:S(2)}) copy-start(f32[2,32,128]{2,1,0:T(8,128)} %param.8) | copy-start | bytes 98308
  5.7 4.4 %copy-start.1 = (f32[4,2,32,128]{3,2,1,0:T(8,128)S(1)}, f32[4,2,32,128]{3,2,1,0:T(8,128)}, u32[]{:S(2)}) copy-start(f32[4,2,32,128]{3,2,1,0:T(8,128)} %param.7) | copy-start | bytes 393220
  5.7 10.5 %copy-start.9 = (f32[64,9]{0,1:T(8,128)S(1)}, f32[64,9]{0,1:T(8,128)}, u32[]{:S(2)}) copy-start(f32[64,9]{0,1:T(8,128)} %param.11) | copy-start | bytes 6916
  5.7 13.9 %all-to-all-start = ((f32[8,40,128]{2,1,0:T(8,128)}), f32[8,40,128]{2,1,0:T(8,128)S(1)}, u32[]{:S(2)}, u32[]{:S(2)}) async-start(f32[8,40,128]{2,1,0:T(8,128)} %get-tuple-element.15), calls=%async_computation | async-start | bytes 327680 | tf_op jit(solution)/shard_map/all_to_all | solution.py:521
  10.1 9.5 %copy-start.3 = (f32[4,2,32,128]{3,2,1,0:T(8,128)S(1)}, f32[4,2,32,128]{3,2,1,0:T(8,128)}, u32[]{:S(2)}) copy-start(f32[4,2,32,128]{3,2,1,0:T(8,128)} %param.13) | copy-start | bytes 393220
  10.3 6.7 %collective-permute-start = (f32[8,128]{1,0:T(8,128)S(1)}, f32[8,128]{1,0:T(8,128)S(1)}, u32[]{:S(2)}, u32[]{:S(2)}) collective-permute-start(f32[8,128]{1,0:T(8,128)S(1)} %get-tuple-element.16), channel_id=1, source_target_pairs={{0,1},{1,2},{2,3},{3,4},{4,5},{5,6},{6,7},{7,8},{8,9},{9,10},{10,1... | collective-permute-start | bytes 12296 | tf_op jit(solution)/shard_map/ppermute | solution.py:513
  14.1 5.5 %collective-permute-start.1 = (f32[8,128]{1,0:T(8,128)S(1)}, f32[8,128]{1,0:T(8,128)S(1)}, u32[]{:S(2)}, u32[]{:S(2)}) collective-permute-start(f32[8,128]{1,0:T(8,128)S(1)} %get-tuple-element.17), channel_id=1, source_target_pairs={{1,0},{2,1},{3,2},{4,3},{5,4},{6,5},{7,6},{8,7},{9,8},{10,9},{11,1... | collective-permute-start | bytes 12296 | tf_op jit(solution)/shard_map/ppermute | solution.py:514
  16.2 0.7 %copy-start.10 = (f32[64]{0:T(128)S(1)}, f32[64]{0:T(128)}, u32[]{:S(2)}) copy-start(f32[64]{0:T(128)} %param.12) | copy-start | bytes 772
  16.9 2.7 %copy-start.5 = (s32[32,128]{1,0:T(8,128)S(1)}, s32[32,128]{1,0:T(8,128)}, u32[]{:S(2)}) copy-start(s32[32,128]{1,0:T(8,128)} %sea_ref.3) | copy-start | bytes 49156
  16.9 2.7 %copy-start.7 = (s32[32,128]{1,0:T(8,128)S(1)}, s32[32,128]{1,0:T(8,128)}, u32[]{:S(2)}) copy-start(s32[32,128]{1,0:T(8,128)} %depth_ref.3) | copy-start | bytes 49156
  36.8 20.9 %all-to-all-start.2 = ((f32[32,8,128]{2,1,0:T(8,128)}), f32[32,8,128]{2,1,0:T(8,128)S(1)}, u32[]{:S(2)}, u32[]{:S(2)}) async-start(f32[32,8,128]{2,1,0:T(8,128)} %shard_map.98), calls=%async_computation.2 | async-start | bytes 262144 | tf_op jit(solution)/shard_map/all_to_all | solution.py:557

commit v2 on v1

--- a/solution.py
+++ b/solution.py
@@ -16,7 +16,7 @@
 NY = 128
 ROWS = 8
 XS = 4
-RIM = 80
+RIM = 64
 
 
 def iota(shape, dim):
@@ -58,12 +58,12 @@
     return high, (values - high.astype(F32)).astype(BF16)
 
 
-def columns_kernel(state_ref, first_ref, last_ref):
+def columns_kernel(fields_ref, first_ref, last_ref):
     lanes = lanes8()
     first = jnp.zeros((ROWS, NY), F32)
     last = jnp.zeros((ROWS, NY), F32)
     for x in range(NX):
-        here = line(state_ref, x)
+        here = fields_ref[x]
         first = jnp.where(lanes == x, pltpu.roll(here, x, 1) if x else here, first)
         last = jnp.where(lanes == x, pltpu.roll(here, x + 1, 1), last)
     first_ref[...] = first
@@ -71,36 +71,75 @@
 
 
 def factor_kernel(
-    state_ref, diff_ref, sea_ref, depth_ref, cot_ref, send_ref, right_ref, recip_ref, left_ref
+    state_hbm,
+    diff_hbm,
+    sea_hbm,
+    depth_hbm,
+    cot_hbm,
+    send_ref,
+    right_ref,
+    recip_ref,
+    left_ref,
+    fields_ref,
+    wets_ref,
+    cots_ref,
+    state_ref,
+    diff_ref,
+    sea_ref,
+    depth_ref,
+    cot_ref,
+    sems,
 ):
+    copies = [
+        pltpu.make_async_copy(source, target, sems.at[n])
+        for n, (source, target) in enumerate(
+            (
+                (sea_hbm, sea_ref),
+                (depth_hbm, depth_ref),
+                (diff_hbm, diff_ref),
+                (cot_hbm, cot_ref),
+                (state_hbm, state_ref),
+            )
+        )
+    ]
+    for copy in copies:
+        copy.start()
     me = lax.axis_index("gx")
     count = send_ref.shape[0]
     row = rows8()
+    for copy in copies[:3]:
+        copy.wait()
     wet = [wet_line(sea_ref, depth_ref, x) for x in range(NX)]
+    for x in range(NX):
+        wets_ref[x] = wet[x]
     rates = rates8()
     bare = [
         by_level(diff_ref[x : x + 1, :], diff_ref[NX + x : NX + x + 1, :]) * wet[x]
         for x in range(NX)
     ]
     cond = [rates * bare[x] * wet[x + 1] for x in range(NX - 1)]
+    copies[3].wait()
     mass = jnp.ones((ROWS, NY), F32)
     carry = jnp.ones((ROWS, NY), F32)
-    load = line(cot_ref, 0)
     mass_back = jnp.ones((ROWS, NY), F32)
-    load_back = line(cot_ref, NX - 1)
+    cots = [line(cot_ref, x) for x in range(NX)]
+    for x in range(NX):
+        cots_ref[x] = cots[x]
+    load = cots[0]
+    load_back = cots[NX - 1]
     for i in range(NX - 1):
         recip = 1.0 / (mass + cond[i])
         ratio = cond[i] * recip
         right_ref[i] = ratio
         recip_ref[i] = recip
         mass = 1.0 + mass * ratio
-        load = line(cot_ref, i + 1) + ratio * load
+        load = cots[i + 1] + ratio * load
         carry = carry * ratio
         j = NX - 2 - i
         ratio_back = cond[j] / (mass_back + cond[j])
         left_ref[j] = ratio_back
         mass_back = 1.0 + mass_back * ratio_back
-        load_back = line(cot_ref, j) + ratio_back * load_back
+        load_back = cots[j] + ratio_back * load_back
     last_self = 1.0 / mass
     first_self = 1.0 / mass_back
     right_ref[NX - 1] = jnp.zeros((ROWS, NY), F32)
@@ -108,6 +147,9 @@
     recip_ref[NX - 1] = last_self
     across = carry * last_self
     upper = (row & 2) == 0
+    copies[4].wait()
+    for x in range(NX):
+        fields_ref[x] = line(state_ref, x)
     tiles = [
         load_back * first_self,
         load * last_self,
@@ -185,69 +227,77 @@
         write(i, value)
 
 
-def network(weights_ref, out_ref):
+def network_kernel(weights_ref, out_ref, forward_ref, back_ref, outw_ref):
     weights = weights_ref[...]
-    where_to = []
+    per_level = []
     for level in range(2):
-        spread = (iota((FEAT + 1, 128), 1) == 2 * iota((FEAT + 1, 128), 0) + level) & (
-            iota((FEAT + 1, 128), 0) < FEAT
-        )
-        where_to.append(
+        spread = iota((16, FEAT + 1), 0) == 2 * iota((16, FEAT + 1), 1) + level
+        per_level.append(
             jnp.dot(
+                spread.astype(F32),
                 weights,
-                spread.astype(F32),
                 precision=lax.Precision.HIGHEST,
                 preferred_element_type=F32,
             )
         )
-    both = jnp.concatenate(where_to, 0)
+    both = jnp.concatenate(per_level, 1)
     high = both.astype(BF16).astype(F32)
     low = both - high
-    bias = weights[:, FEAT : FEAT + 1]
-    bias = jnp.broadcast_to(jnp.concatenate([bias, bias], 0), (2 * HID, 128))
+    bias = weights[FEAT : FEAT + 1, :]
+    bias = jnp.broadcast_to(jnp.concatenate([bias, bias], 1), (16, 2 * HID))
     bias_high = bias.astype(BF16).astype(F32)
     bias_mid = (bias - bias_high).astype(BF16).astype(F32)
     bias_low = bias - bias_high - bias_mid
-    lane = iota((2 * HID, 128), 1)
-    forward = high + pltpu.roll(high, 16, 1) + pltpu.roll(low, 48, 1) + pltpu.roll(low, 64, 1)
-    forward = jnp.where(lane == 32, bias_high, forward)
-    forward = jnp.where(lane == 33, bias_mid, forward)
-    forward = jnp.where(lane == 34, bias_low, forward)
-    turned = jnp.transpose(high + pltpu.roll(low, 16, 1))[:32]
-    back = jnp.concatenate([turned, turned], 1)
+    row = iota((16, 2 * HID), 0)
+    bias = jnp.where(
+        row == 0, bias_high, jnp.where(row == 1, bias_mid, jnp.where(row == 2, bias_low, 0.0))
+    )
+    stack = jnp.concatenate([high, high, bias, low, low, jnp.zeros((48, 2 * HID), F32)], 0)
+    forward_ref[...] = jnp.transpose(stack).astype(BF16)
+    turned = jnp.concatenate([high, low], 0)
+    back_ref[...] = jnp.concatenate([turned, turned], 1).astype(BF16)
     out = out_ref[...]
-    out = jnp.broadcast_to(jnp.concatenate([out, out], 0), (2 * HID, 128))
-    return forward.astype(BF16), back.astype(BF16), out
+    out = jnp.broadcast_to(jnp.concatenate([out, out], 1), (2 * HID, 2 * HID))
+    outw_ref[...] = jnp.transpose(out)
+
+
+def pack(features, bias, out):
+    blank = jnp.zeros((ROWS, HID), F32)
+    row = iota((ROWS, 32), 0)
+    ends = [
+        jnp.broadcast_to(v, (ROWS, 32))
+        for v in (bias[:, 0:32], bias[:, 32:64], out[:, 0:32], out[:, 32:64])
+    ]
+    tail = jnp.zeros((ROWS, 32), F32)
+    for n, end in enumerate(ends):
+        tail = jnp.where(row == n, end, tail)
+    return jnp.concatenate([features, blank[:, :32], tail], 1)
 
 
 def main_kernel(
     got_ref,
     low_ref,
     high_ref,
-    state_ref,
-    sea_ref,
-    depth_ref,
-    cot_ref,
+    lines_ref,
+    wets,
+    cots_ref,
     right_ref,
     recip_ref,
     left_ref,
-    weights_ref,
-    out_ref,
+    forward_ref,
+    back_ref,
+    outw_ref,
     send_ref,
     grad_ref,
     rims_ref,
     rhs_ref,
     fields,
-    wets,
     adj,
     slope_x,
     slope_y,
     curve_x,
     curve_y,
     feats,
-    forward_ref,
-    back_ref,
-    outw_ref,
     sums_ref,
     out_sums_ref,
 ):
@@ -260,8 +310,7 @@
     zero = jnp.zeros((ROWS, NY), F32)
 
     for x in range(NX):
-        wets[x] = wet_line(sea_ref, depth_ref, x)
-        fields[x + 1] = line(state_ref, x)
+        fields[x + 1] = lines_ref[x]
     below = got_ref[jnp.maximum(me - 1, 0), 32:40, :]
     above = got_ref[jnp.minimum(me + 1, count - 1), 32:40, :]
     fields[0] = jnp.where(me > 0, below, zero)
@@ -275,10 +324,10 @@
     def keep(x, value):
         adj[x] = wets[x] * value
 
-    own_lines(lambda x: line(cot_ref, x), right_ref, recip_ref, fluxes, keep)
-
-    low = low_ref[...]
-    high = high_ref[...]
+    own_lines(lambda x: cots_ref[x], right_ref, recip_ref, fluxes, keep)
+
+    low = jnp.where(here_y > 0, low_ref[...], zero)
+    high = jnp.where(here_y < lax.axis_size("gy") - 1, high_ref[...], zero)
     feats[32:48, :] = jnp.ones((16, NX * NY), BF16)
     for x in range(NX):
         center = fields[x + 1]
@@ -301,10 +350,6 @@
         feats[48:64, place] = part_high
         feats[64:80, place] = part_low
 
-    forward, back, outw = network(weights_ref, out_ref)
-    forward_ref[...] = forward
-    back_ref[...] = back
-    outw_ref[...] = outw
     sums_ref[...] = jnp.zeros(sums_ref.shape, F32)
     out_sums_ref[...] = jnp.zeros(out_sums_ref.shape, F32)
     grad_ref[...] = jnp.zeros(grad_ref.shape, F32)
@@ -406,25 +451,27 @@
     last_own = load * recip_ref[NX - 1]
 
     sums = sums_ref[0:128] + sums_ref[128:256]
-    total = jnp.zeros((HID, 128), F32)
+    total = jnp.zeros((16, HID), F32)
     for level in range(2):
-        source = iota((48, 128), 0)
-        target = iota((48, 128), 1)
+        source = iota((16, 48), 1)
+        target = iota((16, 48), 0)
         feature = (source < 32) & ((source & 15) == 2 * target + level) & (target < FEAT)
         gather = feature | ((source == 32) & (target == FEAT))
-        total += jnp.dot(
+        total += lax.dot_general(
+            gather.astype(F32),
             sums[level * HID : (level + 1) * HID],
-            gather.astype(F32),
+            (((1,), (1,)), ((), ())),
             precision=lax.Precision.HIGHEST,
             preferred_element_type=F32,
         )
-    out_total = jnp.sum(out_sums_ref[0:HID] + out_sums_ref[HID:], 1, keepdims=True)
-    total = jnp.where(iota((HID, 128), 1) == FEAT + 1, out_total, total)
-    packed = zero
-    for a in range(HID // 8):
-        piece = total[8 * a : 8 * (a + 1)]
-        piece = pltpu.roll(piece, 10 * a, 1) if a else piece
-        packed = jnp.where((lanes >= 10 * a) & (lanes < 10 * a + 10), piece, packed)
+    out_total = lax.dot_general(
+        jnp.ones((8, 128), F32),
+        out_sums_ref[0:HID] + out_sums_ref[HID:],
+        (((1,), (1,)), ((), ())),
+        precision=lax.Precision.HIGHEST,
+        preferred_element_type=F32,
+    )
+    packed = pack(total[0:8], total[8:9], out_total[0:1])
     to_last = grad_ref[NX + 1]
     to_first = grad_ref[0]
     for j in range(count):
@@ -434,21 +481,21 @@
         send_ref[j, 24:32, :] = jnp.where(j > me, to_last, to_first)
 
 
-def share_kernel(second_ref, rims_ref, send_ref):
-    me = lax.axis_index("gy")
+def share_kernel(
+    second_ref, rims_ref, got_ref, rhs_ref, right_ref, recip_ref, send_ref, final_ref
+):
+    me_y = lax.axis_index("gy")
+    me = lax.axis_index("gx")
+    count = got_ref.shape[0]
     lanes = lanes8()
     total = second_ref[0, 16:24, :]
-    for j in range(1, second_ref.shape[0]):
+    for j in range(1, count):
         total = total + second_ref[j, 16:24, :]
-    upward = jnp.where(lanes < RIM, total, rims_ref[0])
-    downward = jnp.where(lanes < RIM, total, rims_ref[1])
+    rim = (lanes >= RIM) & (lanes < RIM + NX)
+    upward = jnp.where(rim, rims_ref[0], total)
+    downward = jnp.where(rim, rims_ref[1], total)
     for j in range(send_ref.shape[0]):
-        send_ref[j] = jnp.where(j > me, upward, downward)
-
-
-def final_kernel(got_ref, second_ref, rhs_ref, right_ref, recip_ref, final_ref):
-    me = lax.axis_index("gx")
-    count = got_ref.shape[0]
+        send_ref[j] = jnp.where(j > me_y, upward, downward)
     system = reduced(got_ref)
     first = [second_ref[j, 0:8, :] for j in range(count)]
     last = [second_ref[j, 8:16, :] for j in range(count)]
@@ -460,20 +507,17 @@
     own_lines(lambda x: rhs_ref[x], right_ref, recip_ref, fluxes, keep)
 
 
-def finish_kernel(factor, third_ref, second_ref, grad_ref, out_ref, closure_ref):
+def finish_kernel(
+    factor, third_ref, second_ref, grad_ref, final_ref, final_hbm, out_hbm, closure_ref, out_ref, sems
+):
+    copy = pltpu.make_async_copy(final_ref, final_hbm, sems.at[0])
+    copy.start()
     me_x = lax.axis_index("gx")
     me_y = lax.axis_index("gy")
     count_x = second_ref.shape[0]
     count_y = third_ref.shape[0]
     lanes = lanes8()
     zero = jnp.zeros((ROWS, NY), F32)
-    parts = [third_ref[j] for j in range(count_y)]
-    while len(parts) > 1:
-        parts = [a + b for a, b in zip(parts[::2], parts[1::2])]
-    total = parts[0] * factor
-    for a in range(HID // 8):
-        piece = pltpu.roll(total, NY - 10 * a, 1) if a else total
-        closure_ref[8 * a : 8 * (a + 1), :] = piece[:, 0:10]
     before = jnp.where(me_x > 0, second_ref[jnp.maximum(me_x - 1, 0), 24:32, :], zero)
     after = jnp.where(
         me_x < count_x - 1, second_ref[jnp.minimum(me_x + 1, count_x - 1), 24:32, :], zero
@@ -489,6 +533,19 @@
         value = value + jnp.where(lanes == 0, pltpu.roll(south, NY - RIM - x, 1), 0.0)
         value = value + jnp.where(lanes == NY - 1, pltpu.roll(north, NY - 1 - RIM - x, 1), 0.0)
         out_ref[pl.ds(x, ROWS, stride=NX), :] = value
+    copy_out = pltpu.make_async_copy(out_ref, out_hbm, sems.at[1])
+    copy_out.start()
+    parts = [third_ref[j] for j in range(count_y)]
+    while len(parts) > 1:
+        parts = [a + b for a, b in zip(parts[::2], parts[1::2])]
+    total = parts[0] * factor
+    closure_ref[0:8, :] = total[:, 0:HID]
+    for n in range(2):
+        closure_ref[8 + n : 9 + n, :] = jnp.concatenate(
+            [total[2 * n : 2 * n + 1, 96:], total[2 * n + 1 : 2 * n + 2, 96:]], 1
+        )
+    copy.wait()
+    copy_out.wait()
 
 
 def tile(*shape):
@@ -502,31 +559,49 @@
 def per_device(state, diffusivity, sea_mask, depth_index, closure_in, closure_out, cotangent):
     count_x = lax.axis_size("gx")
     count_y = lax.axis_size("gy")
-    flat_state = state.reshape(ROWS * NX, NY)
-    flat_cot = cotangent.reshape(ROWS * NX, NY)
-    flat_diff = diffusivity.reshape(2 * NX, NY)
+    lines = tile(NX, ROWS, NY)
+    in_hbm = pl.BlockSpec(memory_space=pltpu.HBM)
+    in_vmem = pl.BlockSpec(memory_space=pltpu.VMEM)
+    send, right, recip, left, fields, wets, cots = pl.pallas_call(
+        factor_kernel,
+        in_specs=[in_hbm] * 5,
+        out_shape=(tile(count_x, 40, NY),) + (lines,) * 6,
+        scratch_shapes=[
+            pltpu.VMEM((ROWS * NX, NY), F32),
+            pltpu.VMEM((2 * NX, NY), F32),
+            pltpu.VMEM((NX, NY), jnp.int32),
+            pltpu.VMEM((NX, NY), jnp.int32),
+            pltpu.VMEM((ROWS * NX, NY), F32),
+            pltpu.SemaphoreType.DMA((5,)),
+        ],
+        compiler_params=params(),
+    )(
+        state.reshape(ROWS * NX, NY),
+        diffusivity.reshape(2 * NX, NY),
+        sea_mask,
+        depth_index,
+        cotangent.reshape(ROWS * NX, NY),
+    )
+    got = lax.all_to_all(send, "gx", 0, 0, tiled=True)
     first, last = pl.pallas_call(
         columns_kernel, out_shape=(tile(8, NY), tile(8, NY)), compiler_params=params()
-    )(flat_state)
-    upward = [(i, i + 1) for i in range(count_y - 1)]
-    downward = [(i + 1, i) for i in range(count_y - 1)]
-    low = lax.ppermute(last, "gy", upward)
-    high = lax.ppermute(first, "gy", downward)
-    lines = tile(NX, ROWS, NY)
-    send, right, recip, left = pl.pallas_call(
-        factor_kernel,
-        out_shape=(tile(count_x, 40, NY), lines, lines, lines),
+    )(fields)
+    low = lax.ppermute(last, "gy", [(i, (i + 1) % count_y) for i in range(count_y)])
+    high = lax.ppermute(first, "gy", [((i + 1) % count_y, i) for i in range(count_y)])
+    forward, back, outw = pl.pallas_call(
+        network_kernel,
+        out_shape=(
+            jax.ShapeDtypeStruct((2 * HID, 128), BF16),
+            jax.ShapeDtypeStruct((32, 256), BF16),
+            tile(2 * HID, 128),
+        ),
         compiler_params=params(),
-    )(flat_state, flat_diff, sea_mask, depth_index, flat_cot)
-    got = lax.all_to_all(send, "gx", 0, 0, tiled=True)
+    )(closure_in.T, closure_out.reshape(1, HID))
     scratch = (
         [pltpu.VMEM((NX + 2, ROWS, NY), F32)]
-        + [pltpu.VMEM((NX, ROWS, NY), F32)] * 6
+        + [pltpu.VMEM((NX, ROWS, NY), F32)] * 5
         + [
             pltpu.VMEM((80, NX * NY), BF16),
-            pltpu.VMEM((2 * HID, 128), BF16),
-            pltpu.VMEM((32, 256), BF16),
-            pltpu.VMEM((2 * HID, 128), F32),
             pltpu.VMEM((4 * HID, 48), F32),
             pltpu.VMEM((2 * HID, 128), F32),
         ]
@@ -536,37 +611,28 @@
         out_shape=(tile(count_x, 32, NY), tile(NX + 2, ROWS, NY), tile(2, ROWS, NY), lines),
         scratch_shapes=scratch,
         compiler_params=params(),
-    )(
-        got,
-        low,
-        high,
-        flat_state,
-        sea_mask,
-        depth_index,
-        flat_cot,
-        right,
-        recip,
-        left,
-        closure_in,
-        closure_out.reshape(HID, 1),
-    )
+    )(got, low, high, fields, wets, cots, right, recip, left, forward, back, outw)
     second = lax.all_to_all(send, "gx", 0, 0, tiled=True)
-    send = pl.pallas_call(
-        share_kernel, out_shape=tile(count_y, ROWS, NY), compiler_params=params()
-    )(second, rims)
+    send, final = pl.pallas_call(
+        share_kernel,
+        out_shape=(tile(count_y, ROWS, NY), tile(ROWS * NX, NY)),
+        compiler_params=params(),
+    )(second, rims, got, rhs, right, recip)
     third = lax.all_to_all(send, "gy", 0, 0, tiled=True)
-    final = pl.pallas_call(
-        final_kernel, out_shape=tile(ROWS * NX, NY), compiler_params=params()
-    )(got, second, rhs, right, recip)
     factor = 1.0 / math.sqrt(2 * NX * count_x * NY * count_y)
 
     def finish(*refs):
         finish_kernel(factor, *refs)
 
-    state_grad, closure_grad = pl.pallas_call(
-        finish, out_shape=(tile(ROWS * NX, NY), tile(HID, 10)), compiler_params=params()
-    )(third, second, grad)
-    return (final.reshape(state.shape), state_grad.reshape(state.shape), closure_grad)
+    final, state_grad, closure_grad = pl.pallas_call(
+        finish,
+        in_specs=[in_vmem] * 4,
+        out_shape=(tile(ROWS * NX, NY), tile(ROWS * NX, NY), tile(10, HID)),
+        out_specs=(in_hbm, in_hbm, in_vmem),
+        scratch_shapes=[pltpu.VMEM((ROWS * NX, NY), F32), pltpu.SemaphoreType.DMA((2,))],
+        compiler_params=params(),
+    )(third, second, grad, final)
+    return (final.reshape(state.shape), state_grad.reshape(state.shape), closure_grad.T)
 
 
 def solution(mesh):

time: 59.8 us -> 55.8 us (0.933)
  blocking collectives: 10.7 us -> 30.8 us
  starting transfers between devices: 21.5 us -> 6.41 us
  waiting for transfers between devices: 11.4 us -> 3.28 us
  local copies, waits for them, and re-layouts: 5.53 us -> 4.65 us
    all_to_all x0 -> x1, blocking collectives: none -> 20.8 us  [per_device(): third = lax.all_to_all(send, 'gy', 0, 0, tiled=True)]
    all_to_all x1 -> x0, starting transfers between devices: 11.2 us -> none  [per_device(): third = lax.all_to_all(send, 'gy', 0, 0, tiled=True)]
    all_to_all x1 -> x0, waiting for transfers between devices: 8.76 us -> none  [per_device(): third = lax.all_to_all(send, 'gy', 0, 0, tiled=True)]
    ppermute x2, starting transfers between devices: 5.83 us -> 2.1 us  [the longest x1 1.99 us: per_device(): lax.ppermute(last, 'gy', [(i, (i + 1) % count_y) for i in range(count_y)])]
    unnamed x24 -> x14, local copies, waits for them, and re-layouts: 5.44 us -> 4.65 us
    all_to_all x1, waiting for transfers between devices: 0.01 us -> 0.75 us  [per_device(): got = lax.all_to_all(send, 'gx', 0, 0, tiled=True)]
    all_to_all x1, blocking collectives: 10.7 us -> 10 us  [per_device(): second = lax.all_to_all(send, 'gx', 0, 0, tiled=True)]
  transfers between devices with their start and end apart: 4 -> 3, of which waited for: 2 -> 3; matrix products, arithmetic and copies ran while one was open for 0% -> 0% of each run, Pallas kernels for 2% -> 1%
where the time goes in v2:
time: 55.8 us; the launch traced here: 55.3 us
  blocking collectives  30.8 us (55%)
  Pallas kernels  9.46 us (17%)
  starting transfers between devices  6.41 us (11%)
  local copies, waits for them, and re-layouts  4.65 us (8%)
  waiting for transfers between devices  3.28 us (6%)
  between operations  0.68 us (1%)
    all_to_all x1, blocking collectives, per_device(): third = lax.all_to_all(send, 'gy', 0, 0, tiled=True)  20.8 us
    all_to_all x1, blocking collectives, per_device(): second = lax.all_to_all(send, 'gx', 0, 0, tiled=True)  10 us
    pallas_call x1, Pallas kernels, per_device(): pl.pallas_call(main_kernel, out_shape=(tile(count_x, 32, NY), tile(NX + 2...  5.7 us
    unnamed x14, local copies, waits for them, and re-layouts  4.65 us
    all_to_all x1, starting transfers between devices, per_device(): got = lax.all_to_all(send, 'gx', 0, 0, tiled=True)  4.31 us
    ppermute x1, starting transfers between devices, per_device(): lax.ppermute(last, 'gy', [(i, (i + 1) % count_y) for i in range(count_y)])  1.99 us
    ppermute x1, waiting for transfers between devices, per_device(): lax.ppermute(first, 'gy', [((i + 1) % count_y, i) for i in range(count_y)])  1.92 us
    pallas_call x1, Pallas kernels, per_device(): pl.pallas_call(factor_kernel, in_specs=[in_hbm] * 5, out_shape=(tile(coun...  1.63 us
  transfers between devices with their start and end apart: 3, of which 3 were waited for; matrix products, arithmetic and copies ran while one was open for 0% of the time, Pallas kernels for 1%

profile of v2, /device:TPU:32, one launch (start us, length us, event | category | flops | bytes accessed | tf_op | source)
XLA Modules:
  0.0 55.3 jit_solution(14432457296262491745)
XLA Ops:
  0.6 0.0 copy-start
  0.6 0.9 %copy-done = f32[4,2,32,128]{3,2,1,0:T(8,128)S(1)} copy-done((f32[4,2,32,128]{3,2,1,0:T(8,128)S(1)}, f32[4,2,32,128]{3,2,1,0:T(8,128)}, u32[]{:S(2)}) %copy-start) | copy-done | bytes 131096
  1.5 0.0 copy-start.1
  1.5 0.9 %copy-done.1 = f32[4,2,32,128]{3,2,1,0:T(8,128)S(1)} copy-done((f32[4,2,32,128]{3,2,1,0:T(8,128)S(1)}, f32[4,2,32,128]{3,2,1,0:T(8,128)}, u32[]{:S(2)}) %copy-start.1) | copy-done | bytes 131096
  2.4 0.0 copy-start.2
  2.4 0.8 %copy-done.2 = f32[2,32,128]{2,1,0:T(8,128)S(1)} copy-done((f32[2,32,128]{2,1,0:T(8,128)S(1)}, f32[2,32,128]{2,1,0:T(8,128)}, u32[]{:S(2)}) %copy-start.2) | copy-done | bytes 32792
  3.2 0.0 copy-start.3
  3.2 0.7 %copy-done.3 = s32[32,128]{1,0:T(8,128)S(1)} copy-done((s32[32,128]{1,0:T(8,128)S(1)}, s32[32,128]{1,0:T(8,128)}, u32[]{:S(2)}) %copy-start.3) | copy-done | bytes 16408
  3.9 0.0 copy-start.4
  3.9 0.7 %copy-done.4 = s32[32,128]{1,0:T(8,128)S(1)} copy-done((s32[32,128]{1,0:T(8,128)S(1)}, s32[32,128]{1,0:T(8,128)}, u32[]{:S(2)}) %copy-start.4) | copy-done | bytes 16408
  4.6 1.6 %shard_map.94 = (f32[8,40,128]{2,1,0:T(8,128)}, f32[32,8,128]{2,1,0:T(8,128)S(1)}, f32[32,8,128]{2,1,0:T(8,128)S(1)}, f32[32,8,128]{2,1,0:T(8,128)S(1)}, f32[32,...) custom-call(f32[256,128]{1,0:T(8,128)S(1)} %bitcast.8, f32[64,128]{1,0:T(8,128)S(1)} %bitcast.10, ...), custom_call_target="tpu_custom_call" | custom-call | tf_op jit(solution)/shard_map/pallas_call | solution.py:565
  6.3 4.3 %all-to-all-start = ((f32[8,40,128]{2,1,0:T(8,128)}), f32[8,40,128]{2,1,0:T(8,128)S(1)}, u32[]{:S(2)}, u32[]{:S(2)}) async-start(f32[8,40,128]{2,1,0:T(8,128)} %get-tuple-element.24), calls=%async_computation | async-start | bytes 327680 | tf_op jit(solution)/shard_map/all_to_all | solution.py:585
  10.6 0.0 copy-start.5
  10.6 0.1 shard_map.95
  10.7 2.0 %collective-permute-start = (f32[8,128]{1,0:T(8,128)S(1)}, f32[8,128]{1,0:T(8,128)S(1)}, u32[]{:S(2)}, u32[]{:S(2)}) collective-permute-start(f32[8,128]{1,0:T(8,128)S(1)} %get-tuple-element.26), channel_id=1, source_target_pairs={{0,1},{1,2},{2,3},{3,4},{4,5},{5,6},{6,7},{7,8},{8,9},{9,10},{10,1... | collective-permute-start | bytes 12296 | tf_op jit(solution)/shard_map/ppermute | solution.py:589
  12.7 0.1 collective-permute-start.1
  12.8 0.0 copy-start.6
  12.8 0.0 copy-done.5
  12.8 0.7 %copy-done.6 = f32[64]{0:T(128)S(1)} copy-done((f32[64]{0:T(128)S(1)}, f32[64]{0:T(128)}, u32[]{:S(2)}) %copy-start.6) | copy-done | bytes 280
  13.5 0.3 shard_map.96
  13.8 0.6 %collective-permute-done.low_ref = f32[8,128]{1,0:T(8,128)S(1)} collective-permute-done((f32[8,128]{1,0:T(8,128)S(1)}, f32[8,128]{1,0:T(8,128)S(1)}, u32[]{:S(2)}, u32[]{:S(2)}) %collective-permute-start) | collective-permute-done | bytes 4128 | tf_op jit(solution)/shard_map/ppermute | solution.py:589
  14.4 1.9 %collective-permute-done.1.high_ref = f32[8,128]{1,0:T(8,128)S(1)} collective-permute-done((f32[8,128]{1,0:T(8,128)S(1)}, f32[8,128]{1,0:T(8,128)S(1)}, u32[]{:S(2)}, u32[]{:S(2)}) %collective-permute-start.1) | collective-permute-done | bytes 4128 | tf_op jit(solution)/shard_map/ppermute | solution.py:590
  16.3 0.7 %all-to-all-done.got_ref = f32[8,40,128]{2,1,0:T(8,128)S(1)} async-done(((f32[8,40,128]{2,1,0:T(8,128)}), f32[8,40,128]{2,1,0:T(8,128)S(1)}, u32[]{:S(2)}, u32[]{:S(2)}) %all-to-all-start) | async-done | bytes 163872 | tf_op jit(solution)/shard_map/all_to_all | solution.py:585
  17.1 5.7 %shard_map.97 = (f32[8,32,128]{2,1,0:T(8,128)S(1)}, f32[34,8,128]{2,1,0:T(8,128)S(1)}, f32[2,8,128]{2,1,0:T(8,128)S(1)}, f32[32,8,128]{2,1,0:T(8,128)S(1)}) custom-call(f32[8,40,128]{2,1,0:T(8,128)S(1)} %all-to-all-done.got_ref, f32[8,128]{1,0:T(8,128)S(1)} %collective-permute-done.low_ref, f32[8,128]{1,0:T(8,128)S(1)} %collective-permute-done.1.high_ref, ...), custom_call_target="tpu_custom_call" | custom-call | tf_op jit(solution)/shard_map/pallas_call | solution.py:609
  22.8 10.0 %all_to_all.15.second_ref.refs_1_ = f32[8,32,128]{2,1,0:T(8,128)S(1)} all-to-all(f32[8,32,128]{2,1,0:T(8,128)S(1)} %get-tuple-element.36), channel_id=1, replica_groups=mesh['gx'=8,'gy'=32] {'gx'}, dimensions={0} | all-to-all | bytes 262144 | tf_op jit(solution)/shard_map/all_to_all | solution.py:615
  32.8 0.3 shard_map.98
  33.1 20.8 %all_to_all.16.refs_0_ = f32[32,8,128]{2,1,0:T(8,128)S(1)} all-to-all(f32[32,8,128]{2,1,0:T(8,128)S(1)} %get-tuple-element.39), channel_id=1, replica_groups=mesh['gx'=8,'gy'=32] {'gy'}, dimensions={0} | all-to-all | bytes 262144 | tf_op jit(solution)/shard_map/all_to_all | solution.py:621
  53.9 1.4 %shard_map.99 = (f32[256,128]{1,0:T(8,128)}, f32[256,128]{1,0:T(8,128)}, f32[10,64]{1,0:T(8,128)}) custom-call(f32[32,8,128]{2,1,0:T(8,128)S(1)} %all_to_all.16.refs_0_, f32[8,32,128]{2,1,0:T(8,128)S(1)} %all_to_all.15.second_ref.refs_1_, f32[34,8,128]{2,1,0:T(8,128)S(1)} %get-tuple-element.40.refs_2_, f32[256,128]{1,0:T(8,128)S(1)} %get-tuple-element.41.refs_3_), custom_call_target="tpu_custom_call" | custom-call | tf_op jit(solution)/shard_map/pallas_call | solution.py:627
Async XLA Ops:
  0.6 0.9 %copy-start = (f32[4,2,32,128]{3,2,1,0:T(8,128)S(1)}, f32[4,2,32,128]{3,2,1,0:T(8,128)}, u32[]{:S(2)}) copy-start(f32[4,2,32,128]{3,2,1,0:T(8,128)} %param.7) | copy-start | bytes 393220
  1.5 0.9 %copy-start.1 = (f32[4,2,32,128]{3,2,1,0:T(8,128)S(1)}, f32[4,2,32,128]{3,2,1,0:T(8,128)}, u32[]{:S(2)}) copy-start(f32[4,2,32,128]{3,2,1,0:T(8,128)} %param.13) | copy-start | bytes 393220
  2.4 0.8 %copy-start.2 = (f32[2,32,128]{2,1,0:T(8,128)S(1)}, f32[2,32,128]{2,1,0:T(8,128)}, u32[]{:S(2)}) copy-start(f32[2,32,128]{2,1,0:T(8,128)} %param.8) | copy-start | bytes 98308
  3.2 0.7 %copy-start.3 = (s32[32,128]{1,0:T(8,128)S(1)}, s32[32,128]{1,0:T(8,128)}, u32[]{:S(2)}) copy-start(s32[32,128]{1,0:T(8,128)} %sea_hbm.1) | copy-start | bytes 49156
  3.9 0.7 %copy-start.4 = (s32[32,128]{1,0:T(8,128)S(1)}, s32[32,128]{1,0:T(8,128)}, u32[]{:S(2)}) copy-start(s32[32,128]{1,0:T(8,128)} %depth_hbm.1) | copy-start | bytes 49156
  6.3 10.8 %all-to-all-start = ((f32[8,40,128]{2,1,0:T(8,128)}), f32[8,40,128]{2,1,0:T(8,128)S(1)}, u32[]{:S(2)}, u32[]{:S(2)}) async-start(f32[8,40,128]{2,1,0:T(8,128)} %get-tuple-element.24), calls=%async_computation | async-start | bytes 327680 | tf_op jit(solution)/shard_map/all_to_all | solution.py:585
  10.6 2.2 %copy-start.5 = (f32[64,9]{0,1:T(8,128)S(1)}, f32[64,9]{0,1:T(8,128)}, u32[]{:S(2)}) copy-start(f32[64,9]{0,1:T(8,128)} %param.11) | copy-start | bytes 6916
  10.7 3.7 %collective-permute-start = (f32[8,128]{1,0:T(8,128)S(1)}, f32[8,128]{1,0:T(8,128)S(1)}, u32[]{:S(2)}, u32[]{:S(2)}) collective-permute-start(f32[8,128]{1,0:T(8,128)S(1)} %get-tuple-element.26), channel_id=1, source_target_pairs={{0,1},{1,2},{2,3},{3,4},{4,5},{5,6},{6,7},{7,8},{8,9},{9,10},{10,1... | collective-permute-start | bytes 12296 | tf_op jit(solution)/shard_map/ppermute | solution.py:589
  12.7 3.6 %collective-permute-start.1 = (f32[8,128]{1,0:T(8,128)S(1)}, f32[8,128]{1,0:T(8,128)S(1)}, u32[]{:S(2)}, u32[]{:S(2)}) collective-permute-start(f32[8,128]{1,0:T(8,128)S(1)} %get-tuple-element.27), channel_id=1, source_target_pairs={{1,0},{2,1},{3,2},{4,3},{5,4},{6,5},{7,6},{8,7},{9,8},{10,9},{11,1... | collective-permute-start | bytes 12296 | tf_op jit(solution)/shard_map/ppermute | solution.py:590
  12.8 0.7 %copy-start.6 = (f32[64]{0:T(128)S(1)}, f32[64]{0:T(128)}, u32[]{:S(2)}) copy-start(f32[64]{0:T(128)} %param.12) | copy-start | bytes 772

commit v3 on v2

v3 whole, which is shorter than its diff:
```python
import math

import jax
import jax.numpy as jnp
from jax import lax
from jax.experimental import pallas as pl
from jax.experimental.pallas import tpu as pltpu
from jax.sharding import PartitionSpec as P

F32 = jnp.float32
BF16 = jnp.bfloat16
DIFFUSE = 2048.0
FEAT = 8
HID = 64
NX = 32
NY = 128
ROWS = 8
RIM = 64


def iota(shape, dim):
    return lax.broadcasted_iota(jnp.int32, shape, dim)


def rows8():
    return iota((ROWS, NY), 0)


def lanes8():
    return iota((ROWS, NY), 1)


def wide(row):
    return jnp.broadcast_to(row, (ROWS, NY))


def by_level(first, second):
    return jnp.where((rows8() & 1) == 0, wide(first), wide(second))


def line(ref, x):
    return ref[pl.ds(x, ROWS, stride=NX), :]


def wet_line(sea_ref, depth_ref, x):
    sea = wide(sea_ref[x : x + 1, :])
    depth = wide(depth_ref[x : x + 1, :])
    return jnp.where(((rows8() & 1) < depth) & (sea > 0), 1.0, 0.0).astype(F32)


def rates8():
    return jnp.where(rows8() < 4, DIFFUSE, 0.5).astype(F32)


def split(values):
    high = values.astype(BF16)
    return high, (values - high.astype(F32)).astype(BF16)


def load_kernel(
    state_hbm,
    diff_hbm,
    sea_hbm,
    depth_hbm,
    cot_hbm,
    fields_ref,
    first_ref,
    last_ref,
    diff_ref,
    sea_ref,
    depth_ref,
    cot_ref,
    state_ref,
    sems,
):
    copies = [
        pltpu.make_async_copy(source, target, sems.at[n])
        for n, (source, target) in enumerate(
            (
                (state_hbm, state_ref),
                (sea_hbm, sea_ref),
                (depth_hbm, depth_ref),
                (diff_hbm, diff_ref),
                (cot_hbm, cot_ref),
            )
        )
    ]
    for copy in copies:
        copy.start()
    copies[0].wait()
    lanes = lanes8()
    first = jnp.zeros((ROWS, NY), F32)
    last = jnp.zeros((ROWS, NY), F32)
    for x in range(NX):
        here = line(state_ref, x)
        fields_ref[x] = here
        first = jnp.where(lanes == x, pltpu.roll(here, x, 1) if x else here, first)
        last = jnp.where(lanes == x, pltpu.roll(here, x + 1, 1), last)
    first_ref[...] = first
    last_ref[...] = last
    for copy in copies[1:]:
        copy.wait()


def factor_kernel(
    fields_ref,
    diff_ref,
    sea_ref,
    depth_ref,
    cot_ref,
    send_ref,
    right_ref,
    recip_ref,
    left_ref,
    wets_ref,
):
    me = lax.axis_index("gx")
    count = send_ref.shape[0]
    row = rows8()
    wet = [wet_line(sea_ref, depth_ref, x) for x in range(NX)]
    for x in range(NX):
        wets_ref[x] = wet[x]
    rates = rates8()
    bare = [
        by_level(diff_ref[x : x + 1, :], diff_ref[NX + x : NX + x + 1, :]) * wet[x]
        for x in range(NX)
    ]
    cond = [rates * bare[x] * wet[x + 1] for x in range(NX - 1)]
    mass = jnp.ones((ROWS, NY), F32)
    carry = jnp.ones((ROWS, NY), F32)
    mass_back = jnp.ones((ROWS, NY), F32)
    cots = [line(cot_ref, x) for x in range(NX)]
    load = cots[0]
    load_back = cots[NX - 1]
    for i in range(NX - 1):
        recip = 1.0 / (mass + cond[i])
        ratio = cond[i] * recip
        right_ref[i] = ratio
        recip_ref[i] = recip
        mass = 1.0 + mass * ratio
        load = cots[i + 1] + ratio * load
        carry = carry * ratio
        j = NX - 2 - i
        ratio_back = cond[j] / (mass_back + cond[j])
        left_ref[j] = ratio_back
        mass_back = 1.0 + mass_back * ratio_back
        load_back = cots[j] + ratio_back * load_back
    last_self = 1.0 / mass
    first_self = 1.0 / mass_back
    right_ref[NX - 1] = jnp.zeros((ROWS, NY), F32)
    left_ref[NX - 1] = jnp.zeros((ROWS, NY), F32)
    recip_ref[NX - 1] = last_self
    across = carry * last_self
    upper = (row & 2) == 0
    tiles = [
        load_back * first_self,
        load * last_self,
        jnp.where(upper, first_self, across),
        jnp.where(upper, last_self, jnp.where(row < 4, bare[NX - 1], wet[0])),
    ]
    own_last = fields_ref[NX - 1]
    own_first = fields_ref[0]
    for j in range(count):
        for n, tile in enumerate(tiles):
            send_ref[j, ROWS * n : ROWS * (n + 1), :] = tile
        send_ref[j, ROWS * 4 :, :] = jnp.where(j > me, own_last, own_first)


def reduced(got_ref):
    count = got_ref.shape[0]
    upper = (rows8() & 2) == 0
    first_self, across, last_self, bare, wet = [], [], [], [], []
    for j in range(count):
        tile = got_ref[j, 16:24, :]
        first_self.append(jnp.where(upper, tile, pltpu.roll(tile, 2, 0)))
        across.append(jnp.where(upper, pltpu.roll(tile, 6, 0), tile))
        tile = got_ref[j, 24:32, :]
        last_self.append(jnp.where(upper, tile, pltpu.roll(tile, 2, 0)))
        bare.append(by_level(got_ref[j, 26:27, :], got_ref[j, 27:28, :]))
        wet.append(by_level(got_ref[j, 30:31, :], got_ref[j, 31:32, :]))
    face = [rates8() * bare[j] * wet[j + 1] for j in range(count - 1)]
    return first_self, across, last_self, face


def end_fluxes(system, first, last, me):
    first_self, across, last_self, face = system
    count = len(first_self)
    zero = jnp.zeros((ROWS, NY), F32)
    give, value = last_self[0], last[0]
    gives, values, links = [give], [value], [zero]
    for j in range(1, count):
        link = face[j - 1] / (1.0 + face[j - 1] * (give + first_self[j]))
        pull = across[j] * link
        value = last[j] + pull * (value - first[j])
        give = last_self[j] - pull * across[j]
        gives.append(give)
        values.append(value)
        links.append(link)
    back_give, back_value = first_self[count - 1], first[count - 1]
    right_flux = [None] * count
    right_flux[count - 1] = zero
    for j in range(count - 2, -1, -1):
        right_flux[j] = (
            face[j] * (back_value - values[j]) / (1.0 + face[j] * (back_give + gives[j]))
        )
        link = face[j] / (1.0 + face[j] * (back_give + last_self[j]))
        pull = across[j] * link
        back_value = first[j] + pull * (back_value - last[j])
        back_give = first_self[j] - pull * across[j]
    left, right = zero, right_flux[0]
    for j in range(1, count):
        here = links[j] * (values[j - 1] - first[j] - across[j] * right_flux[j])
        left = jnp.where(me == j, here, left)
        right = jnp.where(me == j, right_flux[j], right)
    return left, right


def own_lines(read, right_ref, recip_ref, fluxes, write):
    left, right = fluxes
    load = read(0) + left
    loads = [load]
    for i in range(1, NX):
        load = read(i) + right_ref[i - 1] * load
        loads.append(load)
    value = (loads[NX - 1] + right) * recip_ref[NX - 1]
    write(NX - 1, value)
    for i in range(NX - 2, -1, -1):
        value = right_ref[i] * value + recip_ref[i] * loads[i]
        write(i, value)


def network_kernel(weights_ref, out_ref, forward_ref, back_ref, outw_ref):
    weights = weights_ref[...]
    per_level = []
    for level in range(2):
        spread = iota((16, FEAT + 1), 0) == 2 * iota((16, FEAT + 1), 1) + level
        per_level.append(
            jnp.dot(
                spread.astype(F32),
                weights,
                precision=lax.Precision.HIGHEST,
                preferred_element_type=F32,
            )
        )
    both = jnp.concatenate(per_level, 1)
    high = both.astype(BF16).astype(F32)
    low = both - high
    bias = weights[FEAT : FEAT + 1, :]
    bias = jnp.broadcast_to(jnp.concatenate([bias, bias], 1), (16, 2 * HID))
    bias_high = bias.astype(BF16).astype(F32)
    bias_mid = (bias - bias_high).astype(BF16).astype(F32)
    bias_low = bias - bias_high - bias_mid
    row = iota((16, 2 * HID), 0)
    bias = jnp.where(
        row == 0, bias_high, jnp.where(row == 1, bias_mid, jnp.where(row == 2, bias_low, 0.0))
    )
    stack = jnp.concatenate([high, high, bias, low, low, jnp.zeros((48, 2 * HID), F32)], 0)
    forward_ref[...] = jnp.transpose(stack).astype(BF16)
    turned = jnp.concatenate([high, low], 0)
    back_ref[...] = jnp.concatenate([turned, turned], 1).astype(BF16)
    out = out_ref[...]
    out = jnp.broadcast_to(jnp.concatenate([out, out], 1), (2 * HID, 2 * HID))
    outw_ref[...] = jnp.transpose(out)


def pack(features, bias, out):
    blank = jnp.zeros((ROWS, HID), F32)
    row = iota((ROWS, 32), 0)
    ends = [
        jnp.broadcast_to(v, (ROWS, 32))
        for v in (bias[:, 0:32], bias[:, 32:64], out[:, 0:32], out[:, 32:64])
    ]
    tail = jnp.zeros((ROWS, 32), F32)
    for n, end in enumerate(ends):
        tail = jnp.where(row == n, end, tail)
    return jnp.concatenate([features, blank[:, :32], tail], 1)


def adjoint_kernel(got_ref, cot_ref, wets_ref, right_ref, recip_ref, adj_ref):
    me = lax.axis_index("gx")
    count = got_ref.shape[0]
    system = reduced(got_ref)
    first = [got_ref[j, 0:8, :] for j in range(count)]
    last = [got_ref[j, 8:16, :] for j in range(count)]
    fluxes = end_fluxes(system, first, last, me)

    def keep(x, value):
        adj_ref[x] = wets_ref[x] * value

    own_lines(lambda x: line(cot_ref, x), right_ref, recip_ref, fluxes, keep)


def stencil_kernel(
    got_ref, low_ref, high_ref, lines_ref, slope_x, slope_y, curve_x, curve_y, feats
):
    me = lax.axis_index("gx")
    here_y = lax.axis_index("gy")
    count = got_ref.shape[0]
    lanes = lanes8()
    zero = jnp.zeros((ROWS, NY), F32)
    below = got_ref[jnp.maximum(me - 1, 0), 32:40, :]
    above = got_ref[jnp.minimum(me + 1, count - 1), 32:40, :]
    below = jnp.where(me > 0, below, zero)
    above = jnp.where(me < count - 1, above, zero)
    low = jnp.where(here_y > 0, low_ref[...], zero)
    high = jnp.where(here_y < lax.axis_size("gy") - 1, high_ref[...], zero)
    feats[32:48, :] = jnp.ones((16, NX * NY), BF16)
    for x in range(NX):
        center = lines_ref[x]
        east = lines_ref[x + 1] if x < NX - 1 else above
        west = lines_ref[x - 1] if x else below
        south = jnp.where(
            lanes == 0, pltpu.roll(low, (-x) % NY, 1) if x else low, pltpu.roll(center, 1, 1)
        )
        north = jnp.where(
            lanes == NY - 1, pltpu.roll(high, NY - 1 - x, 1), pltpu.roll(center, NY - 1, 1)
        )
        sx = 0.5 * (east - west)
        sy = 0.5 * (north - south)
        slope_x[x] = sx
        slope_y[x] = sy
        curve_x[x] = east - 2.0 * center + west
        curve_y[x] = north - 2.0 * center + south
        part_high, part_low = split(jnp.concatenate([sx, sy], 0))
        place = slice(x * NY, (x + 1) * NY)
        feats[0:16, place] = part_high
        feats[16:32, place] = part_low
        feats[48:64, place] = part_high
        feats[64:80, place] = part_low


def closure_kernel(
    got_ref,
    lines_ref,
    wets,
    adj,
    slope_x,
    slope_y,
    curve_x,
    curve_y,
    feats,
    forward_ref,
    back_ref,
    outw_ref,
    right_ref,
    recip_ref,
    left_ref,
    send_ref,
    rhs_ref,
    grad_ref,
    rims_ref,
):
    me = lax.axis_index("gx")
    count = got_ref.shape[0]
    here_y = lax.axis_index("gy")
    total_y = NY * lax.axis_size("gy")
    lanes = lanes8()
    row = rows8()
    places = (here_y * NY + lanes).astype(F32)
    turn = 0.3 * (0.5 + 0.5 * places / total_y)
    moment = row < 4
    outw = outw_ref[...]
    hidden = jnp.tanh(jnp.dot(forward_ref[:, 0:80], feats[...], preferred_element_type=F32))
    sharp, keepers = [], []
    out_sums = jnp.zeros((2 * HID, NY), F32)
    for x in range(NX):
        unit = hidden[:, x * NY : (x + 1) * NY]
        weighed = unit * outw
        mixed = by_level(
            jnp.sum(weighed[:HID], 0, keepdims=True), jnp.sum(weighed[HID:], 0, keepdims=True)
        )
        gate = 1.0 / (1.0 + jnp.exp(-mixed))
        nu = jnp.where(moment, 0.24 * gate, 0.0)
        center = lines_ref[x]
        sx, sy, cx, cy = slope_x[x], slope_y[x], curve_x[x], curve_y[x]
        u = by_level(center[0:1], center[1:2])
        v = by_level(center[2:3], center[3:4])
        speed_u = jnp.sqrt(u * u + 0.01)
        speed_v = jnp.sqrt(v * v + 0.01)
        upwind = u * sx + v * sy - 0.5 * (speed_u * cx + speed_v * cy)
        twist = jnp.where(
            row < 2, pltpu.roll(center, 6, 0), jnp.where(moment, -pltpu.roll(center, 2, 0), 0.0)
        )
        rhs_ref[x] = wets[x] * (center - 0.3 * upwind + nu * (cx + cy) + turn * twist)
        g = adj[x]
        to_gate = jnp.where(moment, g * (cx + cy) * (0.24 * gate * (1.0 - gate)), 0.0)
        to_gate = to_gate + pltpu.roll(to_gate, 6, 0)
        gate_level = jnp.concatenate(
            [jnp.broadcast_to(to_gate[0:1], (HID, NY)), jnp.broadcast_to(to_gate[1:2], (HID, NY))],
            0,
        )
        out_sums = out_sums + unit * gate_level
        sharp.append((1.0 - unit * unit) * (outw * gate_level))
        along_u = g * (-0.3 * sx + 0.15 * (u / speed_u) * cx)
        along_v = g * (-0.3 * sy + 0.15 * (v / speed_v) * cy)
        along_u = along_u + pltpu.roll(along_u, 4, 0)
        along_u = along_u + pltpu.roll(along_u, 2, 0)
        along_v = along_v + pltpu.roll(along_v, 4, 0)
        along_v = along_v + pltpu.roll(along_v, 2, 0)
        untwist = jnp.where(
            row < 2, along_u - turn * pltpu.roll(g, 6, 0), along_v + turn * pltpu.roll(g, 2, 0)
        )
        bend_x = g * (0.15 * speed_u + nu)
        bend_y = g * (0.15 * speed_v + nu)
        middle = g + jnp.where(moment, untwist, 0.0) - 2.0 * (bend_x + bend_y)
        keepers.append((-0.3 * u * g, -0.3 * v * g, bend_x, bend_y, middle))
    stacked = jnp.concatenate(split(jnp.concatenate(sharp, 1)), 0)
    to_feats = jnp.dot(back_ref[...], stacked, preferred_element_type=F32)
    to_feats = to_feats[0:16] + to_feats[16:32]
    sums = lax.dot_general(
        stacked, feats[0:48, :], (((1,), (1,)), ((), ())), preferred_element_type=F32
    )

    load = rhs_ref[0]
    load_back = rhs_ref[NX - 1]
    for i in range(NX - 1):
        load = rhs_ref[i + 1] + right_ref[i] * load
        j = NX - 2 - i
        load_back = rhs_ref[j] + left_ref[j] * load_back
    first_own = load_back * jnp.where(
        (row & 2) == 0, got_ref[me, 16:24, :], pltpu.roll(got_ref[me, 16:24, :], 2, 0)
    )
    last_own = load * recip_ref[NX - 1]

    rim_north = jnp.zeros((ROWS, NY), F32)
    rim_south = jnp.zeros((ROWS, NY), F32)
    to_east, to_west, kept = [], [], []
    for x in range(NX):
        to_sx, to_sy, bend_x, bend_y, middle = keepers[x]
        mine = to_feats[:, x * NY : (x + 1) * NY]
        half_x = 0.5 * (to_sx + mine[0:8])
        half_y = 0.5 * (to_sy + mine[8:16])
        to_north = bend_y + half_y
        to_south = bend_y - half_y
        rim_north = jnp.where(lanes == RIM + x, pltpu.roll(to_north, RIM + x + 1, 1), rim_north)
        rim_south = jnp.where(lanes == RIM + x, pltpu.roll(to_south, RIM + x, 1), rim_south)
        to_east.append(bend_x + half_x)
        to_west.append(bend_x - half_x)
        kept.append(
            middle
            + jnp.where(lanes == 0, 0.0, pltpu.roll(to_north, 1, 1))
            + jnp.where(lanes == NY - 1, 0.0, pltpu.roll(to_south, NY - 1, 1))
        )
    for x in range(NX):
        total = kept[x]
        if x:
            total = total + to_east[x - 1]
        if x < NX - 1:
            total = total + to_west[x + 1]
        grad_ref[x] = total
    rims_ref[0] = rim_north
    rims_ref[1] = rim_south
    to_last = to_east[NX - 1]
    to_first = to_west[0]

    sums = sums[0:128] + sums[128:256]
    total = jnp.zeros((16, HID), F32)
    for level in range(2):
        source = iota((16, 48), 1)
        target = iota((16, 48), 0)
        feature = (source < 32) & ((source & 15) == 2 * target + level) & (target < FEAT)
        gather = feature | ((source == 32) & (target == FEAT))
        total += lax.dot_general(
            gather.astype(F32),
            sums[level * HID : (level + 1) * HID],
            (((1,), (1,)), ((), ())),
            precision=lax.Precision.HIGHEST,
            preferred_element_type=F32,
        )
    out_total = lax.dot_general(
        jnp.ones((8, 128), F32),
        out_sums[0:HID] + out_sums[HID:],
        (((1,), (1,)), ((), ())),
        precision=lax.Precision.HIGHEST,
        preferred_element_type=F32,
    )
    packed = pack(total[0:8], total[8:9], out_total[0:1])
    for j in range(count):
        send_ref[j, 0:8, :] = first_own
        send_ref[j, 8:16, :] = last_own
        send_ref[j, 16:24, :] = packed
        send_ref[j, 24:32, :] = jnp.where(j > me, to_last, to_first)


def share_kernel(
    second_ref, rims_ref, got_ref, rhs_ref, right_ref, recip_ref, send_ref, final_ref
):
    me_y = lax.axis_index("gy")
    me = lax.axis_index("gx")
    count = got_ref.shape[0]
    lanes = lanes8()
    total = second_ref[0, 16:24, :]
    for j in range(1, count):
        total = total + second_ref[j, 16:24, :]
    rim = (lanes >= RIM) & (lanes < RIM + NX)
    upward = jnp.where(rim, rims_ref[0], total)
    downward = jnp.where(rim, rims_ref[1], total)
    for j in range(send_ref.shape[0]):
        send_ref[j] = jnp.where(j > me_y, upward, downward)
    system = reduced(got_ref)
    first = [second_ref[j, 0:8, :] for j in range(count)]
    last = [second_ref[j, 8:16, :] for j in range(count)]
    fluxes = end_fluxes(system, first, last, me)

    def keep(x, value):
        final_ref[pl.ds(x, ROWS, stride=NX), :] = value

    own_lines(lambda x: rhs_ref[x], right_ref, recip_ref, fluxes, keep)


def finish_kernel(
    factor,
    third_ref,
    second_ref,
    grad_ref,
    final_ref,
    final_hbm,
    out_hbm,
    closure_hbm,
    closure_ref,
    out_ref,
    sems,
):
    copies = [pltpu.make_async_copy(final_ref, final_hbm, sems.at[0])]
    copies[0].start()
    me_x = lax.axis_index("gx")
    me_y = lax.axis_index("gy")
    count_x = second_ref.shape[0]
    count_y = third_ref.shape[0]
    lanes = lanes8()
    zero = jnp.zeros((ROWS, NY), F32)
    parts = [third_ref[j] for j in range(count_y)]
    while len(parts) > 1:
        parts = [a + b for a, b in zip(parts[::2], parts[1::2])]
    total = parts[0] * factor
    closure_ref[0:8, :] = total[:, 0:HID]
    for n in range(2):
        closure_ref[8 + n : 9 + n, :] = jnp.concatenate(
            [total[2 * n : 2 * n + 1, 96:], total[2 * n + 1 : 2 * n + 2, 96:]], 1
        )
    copies.append(pltpu.make_async_copy(closure_ref, closure_hbm, sems.at[1]))
    copies[1].start()
    before = jnp.where(me_x > 0, second_ref[jnp.maximum(me_x - 1, 0), 24:32, :], zero)
    after = jnp.where(
        me_x < count_x - 1, second_ref[jnp.minimum(me_x + 1, count_x - 1), 24:32, :], zero
    )
    south = jnp.where(me_y > 0, third_ref[jnp.maximum(me_y - 1, 0)], zero)
    north = jnp.where(me_y < count_y - 1, third_ref[jnp.minimum(me_y + 1, count_y - 1)], zero)
    for x in range(NX):
        value = grad_ref[x]
        if x == 0:
            value = value + before
        if x == NX - 1:
            value = value + after
        value = value + jnp.where(lanes == 0, pltpu.roll(south, NY - RIM - x, 1), 0.0)
        value = value + jnp.where(lanes == NY - 1, pltpu.roll(north, NY - 1 - RIM - x, 1), 0.0)
        out_ref[pl.ds(x, ROWS, stride=NX), :] = value
    copies.append(pltpu.make_async_copy(out_ref, out_hbm, sems.at[2]))
    copies[2].start()
    for copy in copies:
        copy.wait()


def tile(*shape):
    return jax.ShapeDtypeStruct(shape, F32)


def keep_in_hbm(values):
    return pltpu.with_memory_space_constraint(values, pltpu.HBM)


def params():
    return pltpu.CompilerParams(vmem_limit_bytes=40 * 1024 * 1024)


def per_device(state, diffusivity, sea_mask, depth_index, closure_in, closure_out, cotangent):
    count_x = lax.axis_size("gx")
    count_y = lax.axis_size("gy")
    lines = tile(NX, ROWS, NY)
    in_hbm = pl.BlockSpec(memory_space=pltpu.HBM)
    in_vmem = pl.BlockSpec(memory_space=pltpu.VMEM)
    ints = jax.ShapeDtypeStruct((NX, NY), jnp.int32)
    fields, first, last, diff, sea, depth, cot = pl.pallas_call(
        load_kernel,
        in_specs=[in_hbm] * 5,
        out_shape=(
            lines,
            tile(ROWS, NY),
            tile(ROWS, NY),
            tile(2 * NX, NY),
            ints,
            ints,
            tile(ROWS * NX, NY),
        ),
        scratch_shapes=[pltpu.VMEM((ROWS * NX, NY), F32), pltpu.SemaphoreType.DMA((5,))],
        compiler_params=params(),
    )(
        keep_in_hbm(state.reshape(ROWS * NX, NY)),
        keep_in_hbm(diffusivity.reshape(2 * NX, NY)),
        keep_in_hbm(sea_mask),
        keep_in_hbm(depth_index),
        keep_in_hbm(cotangent.reshape(ROWS * NX, NY)),
    )
    send, right, recip, left, wets = pl.pallas_call(
        factor_kernel,
        out_shape=(tile(count_x, 40, NY),) + (lines,) * 4,
        compiler_params=params(),
    )(fields, diff, sea, depth, cot)
    got = lax.all_to_all(send, "gx", 0, 0, tiled=True)
    low = lax.ppermute(last, "gy", [(i, (i + 1) % count_y) for i in range(count_y)])
    high = lax.ppermute(first, "gy", [((i + 1) % count_y, i) for i in range(count_y)])
    forward, back, outw = pl.pallas_call(
        network_kernel,
        out_shape=(
            jax.ShapeDtypeStruct((2 * HID, 128), BF16),
            jax.ShapeDtypeStruct((32, 256), BF16),
            tile(2 * HID, 128),
        ),
        compiler_params=params(),
    )(closure_in.T, closure_out.reshape(1, HID))
    adj = pl.pallas_call(adjoint_kernel, out_shape=lines, compiler_params=params())(
        got, cot, wets, right, recip
    )
    feats_shape = jax.ShapeDtypeStruct((80, NX * NY), BF16)
    stencil = pl.pallas_call(
        stencil_kernel, out_shape=(lines,) * 4 + (feats_shape,), compiler_params=params()
    )(got, low, high, fields)
    send, rhs, grad, rims = pl.pallas_call(
        closure_kernel,
        out_shape=(tile(count_x, 32, NY), lines, lines, tile(2, ROWS, NY)),
        compiler_params=params(),
    )(got, fields, wets, adj, *stencil, forward, back, outw, right, recip, left)
    second = lax.all_to_all(send, "gx", 0, 0, tiled=True)
    send, final = pl.pallas_call(
        share_kernel,
        out_shape=(tile(count_y, ROWS, NY), tile(ROWS * NX, NY)),
        compiler_params=params(),
    )(second, rims, got, rhs, right, recip)
    third = lax.all_to_all(send, "gy", 0, 0, tiled=True)
    factor = 1.0 / math.sqrt(2 * NX * count_x * NY * count_y)

    def finish(*refs):
        finish_kernel(factor, *refs)

    final, state_grad, closure_grad = pl.pallas_call(
        finish,
        in_specs=[in_vmem] * 4,
        out_shape=(tile(ROWS * NX, NY), tile(ROWS * NX, NY), tile(10, HID)),
        out_specs=(in_hbm,) * 3,
        scratch_shapes=[
            pltpu.VMEM((10, HID), F32),
            pltpu.VMEM((ROWS * NX, NY), F32),
            pltpu.SemaphoreType.DMA((3,)),
        ],
        compiler_params=params(),
    )(third, second, grad, final)
    return (final.reshape(state.shape), state_grad.reshape(state.shape), closure_grad.T)


def solution(mesh):
    return jax.shard_map(
        per_device,
        mesh=mesh,
        in_specs=(
            P(None, None, "gx", "gy"),
            P(None, "gx", "gy"),
            P("gx", "gy"),
            P("gx", "gy"),
            P(),
            P(),
            P(None, None, "gx", "gy"),
        ),
        out_specs=(P(None, None, "gx", "gy"), P(None, None, "gx", "gy"), P()),
        check_vma=False,
    )
```

time: 55.8 us -> 48.8 us (0.87)
  local copies, waits for them, and re-layouts: 4.65 us -> 0.66 us
  Pallas kernels: 9.46 us -> 6.76 us
    unnamed x14 -> x4, local copies, waits for them, and re-layouts: 4.65 us -> 0.66 us
    pallas_call x3 -> x5, Pallas kernels: 7.46 us -> 5.33 us  [the longest x1 2.74 us: per_device(): pl.pallas_call(closure_kernel, out_shape=(tile(count_x, 32, NY), lines, l...]
    pallas_call x1, Pallas kernels: 1.44 us -> 0.86 us  [per_device(): pl.pallas_call(finish, in_specs=[in_vmem] * 4, out_shape=(tile(ROWS * NX,...]
where the time goes in v3:
time: 48.8 us; the launch traced here: 48.5 us
  blocking collectives  30.5 us (63%)
  Pallas kernels  6.76 us (14%)
  starting transfers between devices  6.46 us (13%)
  waiting for transfers between devices  3.49 us (7%)
  between operations  0.67 us (1%)
  local copies, waits for them, and re-layouts  0.66 us (1%)
    all_to_all x1, blocking collectives, per_device(): third = lax.all_to_all(send, 'gy', 0, 0, tiled=True)  20.7 us
    all_to_all x1, blocking collectives, per_device(): second = lax.all_to_all(send, 'gx', 0, 0, tiled=True)  9.78 us
    all_to_all x1, starting transfers between devices, per_device(): got = lax.all_to_all(send, 'gx', 0, 0, tiled=True)  4.43 us
    pallas_call x1, Pallas kernels, per_device(): pl.pallas_call(closure_kernel, out_shape=(tile(count_x, 32, NY), lines, l...  2.74 us
    ppermute x1, starting transfers between devices, per_device(): lax.ppermute(last, 'gy', [(i, (i + 1) % count_y) for i in range(count_y)])  1.92 us
    ppermute x1, waiting for transfers between devices, per_device(): lax.ppermute(first, 'gy', [((i + 1) % count_y, i) for i in range(count_y)])  1.92 us
    pallas_call x1, Pallas kernels, per_device(): pl.pallas_call(load_kernel, in_specs=[in_hbm] * 5, out_shape=(lines, tile...  1.11 us
    pallas_call x1, Pallas kernels, per_device(): pl.pallas_call(factor_kernel, out_shape=(tile(count_x, 40, NY),) + (lines...  1.04 us
  transfers between devices with their start and end apart: 3, of which 3 were waited for; matrix products, arithmetic and copies ran while one was open for 0% of the time, Pallas kernels for 1%

profile of v3, /device:TPU:32, one launch (start us, length us, event | category | flops | bytes accessed | tf_op | source)
XLA Modules:
  0.0 48.5 jit_solution(3185382957116791386)
XLA Ops:
  0.6 1.1 %shard_map.94 = (f32[32,8,128]{2,1,0:T(8,128)S(1)}, f32[8,128]{1,0:T(8,128)S(1)}, f32[8,128]{1,0:T(8,128)S(1)}, f32[64,128]{1,0:T(8,128)S(1)}, s32[32,128]{1,0:T...) custom-call(f32[256,128]{1,0:T(8,128)} %bitcast.10, f32[64,128]{1,0:T(8,128)} %bitcast.12, s32[32,128]{1,0:T(8,128)} %sea_hbm.1, ...), custom_call_target="tpu_custom_call" | custom-call | tf_op jit(solution)/shard_map/pallas_call | solution.py:583
  1.7 1.0 %shard_map.95 = (f32[8,40,128]{2,1,0:T(8,128)}, f32[32,8,128]{2,1,0:T(8,128)S(1)}, f32[32,8,128]{2,1,0:T(8,128)S(1)}, f32[32,8,128]{2,1,0:T(8,128)S(1)}, f32[32,8,128]{2,1,0:T(8,128)S(1)}) custom-call(f32[32,8,128]{2,1,0:T(8,128)S(1)} %get-tuple-element.32.fields_ref.lines_ref, f32[64,128]{1,0:T(8,128)S(1)} %get-tuple-element.33.diff_ref, ...), custom_call_target="tpu_custom_call" | custom-call | tf_op jit(solution)/shard_map/pallas_call | solution.py:604
  2.8 0.0 copy-start
  2.8 4.4 %all-to-all-start = ((f32[8,40,128]{2,1,0:T(8,128)}), f32[8,40,128]{2,1,0:T(8,128)S(1)}, u32[]{:S(2)}, u32[]{:S(2)}) async-start(f32[8,40,128]{2,1,0:T(8,128)} %get-tuple-element.37), calls=%async_computation | async-start | bytes 327680 | tf_op jit(solution)/shard_map/all_to_all | solution.py:609
  7.2 1.9 %collective-permute-start = (f32[8,128]{1,0:T(8,128)S(1)}, f32[8,128]{1,0:T(8,128)S(1)}, u32[]{:S(2)}, u32[]{:S(2)}) collective-permute-start(f32[8,128]{1,0:T(8,128)S(1)} %get-tuple-element.41), channel_id=1, source_target_pairs={{0,1},{1,2},{2,3},{3,4},{4,5},{5,6},{6,7},{7,8},{8,9},{9,10},{10,1... | collective-permute-start | bytes 12296 | tf_op jit(solution)/shard_map/ppermute | solution.py:610
  9.1 0.1 collective-permute-start.1
  9.2 0.0 copy-start.1
  9.2 0.0 copy-done
  9.3 0.7 %copy-done.1 = f32[64]{0:T(128)S(1)} copy-done((f32[64]{0:T(128)S(1)}, f32[64]{0:T(128)}, u32[]{:S(2)}) %copy-start.1) | copy-done | bytes 280
  9.9 0.3 shard_map.98
  10.2 0.6 %collective-permute-done.low_ref = f32[8,128]{1,0:T(8,128)S(1)} collective-permute-done((f32[8,128]{1,0:T(8,128)S(1)}, f32[8,128]{1,0:T(8,128)S(1)}, u32[]{:S(2)}, u32[]{:S(2)}) %collective-permute-start) | collective-permute-done | bytes 4128 | tf_op jit(solution)/shard_map/ppermute | solution.py:610
  10.8 1.9 %collective-permute-done.1.high_ref = f32[8,128]{1,0:T(8,128)S(1)} collective-permute-done((f32[8,128]{1,0:T(8,128)S(1)}, f32[8,128]{1,0:T(8,128)S(1)}, u32[]{:S(2)}, u32[]{:S(2)}) %collective-permute-start.1) | collective-permute-done | bytes 4128 | tf_op jit(solution)/shard_map/ppermute | solution.py:611
  12.7 1.0 %all-to-all-done.got_ref = f32[8,40,128]{2,1,0:T(8,128)S(1)} async-done(((f32[8,40,128]{2,1,0:T(8,128)}), f32[8,40,128]{2,1,0:T(8,128)S(1)}, u32[]{:S(2)}, u32[]{:S(2)}) %all-to-all-start) | async-done | bytes 163872 | tf_op jit(solution)/shard_map/all_to_all | solution.py:609
  13.7 0.2 shard_map.97
  13.9 0.2 shard_map.96.adj
  14.2 2.7 %shard_map.99 = (f32[8,32,128]{2,1,0:T(8,128)S(1)}, f32[32,8,128]{2,1,0:T(8,128)S(1)}, f32[32,8,128]{2,1,0:T(8,128)S(1)}, f32[2,8,128]{2,1,0:T(8,128)S(1)}) custom-call(f32[8,40,128]{2,1,0:T(8,128)S(1)} %all-to-all-done.got_ref, f32[32,8,128]{2,1,0:T(8,128)S(1)} %get-tuple-element.32.fields_ref.lines_ref, f32[32,8,128]{2,1,0:T(8,128)S(1)} %get-tuple-element.38.wets_ref.wets, ...), custom_call_target="tpu_custom_call" | custom-call | tf_op jit(solution)/shard_map/pallas_call | solution.py:628
  16.9 9.8 %all_to_all.15.second_ref.refs_1_ = f32[8,32,128]{2,1,0:T(8,128)S(1)} all-to-all(f32[8,32,128]{2,1,0:T(8,128)S(1)} %get-tuple-element.52), channel_id=1, replica_groups=mesh['gx'=8,'gy'=32] {'gx'}, dimensions={0} | all-to-all | bytes 262144 | tf_op jit(solution)/shard_map/all_to_all | solution.py:633
  26.7 0.3 shard_map.100
  26.9 20.7 %all_to_all.16.refs_0_ = f32[32,8,128]{2,1,0:T(8,128)S(1)} all-to-all(f32[32,8,128]{2,1,0:T(8,128)S(1)} %get-tuple-element.55), channel_id=1, replica_groups=mesh['gx'=8,'gy'=32] {'gy'}, dimensions={0} | all-to-all | bytes 262144 | tf_op jit(solution)/shard_map/all_to_all | solution.py:639
  47.7 0.9 %shard_map.101 = (f32[256,128]{1,0:T(8,128)}, f32[256,128]{1,0:T(8,128)}, f32[10,64]{1,0:T(8,128)}) custom-call(f32[32,8,128]{2,1,0:T(8,128)S(1)} %all_to_all.16.refs_0_, f32[8,32,128]{2,1,0:T(8,128)S(1)} %all_to_all.15.second_ref.refs_1_, f32[32,8,128]{2,1,0:T(8,128)S(1)} %get-tuple-element.56.refs_2_, f32[256,128]{1,0:T(8,128)S(1)} %get-tuple-element.57.refs_3_), custom_call_target="tpu_custom_call" | custom-call | tf_op jit(solution)/shard_map/pallas_call | solution.py:645
Async XLA Ops:
  2.8 6.5 %copy-start = (f32[64,9]{0,1:T(8,128)S(1)}, f32[64,9]{0,1:T(8,128)}, u32[]{:S(2)}) copy-start(f32[64,9]{0,1:T(8,128)} %param.11) | copy-start | bytes 6916
  2.8 10.9 %all-to-all-start = ((f32[8,40,128]{2,1,0:T(8,128)}), f32[8,40,128]{2,1,0:T(8,128)S(1)}, u32[]{:S(2)}, u32[]{:S(2)}) async-start(f32[8,40,128]{2,1,0:T(8,128)} %get-tuple-element.37), calls=%async_computation | async-start | bytes 327680 | tf_op jit(solution)/shard_map/all_to_all | solution.py:609
  7.2 3.6 %collective-permute-start = (f32[8,128]{1,0:T(8,128)S(1)}, f32[8,128]{1,0:T(8,128)S(1)}, u32[]{:S(2)}, u32[]{:S(2)}) collective-permute-start(f32[8,128]{1,0:T(8,128)S(1)} %get-tuple-element.41), channel_id=1, source_target_pairs={{0,1},{1,2},{2,3},{3,4},{4,5},{5,6},{6,7},{7,8},{8,9},{9,10},{10,1... | collective-permute-start | bytes 12296 | tf_op jit(solution)/shard_map/ppermute | solution.py:610
  9.1 3.6 %collective-permute-start.1 = (f32[8,128]{1,0:T(8,128)S(1)}, f32[8,128]{1,0:T(8,128)S(1)}, u32[]{:S(2)}, u32[]{:S(2)}) collective-permute-start(f32[8,128]{1,0:T(8,128)S(1)} %get-tuple-element.42), channel_id=1, source_target_pairs={{1,0},{2,1},{3,2},{4,3},{5,4},{6,5},{7,6},{8,7},{9,8},{10,9},{11,1... | collective-permute-start | bytes 12296 | tf_op jit(solution)/shard_map/ppermute | solution.py:611
  9.2 0.7 %copy-start.1 = (f32[64]{0:T(128)S(1)}, f32[64]{0:T(128)}, u32[]{:S(2)}) copy-start(f32[64]{0:T(128)} %param.12) | copy-start | bytes 772

commit v4 on v3

--- a/solution.py
+++ b/solution.py
@@ -14,6 +14,7 @@
 HID = 64
 NX = 32
 NY = 128
+XS = 8
 ROWS = 8
 RIM = 64
 
@@ -130,6 +131,7 @@
     carry = jnp.ones((ROWS, NY), F32)
     mass_back = jnp.ones((ROWS, NY), F32)
     cots = [line(cot_ref, x) for x in range(NX)]
+    backs = []
     load = cots[0]
     load_back = cots[NX - 1]
     for i in range(NX - 1):
@@ -142,13 +144,17 @@
         carry = carry * ratio
         j = NX - 2 - i
         ratio_back = cond[j] / (mass_back + cond[j])
-        left_ref[j] = ratio_back
+        backs.append(ratio_back)
         mass_back = 1.0 + mass_back * ratio_back
         load_back = cots[j] + ratio_back * load_back
     last_self = 1.0 / mass
     first_self = 1.0 / mass_back
     right_ref[NX - 1] = jnp.zeros((ROWS, NY), F32)
-    left_ref[NX - 1] = jnp.zeros((ROWS, NY), F32)
+    product = backs[NX - 2]
+    for x in range(1, NX):
+        left_ref[x] = product
+        if x < NX - 1:
+            product = product * backs[NX - 2 - x]
     recip_ref[NX - 1] = last_self
     across = carry * last_self
     upper = (row & 2) == 0
@@ -229,7 +235,7 @@
         write(i, value)
 
 
-def network_kernel(weights_ref, out_ref, forward_ref, back_ref, outw_ref):
+def network_kernel(weights_ref, out_ref, forward_ref, back_ref, outw_ref, outr_ref):
     weights = weights_ref[...]
     per_level = []
     for level in range(2):
@@ -256,11 +262,13 @@
     )
     stack = jnp.concatenate([high, high, bias, low, low, jnp.zeros((48, 2 * HID), F32)], 0)
     forward_ref[...] = jnp.transpose(stack).astype(BF16)
-    turned = jnp.concatenate([high, low], 0)
-    back_ref[...] = jnp.concatenate([turned, turned], 1).astype(BF16)
     out = out_ref[...]
     out = jnp.broadcast_to(jnp.concatenate([out, out], 1), (2 * HID, 2 * HID))
     outw_ref[...] = jnp.transpose(out)
+    outr_ref[...] = out[0:48]
+    scaled = both * out[0:16]
+    turned = jnp.concatenate(split(scaled), 0)
+    back_ref[...] = jnp.concatenate([turned, turned], 1)
 
 
 def pack(features, bias, out):
@@ -276,52 +284,51 @@
     return jnp.concatenate([features, blank[:, :32], tail], 1)
 
 
-def adjoint_kernel(got_ref, cot_ref, wets_ref, right_ref, recip_ref, adj_ref):
+def adjoint_kernel(
+    got_ref, cot_ref, wets_ref, right_ref, recip_ref, lines_ref, adj_ref, slope_x, curve_x
+):
     me = lax.axis_index("gx")
     count = got_ref.shape[0]
-    system = reduced(got_ref)
-    first = [got_ref[j, 0:8, :] for j in range(count)]
-    last = [got_ref[j, 8:16, :] for j in range(count)]
-    fluxes = end_fluxes(system, first, last, me)
-
-    def keep(x, value):
-        adj_ref[x] = wets_ref[x] * value
-
-    own_lines(lambda x: line(cot_ref, x), right_ref, recip_ref, fluxes, keep)
-
-
-def stencil_kernel(
-    got_ref, low_ref, high_ref, lines_ref, slope_x, slope_y, curve_x, curve_y, feats
-):
-    me = lax.axis_index("gx")
-    here_y = lax.axis_index("gy")
-    count = got_ref.shape[0]
-    lanes = lanes8()
     zero = jnp.zeros((ROWS, NY), F32)
     below = got_ref[jnp.maximum(me - 1, 0), 32:40, :]
     above = got_ref[jnp.minimum(me + 1, count - 1), 32:40, :]
     below = jnp.where(me > 0, below, zero)
     above = jnp.where(me < count - 1, above, zero)
+    for x in range(NX):
+        east = lines_ref[x + 1] if x < NX - 1 else above
+        west = lines_ref[x - 1] if x else below
+        slope_x[x] = 0.5 * (east - west)
+        curve_x[x] = east - 2.0 * lines_ref[x] + west
+    system = reduced(got_ref)
+    first = [got_ref[j, 0:8, :] for j in range(count)]
+    last = [got_ref[j, 8:16, :] for j in range(count)]
+    fluxes = end_fluxes(system, first, last, me)
+
+    def keep(x, value):
+        adj_ref[x] = wets_ref[x] * value
+
+    own_lines(lambda x: line(cot_ref, x), right_ref, recip_ref, fluxes, keep)
+
+
+def stencil_kernel(low_ref, high_ref, lines_ref, slope_x, slope_y, curve_y, feats):
+    here_y = lax.axis_index("gy")
+    lanes = lanes8()
+    zero = jnp.zeros((ROWS, NY), F32)
     low = jnp.where(here_y > 0, low_ref[...], zero)
     high = jnp.where(here_y < lax.axis_size("gy") - 1, high_ref[...], zero)
     feats[32:48, :] = jnp.ones((16, NX * NY), BF16)
     for x in range(NX):
         center = lines_ref[x]
-        east = lines_ref[x + 1] if x < NX - 1 else above
-        west = lines_ref[x - 1] if x else below
         south = jnp.where(
             lanes == 0, pltpu.roll(low, (-x) % NY, 1) if x else low, pltpu.roll(center, 1, 1)
         )
         north = jnp.where(
             lanes == NY - 1, pltpu.roll(high, NY - 1 - x, 1), pltpu.roll(center, NY - 1, 1)
         )
-        sx = 0.5 * (east - west)
         sy = 0.5 * (north - south)
-        slope_x[x] = sx
         slope_y[x] = sy
-        curve_x[x] = east - 2.0 * center + west
         curve_y[x] = north - 2.0 * center + south
-        part_high, part_low = split(jnp.concatenate([sx, sy], 0))
+        part_high, part_low = split(jnp.concatenate([slope_x[x], sy], 0))
         place = slice(x * NY, (x + 1) * NY)
         feats[0:16, place] = part_high
         feats[16:32, place] = part_low
@@ -342,6 +349,7 @@
     forward_ref,
     back_ref,
     outw_ref,
+    outr_ref,
     right_ref,
     recip_ref,
     left_ref,
@@ -349,6 +357,7 @@
     rhs_ref,
     grad_ref,
     rims_ref,
+    pairs_ref,
 ):
     me = lax.axis_index("gx")
     count = got_ref.shape[0]
@@ -360,11 +369,17 @@
     turn = 0.3 * (0.5 + 0.5 * places / total_y)
     moment = row < 4
     outw = outw_ref[...]
-    hidden = jnp.tanh(jnp.dot(forward_ref[:, 0:80], feats[...], preferred_element_type=F32))
-    sharp, keepers = [], []
+    sharp, keepers, to_feats = [], [], []
+    sums = jnp.zeros((48, 256), F32)
     out_sums = jnp.zeros((2 * HID, NY), F32)
-    for x in range(NX):
-        unit = hidden[:, x * NY : (x + 1) * NY]
+    load = load_back = jnp.zeros((ROWS, NY), F32)
+    for x in range(NX):
+        if x % XS == 0:
+            place = slice(x * NY, (x + XS) * NY)
+            hidden = jnp.tanh(
+                jnp.dot(forward_ref[:, 0:80], feats[:, place], preferred_element_type=F32)
+            )
+        unit = hidden[:, (x % XS) * NY : (x % XS + 1) * NY]
         weighed = unit * outw
         mixed = by_level(
             jnp.sum(weighed[:HID], 0, keepdims=True), jnp.sum(weighed[HID:], 0, keepdims=True)
@@ -381,7 +396,10 @@
         twist = jnp.where(
             row < 2, pltpu.roll(center, 6, 0), jnp.where(moment, -pltpu.roll(center, 2, 0), 0.0)
         )
-        rhs_ref[x] = wets[x] * (center - 0.3 * upwind + nu * (cx + cy) + turn * twist)
+        explicit = wets[x] * (center - 0.3 * upwind + nu * (cx + cy) + turn * twist)
+        rhs_ref[x] = explicit
+        load = explicit + right_ref[x - 1] * load if x else explicit
+        load_back = load_back + left_ref[x] * explicit if x else explicit
         g = adj[x]
         to_gate = jnp.where(moment, g * (cx + cy) * (0.24 * gate * (1.0 - gate)), 0.0)
         to_gate = to_gate + pltpu.roll(to_gate, 6, 0)
@@ -389,8 +407,9 @@
             [jnp.broadcast_to(to_gate[0:1], (HID, NY)), jnp.broadcast_to(to_gate[1:2], (HID, NY))],
             0,
         )
-        out_sums = out_sums + unit * gate_level
-        sharp.append((1.0 - unit * unit) * (outw * gate_level))
+        pulled = unit * gate_level
+        out_sums = out_sums + pulled
+        sharp.append(gate_level - unit * pulled)
         along_u = g * (-0.3 * sx + 0.15 * (u / speed_u) * cx)
         along_v = g * (-0.3 * sy + 0.15 * (v / speed_v) * cy)
         along_u = along_u + pltpu.roll(along_u, 4, 0)
@@ -404,19 +423,15 @@
         bend_y = g * (0.15 * speed_v + nu)
         middle = g + jnp.where(moment, untwist, 0.0) - 2.0 * (bend_x + bend_y)
         keepers.append((-0.3 * u * g, -0.3 * v * g, bend_x, bend_y, middle))
-    stacked = jnp.concatenate(split(jnp.concatenate(sharp, 1)), 0)
-    to_feats = jnp.dot(back_ref[...], stacked, preferred_element_type=F32)
-    to_feats = to_feats[0:16] + to_feats[16:32]
-    sums = lax.dot_general(
-        stacked, feats[0:48, :], (((1,), (1,)), ((), ())), preferred_element_type=F32
-    )
-
-    load = rhs_ref[0]
-    load_back = rhs_ref[NX - 1]
-    for i in range(NX - 1):
-        load = rhs_ref[i + 1] + right_ref[i] * load
-        j = NX - 2 - i
-        load_back = rhs_ref[j] + left_ref[j] * load_back
+        if x % XS == XS - 1:
+            stacked = jnp.concatenate(split(jnp.concatenate(sharp, 1)), 0)
+            sharp = []
+            back = jnp.dot(back_ref[...], stacked, preferred_element_type=F32)
+            to_feats.append(back[0:16] + back[16:32])
+            sums = sums + lax.dot_general(
+                feats[0:48, place], stacked, (((1,), (1,)), ((), ())), preferred_element_type=F32
+            )
+
     first_own = load_back * jnp.where(
         (row & 2) == 0, got_ref[me, 16:24, :], pltpu.roll(got_ref[me, 16:24, :], 2, 0)
     )
@@ -427,7 +442,7 @@
     to_east, to_west, kept = [], [], []
     for x in range(NX):
         to_sx, to_sy, bend_x, bend_y, middle = keepers[x]
-        mine = to_feats[:, x * NY : (x + 1) * NY]
+        mine = to_feats[x // XS][:, (x % XS) * NY : (x % XS + 1) * NY]
         half_x = 0.5 * (to_sx + mine[0:8])
         half_y = 0.5 * (to_sy + mine[8:16])
         to_north = bend_y + half_y
@@ -453,28 +468,14 @@
     to_last = to_east[NX - 1]
     to_first = to_west[0]
 
-    sums = sums[0:128] + sums[128:256]
-    total = jnp.zeros((16, HID), F32)
-    for level in range(2):
-        source = iota((16, 48), 1)
-        target = iota((16, 48), 0)
-        feature = (source < 32) & ((source & 15) == 2 * target + level) & (target < FEAT)
-        gather = feature | ((source == 32) & (target == FEAT))
-        total += lax.dot_general(
-            gather.astype(F32),
-            sums[level * HID : (level + 1) * HID],
-            (((1,), (1,)), ((), ())),
-            precision=lax.Precision.HIGHEST,
-            preferred_element_type=F32,
-        )
-    out_total = lax.dot_general(
-        jnp.ones((8, 128), F32),
-        out_sums[0:HID] + out_sums[HID:],
-        (((1,), (1,)), ((), ())),
-        precision=lax.Precision.HIGHEST,
-        preferred_element_type=F32,
+    sums = (sums[:, 0:128] + sums[:, 128:256]) * outr_ref[...]
+    pairs_ref[...] = sums[0:16] + sums[16:32]
+    features = pairs_ref[pl.ds(0, 8, stride=2), :] + pltpu.roll(
+        pairs_ref[pl.ds(1, 8, stride=2), :], HID, 1
     )
-    packed = pack(total[0:8], total[8:9], out_total[0:1])
+    bias = sums[32:40] + pltpu.roll(sums[32:40], HID, 1)
+    out_total = jnp.sum(jnp.transpose(out_sums[0:HID] + out_sums[HID:]), 0, keepdims=True)
+    packed = pack(features[:, 0:HID], bias[0:1, 0:HID], out_total)
     for j in range(count):
         send_ref[j, 0:8, :] = first_own
         send_ref[j, 8:16, :] = last_own
@@ -609,27 +610,29 @@
     got = lax.all_to_all(send, "gx", 0, 0, tiled=True)
     low = lax.ppermute(last, "gy", [(i, (i + 1) % count_y) for i in range(count_y)])
     high = lax.ppermute(first, "gy", [((i + 1) % count_y, i) for i in range(count_y)])
-    forward, back, outw = pl.pallas_call(
+    forward, back, outw, outr = pl.pallas_call(
         network_kernel,
         out_shape=(
             jax.ShapeDtypeStruct((2 * HID, 128), BF16),
             jax.ShapeDtypeStruct((32, 256), BF16),
             tile(2 * HID, 128),
+            tile(48, 128),
         ),
         compiler_params=params(),
     )(closure_in.T, closure_out.reshape(1, HID))
-    adj = pl.pallas_call(adjoint_kernel, out_shape=lines, compiler_params=params())(
-        got, cot, wets, right, recip
-    )
+    adj, slope_x, curve_x = pl.pallas_call(
+        adjoint_kernel, out_shape=(lines,) * 3, compiler_params=params()
+    )(got, cot, wets, right, recip, fields)
     feats_shape = jax.ShapeDtypeStruct((80, NX * NY), BF16)
-    stencil = pl.pallas_call(
-        stencil_kernel, out_shape=(lines,) * 4 + (feats_shape,), compiler_params=params()
-    )(got, low, high, fields)
+    slope_y, curve_y, feats = pl.pallas_call(
+        stencil_kernel, out_shape=(lines,) * 2 + (feats_shape,), compiler_params=params()
+    )(low, high, fields, slope_x)
     send, rhs, grad, rims = pl.pallas_call(
         closure_kernel,
         out_shape=(tile(count_x, 32, NY), lines, lines, tile(2, ROWS, NY)),
+        scratch_shapes=[pltpu.VMEM((16, 128), F32)],
         compiler_params=params(),
-    )(got, fields, wets, adj, *stencil, forward, back, outw, right, recip, left)
+    )(got, fields, wets, adj, slope_x, slope_y, curve_x, curve_y, feats, forward, back, outw, outr, right, recip, left)
     second = lax.all_to_all(send, "gx", 0, 0, tiled=True)
     send, final = pl.pallas_call(
         share_kernel,

time: 48.8 us -> 48.3 us (0.990)
    all_to_all x1, waiting for transfers between devices: 0.96 us -> 3.49 us  [per_device(): got = lax.all_to_all(send, 'gx', 0, 0, tiled=True)]
    ppermute x1, waiting for transfers between devices: 1.92 us -> 0.01 us  [per_device(): lax.ppermute(first, 'gy', [((i + 1) % count_y, i) for i in range(count_y)])]
    ppermute x1, waiting for transfers between devices: 0.61 us -> 0.01 us  [per_device(): lax.ppermute(last, 'gy', [(i, (i + 1) % count_y) for i in range(count_y)])]
  transfers between devices with their start and end apart: 3 -> 3, of which waited for: 3 -> 1; matrix products, arithmetic and copies ran while one was open for 0% -> 0% of each run, Pallas kernels for 1% -> 1%
where the time goes in v4:
time: 48.3 us; the launch traced here: 48 us
  blocking collectives  30.2 us (63%)
  Pallas kernels  6.46 us (13%)
  starting transfers between devices  6.46 us (13%)
  waiting for transfers between devices  3.5 us (7%)
  between operations  0.68 us (1%)
  local copies, waits for them, and re-layouts  0.66 us (1%)
    all_to_all x1, blocking collectives, per_device(): third = lax.all_to_all(send, 'gy', 0, 0, tiled=True)  20.7 us
    all_to_all x1, blocking collectives, per_device(): second = lax.all_to_all(send, 'gx', 0, 0, tiled=True)  9.5 us
    all_to_all x1, starting transfers between devices, per_device(): got = lax.all_to_all(send, 'gx', 0, 0, tiled=True)  4.43 us
    all_to_all x1, waiting for transfers between devices, per_device(): got = lax.all_to_all(send, 'gx', 0, 0, tiled=True)  3.49 us
    pallas_call x1, Pallas kernels, per_device(): pl.pallas_call(closure_kernel, out_shape=(tile(count_x, 32, NY), lines, l...  2.42 us
    ppermute x1, starting transfers between devices, per_device(): lax.ppermute(last, 'gy', [(i, (i + 1) % count_y) for i in range(count_y)])  1.92 us
    pallas_call x1, Pallas kernels, per_device(): pl.pallas_call(load_kernel, in_specs=[in_hbm] * 5, out_shape=(lines, tile...  1.11 us
    pallas_call x1, Pallas kernels, per_device(): pl.pallas_call(factor_kernel, out_shape=(tile(count_x, 40, NY),) + (lines...  1.04 us
  transfers between devices with their start and end apart: 3, of which 1 were waited for; matrix products, arithmetic and copies ran while one was open for 0% of the time, Pallas kernels for 1%

profile of v4, /device:TPU:32, one launch (start us, length us, event | category | flops | bytes accessed | tf_op | source)
XLA Modules:
  0.0 48.0 jit_solution(7104487121017006211)
XLA Ops:
  0.6 1.1 %shard_map.94 = (f32[32,8,128]{2,1,0:T(8,128)S(1)}, f32[8,128]{1,0:T(8,128)S(1)}, f32[8,128]{1,0:T(8,128)S(1)}, f32[64,128]{1,0:T(8,128)S(1)}, s32[32,128]{1,0:T...) custom-call(f32[256,128]{1,0:T(8,128)} %bitcast.10, f32[64,128]{1,0:T(8,128)} %bitcast.12, s32[32,128]{1,0:T(8,128)} %sea_hbm.1, ...), custom_call_target="tpu_custom_call" | custom-call | tf_op jit(solution)/shard_map/pallas_call | solution.py:584
  1.7 1.0 %shard_map.95 = (f32[8,40,128]{2,1,0:T(8,128)}, f32[32,8,128]{2,1,0:T(8,128)S(1)}, f32[32,8,128]{2,1,0:T(8,128)S(1)}, f32[32,8,128]{2,1,0:T(8,128)S(1)}, f32[32,8,128]{2,1,0:T(8,128)S(1)}) custom-call(f32[32,8,128]{2,1,0:T(8,128)S(1)} %get-tuple-element.34.fields_ref.lines_ref, f32[64,128]{1,0:T(8,128)S(1)} %get-tuple-element.35.diff_ref, ...), custom_call_target="tpu_custom_call" | custom-call | tf_op jit(solution)/shard_map/pallas_call | solution.py:605
  2.8 0.0 copy-start
  2.8 4.4 %all-to-all-start = ((f32[8,40,128]{2,1,0:T(8,128)}), f32[8,40,128]{2,1,0:T(8,128)S(1)}, u32[]{:S(2)}, u32[]{:S(2)}) async-start(f32[8,40,128]{2,1,0:T(8,128)} %get-tuple-element.39), calls=%async_computation | async-start | bytes 327680 | tf_op jit(solution)/shard_map/all_to_all | solution.py:610
  7.2 1.9 %collective-permute-start = (f32[8,128]{1,0:T(8,128)S(1)}, f32[8,128]{1,0:T(8,128)S(1)}, u32[]{:S(2)}, u32[]{:S(2)}) collective-permute-start(f32[8,128]{1,0:T(8,128)S(1)} %get-tuple-element.45), channel_id=1, source_target_pairs={{0,1},{1,2},{2,3},{3,4},{4,5},{5,6},{6,7},{7,8},{8,9},{9,10},{10,1... | collective-permute-start | bytes 12296 | tf_op jit(solution)/shard_map/ppermute | solution.py:611
  9.1 0.1 collective-permute-start.1
  9.2 0.0 copy-start.1
  9.2 0.0 copy-done
  9.3 0.7 %copy-done.1 = f32[64]{0:T(128)S(1)} copy-done((f32[64]{0:T(128)S(1)}, f32[64]{0:T(128)}, u32[]{:S(2)}) %copy-start.1) | copy-done | bytes 280
  9.9 0.3 shard_map.98
  10.2 3.5 %all-to-all-done.got_ref = f32[8,40,128]{2,1,0:T(8,128)S(1)} async-done(((f32[8,40,128]{2,1,0:T(8,128)}), f32[8,40,128]{2,1,0:T(8,128)S(1)}, u32[]{:S(2)}, u32[]{:S(2)}) %all-to-all-start) | async-done | bytes 163872 | tf_op jit(solution)/shard_map/all_to_all | solution.py:610
  13.7 0.3 shard_map.96
  14.0 0.0 collective-permute-done.low_ref
  14.0 0.0 collective-permute-done.1.high_ref
  14.0 0.2 shard_map.97
  14.2 2.4 %shard_map.99 = (f32[8,32,128]{2,1,0:T(8,128)S(1)}, f32[32,8,128]{2,1,0:T(8,128)S(1)}, f32[32,8,128]{2,1,0:T(8,128)S(1)}, f32[2,8,128]{2,1,0:T(8,128)S(1)}) custom-call(f32[8,40,128]{2,1,0:T(8,128)S(1)} %all-to-all-done.got_ref, f32[32,8,128]{2,1,0:T(8,128)S(1)} %get-tuple-element.34.fields_ref.lines_ref, f32[32,8,128]{2,1,0:T(8,128)S(1)} %get-tuple-element.40.wets_ref.wets, ...), custom_call_target="tpu_custom_call" | custom-call | tf_op jit(solution)/shard_map/pallas_call | solution.py:630
  16.6 9.5 %all_to_all.15.second_ref.refs_1_ = f32[8,32,128]{2,1,0:T(8,128)S(1)} all-to-all(f32[8,32,128]{2,1,0:T(8,128)S(1)} %get-tuple-element.56), channel_id=1, replica_groups=mesh['gx'=8,'gy'=32] {'gx'}, dimensions={0} | all-to-all | bytes 262144 | tf_op jit(solution)/shard_map/all_to_all | solution.py:636
  26.1 0.3 shard_map.100
  26.4 20.7 %all_to_all.16.refs_0_ = f32[32,8,128]{2,1,0:T(8,128)S(1)} all-to-all(f32[32,8,128]{2,1,0:T(8,128)S(1)} %get-tuple-element.59), channel_id=1, replica_groups=mesh['gx'=8,'gy'=32] {'gy'}, dimensions={0} | all-to-all | bytes 262144 | tf_op jit(solution)/shard_map/all_to_all | solution.py:642
  47.1 0.9 %shard_map.101 = (f32[256,128]{1,0:T(8,128)}, f32[256,128]{1,0:T(8,128)}, f32[10,64]{1,0:T(8,128)}) custom-call(f32[32,8,128]{2,1,0:T(8,128)S(1)} %all_to_all.16.refs_0_, f32[8,32,128]{2,1,0:T(8,128)S(1)} %all_to_all.15.second_ref.refs_1_, f32[32,8,128]{2,1,0:T(8,128)S(1)} %get-tuple-element.60.refs_2_, f32[256,128]{1,0:T(8,128)S(1)} %get-tuple-element.61.refs_3_), custom_call_target="tpu_custom_call" | custom-call | tf_op jit(solution)/shard_map/pallas_call | solution.py:648
Async XLA Ops:
  2.8 6.5 %copy-start = (f32[64,9]{0,1:T(8,128)S(1)}, f32[64,9]{0,1:T(8,128)}, u32[]{:S(2)}) copy-start(f32[64,9]{0,1:T(8,128)} %param.11) | copy-start | bytes 6916
  2.8 10.9 %all-to-all-start = ((f32[8,40,128]{2,1,0:T(8,128)}), f32[8,40,128]{2,1,0:T(8,128)S(1)}, u32[]{:S(2)}, u32[]{:S(2)}) async-start(f32[8,40,128]{2,1,0:T(8,128)} %get-tuple-element.39), calls=%async_computation | async-start | bytes 327680 | tf_op jit(solution)/shard_map/all_to_all | solution.py:610
  7.2 6.7 %collective-permute-start = (f32[8,128]{1,0:T(8,128)S(1)}, f32[8,128]{1,0:T(8,128)S(1)}, u32[]{:S(2)}, u32[]{:S(2)}) collective-permute-start(f32[8,128]{1,0:T(8,128)S(1)} %get-tuple-element.45), channel_id=1, source_target_pairs={{0,1},{1,2},{2,3},{3,4},{4,5},{5,6},{6,7},{7,8},{8,9},{9,10},{10,1... | collective-permute-start | bytes 12296 | tf_op jit(solution)/shard_map/ppermute | solution.py:611
  9.1 4.8 %collective-permute-start.1 = (f32[8,128]{1,0:T(8,128)S(1)}, f32[8,128]{1,0:T(8,128)S(1)}, u32[]{:S(2)}, u32[]{:S(2)}) collective-permute-start(f32[8,128]{1,0:T(8,128)S(1)} %get-tuple-element.46), channel_id=1, source_target_pairs={{1,0},{2,1},{3,2},{4,3},{5,4},{6,5},{7,6},{8,7},{9,8},{10,9},{11,1... | collective-permute-start | bytes 12296 | tf_op jit(solution)/shard_map/ppermute | solution.py:612
  9.2 0.7 %copy-start.1 = (f32[64]{0:T(128)S(1)}, f32[64]{0:T(128)}, u32[]{:S(2)}) copy-start(f32[64]{0:T(128)} %param.12) | copy-start | bytes 772

commit v5 on v4

--- a/solution.py
+++ b/solution.py
@@ -115,8 +115,6 @@
     left_ref,
     wets_ref,
 ):
-    me = lax.axis_index("gx")
-    count = send_ref.shape[0]
     row = rows8()
     wet = [wet_line(sea_ref, depth_ref, x) for x in range(NX)]
     for x in range(NX):
@@ -164,28 +162,89 @@
         jnp.where(upper, first_self, across),
         jnp.where(upper, last_self, jnp.where(row < 4, bare[NX - 1], wet[0])),
     ]
-    own_last = fields_ref[NX - 1]
-    own_first = fields_ref[0]
-    for j in range(count):
-        for n, tile in enumerate(tiles):
-            send_ref[j, ROWS * n : ROWS * (n + 1), :] = tile
-        send_ref[j, ROWS * 4 :, :] = jnp.where(j > me, own_last, own_first)
-
-
-def reduced(got_ref):
-    count = got_ref.shape[0]
+    tiles += [fields_ref[0], fields_ref[NX - 1]]
+    for n, tile in enumerate(tiles):
+        send_ref[ROWS * n : ROWS * (n + 1), :] = tile
+
+
+def two_port(responses, far_response):
     upper = (rows8() & 2) == 0
-    first_self, across, last_self, bare, wet = [], [], [], [], []
-    for j in range(count):
-        tile = got_ref[j, 16:24, :]
-        first_self.append(jnp.where(upper, tile, pltpu.roll(tile, 2, 0)))
-        across.append(jnp.where(upper, pltpu.roll(tile, 6, 0), tile))
-        tile = got_ref[j, 24:32, :]
-        last_self.append(jnp.where(upper, tile, pltpu.roll(tile, 2, 0)))
-        bare.append(by_level(got_ref[j, 26:27, :], got_ref[j, 27:28, :]))
-        wet.append(by_level(got_ref[j, 30:31, :], got_ref[j, 31:32, :]))
-    face = [rates8() * bare[j] * wet[j + 1] for j in range(count - 1)]
-    return first_self, across, last_self, face
+    return (
+        jnp.where(upper, responses, pltpu.roll(responses, 2, 0)),
+        jnp.where(upper, pltpu.roll(responses, 6, 0), responses),
+        jnp.where(upper, far_response, pltpu.roll(far_response, 2, 0)),
+        by_level(far_response[2:3], far_response[3:4]),
+        by_level(far_response[6:7], far_response[7:8]),
+    )
+
+
+def side_by_side(own_ref, other_ref, start, stop):
+    own, other = own_ref[start:stop, :], other_ref[start:stop, :]
+    core = lax.axis_index("gx") & 1
+    return jnp.where(core == 0, own, other), jnp.where(core == 0, other, own)
+
+
+def middle_face(own_ref, other_ref):
+    responses = side_by_side(own_ref, other_ref, 16, 24)
+    far = side_by_side(own_ref, other_ref, 24, 32)
+    left = two_port(responses[0], far[0])
+    right = two_port(responses[1], far[1])
+    face = rates8() * left[3] * right[4]
+    return left, right, face / (1.0 + face * (left[2] + right[0])), far
+
+
+def chip_values(left, right, link, first, last):
+    flux = link * (last[0] - first[1])
+    return first[0] - left[1] * flux, last[1] + right[1] * flux
+
+
+def own_fluxes(left, right, link, first, last, outer):
+    flux = link * (last[0] - first[1] + left[1] * outer[0] - right[1] * outer[1])
+    core = lax.axis_index("gx") & 1
+    return jnp.where(core == 0, outer[0], flux), jnp.where(core == 0, -flux, outer[1])
+
+
+def gather_chips(chips_ref, own, before, after, far):
+    me = lax.axis_index("gx") >> 1
+    count = chips_ref.shape[0]
+    chips_ref[me] = own
+    chips_ref[(me + count - 1) & (count - 1)] = before
+    chips_ref[(me + 1) & (count - 1)] = after
+    chips_ref[(me + 2) & (count - 1)] = far
+
+
+def reduced(chips_ref):
+    count = chips_ref.shape[0]
+    ports = [two_port(chips_ref[j, 16:24, :], chips_ref[j, 24:32, :]) for j in range(count)]
+    face = [rates8() * ports[j][3] * ports[j + 1][4] for j in range(count - 1)]
+    return [p[0] for p in ports], [p[1] for p in ports], [p[2] for p in ports], face
+
+
+def merge_kernel(own_ref, other_ref, up_ref, down_ref, far_ref):
+    left, right, link, far = middle_face(own_ref, other_ref)
+    values = chip_values(
+        left,
+        right,
+        link,
+        side_by_side(own_ref, other_ref, 0, 8),
+        side_by_side(own_ref, other_ref, 8, 16),
+    )
+    row = rows8()
+    upper = (row & 2) == 0
+    tiles = [
+        values[0],
+        values[1],
+        jnp.where(upper, left[0] - link * left[1] * left[1], link * left[1] * right[1]),
+        jnp.where(
+            upper, right[2] - link * right[1] * right[1], jnp.where(row < 4, far[1], far[0])
+        ),
+        jnp.where(upper, link * left[1], link * right[1]),
+    ]
+    for n, tile in enumerate(tiles):
+        for ref in (up_ref, down_ref, far_ref):
+            ref[ROWS * n : ROWS * (n + 1), :] = tile
+    up_ref[40:48, :] = other_ref[40:48, :]
+    down_ref[40:48, :] = other_ref[32:40, :]
 
 
 def end_fluxes(system, first, last, me):
@@ -285,13 +344,28 @@
 
 
 def adjoint_kernel(
-    got_ref, cot_ref, wets_ref, right_ref, recip_ref, lines_ref, adj_ref, slope_x, curve_x
+    own_ref,
+    other_ref,
+    chip_ref,
+    before_ref,
+    after_ref,
+    far_ref,
+    cot_ref,
+    wets_ref,
+    right_ref,
+    recip_ref,
+    lines_ref,
+    adj_ref,
+    slope_x,
+    curve_x,
+    chips_ref,
 ):
     me = lax.axis_index("gx")
-    count = got_ref.shape[0]
+    count = lax.axis_size("gx")
+    core = me & 1
     zero = jnp.zeros((ROWS, NY), F32)
-    below = got_ref[jnp.maximum(me - 1, 0), 32:40, :]
-    above = got_ref[jnp.minimum(me + 1, count - 1), 32:40, :]
+    below = jnp.where(core == 0, before_ref[40:48, :], other_ref[40:48, :])
+    above = jnp.where(core == 0, other_ref[32:40, :], after_ref[40:48, :])
     below = jnp.where(me > 0, below, zero)
     above = jnp.where(me < count - 1, above, zero)
     for x in range(NX):
@@ -299,10 +373,22 @@
         west = lines_ref[x - 1] if x else below
         slope_x[x] = 0.5 * (east - west)
         curve_x[x] = east - 2.0 * lines_ref[x] + west
-    system = reduced(got_ref)
-    first = [got_ref[j, 0:8, :] for j in range(count)]
-    last = [got_ref[j, 8:16, :] for j in range(count)]
-    fluxes = end_fluxes(system, first, last, me)
+    gather_chips(
+        chips_ref, chip_ref[...], before_ref[0:40, :], after_ref[0:40, :], far_ref[...]
+    )
+    count = chips_ref.shape[0]
+    first = [chips_ref[j, 0:8, :] for j in range(count)]
+    last = [chips_ref[j, 8:16, :] for j in range(count)]
+    outer = end_fluxes(reduced(chips_ref), first, last, me >> 1)
+    left, right, link, _ = middle_face(own_ref, other_ref)
+    fluxes = own_fluxes(
+        left,
+        right,
+        link,
+        side_by_side(own_ref, other_ref, 0, 8),
+        side_by_side(own_ref, other_ref, 8, 16),
+        outer,
+    )
 
     def keep(x, value):
         adj_ref[x] = wets_ref[x] * value
@@ -337,7 +423,7 @@
 
 
 def closure_kernel(
-    got_ref,
+    own_ref,
     lines_ref,
     wets,
     adj,
@@ -359,8 +445,6 @@
     rims_ref,
     pairs_ref,
 ):
-    me = lax.axis_index("gx")
-    count = got_ref.shape[0]
     here_y = lax.axis_index("gy")
     total_y = NY * lax.axis_size("gy")
     lanes = lanes8()
@@ -433,7 +517,7 @@
             )
 
     first_own = load_back * jnp.where(
-        (row & 2) == 0, got_ref[me, 16:24, :], pltpu.roll(got_ref[me, 16:24, :], 2, 0)
+        (row & 2) == 0, own_ref[16:24, :], pltpu.roll(own_ref[16:24, :], 2, 0)
     )
     last_own = load * recip_ref[NX - 1]
 
@@ -476,7 +560,8 @@
     bias = sums[32:40] + pltpu.roll(sums[32:40], HID, 1)
     out_total = jnp.sum(jnp.transpose(out_sums[0:HID] + out_sums[HID:]), 0, keepdims=True)
     packed = pack(features[:, 0:HID], bias[0:1, 0:HID], out_total)
-    for j in range(count):
+    me = lax.axis_index("gx")
+    for j in range(send_ref.shape[0]):
         send_ref[j, 0:8, :] = first_own
         send_ref[j, 8:16, :] = last_own
         send_ref[j, 16:24, :] = packed
@@ -484,24 +569,55 @@
 
 
 def share_kernel(
-    second_ref, rims_ref, got_ref, rhs_ref, right_ref, recip_ref, send_ref, final_ref
+    own_ref,
+    other_ref,
+    chips_ref,
+    second_ref,
+    rims_ref,
+    rhs_ref,
+    right_ref,
+    recip_ref,
+    send_ref,
+    final_ref,
+    sides_ref,
 ):
     me_y = lax.axis_index("gy")
     me = lax.axis_index("gx")
-    count = got_ref.shape[0]
+    blocks = second_ref.shape[0]
     lanes = lanes8()
+    zero = jnp.zeros((ROWS, NY), F32)
     total = second_ref[0, 16:24, :]
-    for j in range(1, count):
+    for j in range(1, blocks):
         total = total + second_ref[j, 16:24, :]
     rim = (lanes >= RIM) & (lanes < RIM + NX)
     upward = jnp.where(rim, rims_ref[0], total)
     downward = jnp.where(rim, rims_ref[1], total)
     for j in range(send_ref.shape[0]):
         send_ref[j] = jnp.where(j > me_y, upward, downward)
-    system = reduced(got_ref)
-    first = [second_ref[j, 0:8, :] for j in range(count)]
-    last = [second_ref[j, 8:16, :] for j in range(count)]
-    fluxes = end_fluxes(system, first, last, me)
+    below = second_ref[jnp.maximum(me - 1, 0), 24:32, :]
+    above = second_ref[jnp.minimum(me + 1, blocks - 1), 24:32, :]
+    sides_ref[0] = jnp.where(me > 0, below, zero)
+    sides_ref[1] = jnp.where(me < blocks - 1, above, zero)
+    upper = (rows8() & 2) == 0
+    first, last = [], []
+    for j in range(chips_ref.shape[0]):
+        pulls = chips_ref[j, 32:40, :]
+        gap = second_ref[2 * j, 8:16, :] - second_ref[2 * j + 1, 0:8, :]
+        left_pull = jnp.where(upper, pulls, pltpu.roll(pulls, 2, 0))
+        right_pull = jnp.where(upper, pltpu.roll(pulls, 6, 0), pulls)
+        first.append(second_ref[2 * j, 0:8, :] - left_pull * gap)
+        last.append(second_ref[2 * j + 1, 8:16, :] + right_pull * gap)
+    outer = end_fluxes(reduced(chips_ref), first, last, me >> 1)
+    left, right, link, _ = middle_face(own_ref, other_ref)
+    pair = me & (blocks - 2)
+    fluxes = own_fluxes(
+        left,
+        right,
+        link,
+        (second_ref[pair, 0:8, :], second_ref[pair + 1, 0:8, :]),
+        (second_ref[pair, 8:16, :], second_ref[pair + 1, 8:16, :]),
+        outer,
+    )
 
     def keep(x, value):
         final_ref[pl.ds(x, ROWS, stride=NX), :] = value
@@ -512,7 +628,7 @@
 def finish_kernel(
     factor,
     third_ref,
-    second_ref,
+    sides_ref,
     grad_ref,
     final_ref,
     final_hbm,
@@ -524,9 +640,7 @@
 ):
     copies = [pltpu.make_async_copy(final_ref, final_hbm, sems.at[0])]
     copies[0].start()
-    me_x = lax.axis_index("gx")
     me_y = lax.axis_index("gy")
-    count_x = second_ref.shape[0]
     count_y = third_ref.shape[0]
     lanes = lanes8()
     zero = jnp.zeros((ROWS, NY), F32)
@@ -541,18 +655,14 @@
         )
     copies.append(pltpu.make_async_copy(closure_ref, closure_hbm, sems.at[1]))
     copies[1].start()
-    before = jnp.where(me_x > 0, second_ref[jnp.maximum(me_x - 1, 0), 24:32, :], zero)
-    after = jnp.where(
-        me_x < count_x - 1, second_ref[jnp.minimum(me_x + 1, count_x - 1), 24:32, :], zero
-    )
     south = jnp.where(me_y > 0, third_ref[jnp.maximum(me_y - 1, 0)], zero)
     north = jnp.where(me_y < count_y - 1, third_ref[jnp.minimum(me_y + 1, count_y - 1)], zero)
     for x in range(NX):
         value = grad_ref[x]
         if x == 0:
-            value = value + before
+            value = value + sides_ref[0]
         if x == NX - 1:
-            value = value + after
+            value = value + sides_ref[1]
         value = value + jnp.where(lanes == 0, pltpu.roll(south, NY - RIM - x, 1), 0.0)
         value = value + jnp.where(lanes == NY - 1, pltpu.roll(north, NY - 1 - RIM - x, 1), 0.0)
         out_ref[pl.ds(x, ROWS, stride=NX), :] = value
@@ -564,6 +674,14 @@
 
 def tile(*shape):
     return jax.ShapeDtypeStruct(shape, F32)
+
+
+def along_x(up, down, far):
+    count = lax.axis_size("gx")
+    return tuple(
+        lax.ppermute(values, "gx", [(i, (i + shift) % count) for i in range(count)])
+        for values, shift in ((up, 2), (down, count - 2), (far, 4))
+    )
 
 
 def keep_in_hbm(values):
@@ -602,12 +720,18 @@
         keep_in_hbm(depth_index),
         keep_in_hbm(cotangent.reshape(ROWS * NX, NY)),
     )
-    send, right, recip, left, wets = pl.pallas_call(
+    own, right, recip, left, wets = pl.pallas_call(
         factor_kernel,
-        out_shape=(tile(count_x, 40, NY),) + (lines,) * 4,
+        out_shape=(tile(48, NY),) + (lines,) * 4,
         compiler_params=params(),
     )(fields, diff, sea, depth, cot)
-    got = lax.all_to_all(send, "gx", 0, 0, tiled=True)
+    other = lax.ppermute(own, "gx", [(i, i ^ 1) for i in range(count_x)])
+    up, down, chip = pl.pallas_call(
+        merge_kernel,
+        out_shape=(tile(48, NY), tile(48, NY), tile(40, NY)),
+        compiler_params=params(),
+    )(own, other)
+    before, after, far = along_x(up, down, chip)
     low = lax.ppermute(last, "gy", [(i, (i + 1) % count_y) for i in range(count_y)])
     high = lax.ppermute(first, "gy", [((i + 1) % count_y, i) for i in range(count_y)])
     forward, back, outw, outr = pl.pallas_call(
@@ -620,9 +744,12 @@
         ),
         compiler_params=params(),
     )(closure_in.T, closure_out.reshape(1, HID))
-    adj, slope_x, curve_x = pl.pallas_call(
-        adjoint_kernel, out_shape=(lines,) * 3, compiler_params=params()
-    )(got, cot, wets, right, recip, fields)
+    chips_x = count_x // 2
+    adj, slope_x, curve_x, chips = pl.pallas_call(
+        adjoint_kernel,
+        out_shape=(lines,) * 3 + (tile(chips_x, 40, NY),),
+        compiler_params=params(),
+    )(own, other, chip, before, after, far, cot, wets, right, recip, fields)
     feats_shape = jax.ShapeDtypeStruct((80, NX * NY), BF16)
     slope_y, curve_y, feats = pl.pallas_call(
         stencil_kernel, out_shape=(lines,) * 2 + (feats_shape,), compiler_params=params()
@@ -632,13 +759,13 @@
         out_shape=(tile(count_x, 32, NY), lines, lines, tile(2, ROWS, NY)),
         scratch_shapes=[pltpu.VMEM((16, 128), F32)],
         compiler_params=params(),
-    )(got, fields, wets, adj, slope_x, slope_y, curve_x, curve_y, feats, forward, back, outw, outr, right, recip, left)
+    )(own, fields, wets, adj, slope_x, slope_y, curve_x, curve_y, feats, forward, back, outw, outr, right, recip, left)
     second = lax.all_to_all(send, "gx", 0, 0, tiled=True)
-    send, final = pl.pallas_call(
+    send, final, sides = pl.pallas_call(
         share_kernel,
-        out_shape=(tile(count_y, ROWS, NY), tile(ROWS * NX, NY)),
+        out_shape=(tile(count_y, ROWS, NY), tile(ROWS * NX, NY), tile(2, ROWS, NY)),
         compiler_params=params(),
-    )(second, rims, got, rhs, right, recip)
+    )(own, other, chips, second, rims, rhs, right, recip)
     third = lax.all_to_all(send, "gy", 0, 0, tiled=True)
     factor = 1.0 / math.sqrt(2 * NX * count_x * NY * count_y)
 
@@ -656,7 +783,7 @@
             pltpu.SemaphoreType.DMA((3,)),
         ],
         compiler_params=params(),
-    )(third, second, grad, final)
+    )(third, sides, grad, final)
     return (final.reshape(state.shape), state_grad.reshape(state.shape), closure_grad.T)
 
 

time: 48.3 us -> 47.7 us (0.988)
  starting transfers between devices: 6.46 us -> 7.25 us
  Pallas kernels: 6.46 us -> 5.77 us
  blocking collectives: 30.2 us -> 29.6 us
    ppermute x0 -> x4, starting transfers between devices: none -> 5.22 us  [the longest x3 5.13 us: along_x(): lax.ppermute(values, 'gx', [(i, (i + shift) % count) for i in range(count)])]
    all_to_all x1 -> x0, starting transfers between devices: 4.43 us -> none  [per_device(): got = lax.all_to_all(send, 'gx', 0, 0, tiled=True)]
    all_to_all x1 -> x0, waiting for transfers between devices: 3.49 us -> none  [per_device(): got = lax.all_to_all(send, 'gx', 0, 0, tiled=True)]
    ppermute x1, waiting for transfers between devices: 0.01 us -> 1.82 us  [per_device(): lax.ppermute(first, 'gy', [((i + 1) % count_y, i) for i in range(count_y)])]
    ppermute x0 -> x4, waiting for transfers between devices: none -> 1.66 us  [the longest x1 1.18 us: per_device(): other = lax.ppermute(own, 'gx', [(i, i ^ 1) for i in range(count_x)])]
    pallas_call x2 -> x3, Pallas kernels: 1.29 us -> 0.63 us  [the longest x1 0.4 us: per_device(): pl.pallas_call(factor_kernel, out_shape=(tile(48, NY),) + (lines,) * 4, c...]
    all_to_all x1, blocking collectives: 9.5 us -> 8.92 us  [per_device(): second = lax.all_to_all(send, 'gx', 0, 0, tiled=True)]
  transfers between devices with their start and end apart: 3 -> 6, of which waited for: 1 -> 3; matrix products, arithmetic and copies ran while one was open for 0% -> 0% of each run, Pallas kernels for 1% -> 1%
where the time goes in v5:
time: 47.7 us; the launch traced here: 47.5 us
  blocking collectives  29.6 us (62%)
  starting transfers between devices  7.25 us (15%)
  Pallas kernels  5.77 us (12%)
  waiting for transfers between devices  3.49 us (7%)
  between operations  0.7 us (1%)
  local copies, waits for them, and re-layouts  0.66 us (1%)
    all_to_all x1, blocking collectives, per_device(): third = lax.all_to_all(send, 'gy', 0, 0, tiled=True)  20.7 us
    all_to_all x1, blocking collectives, per_device(): second = lax.all_to_all(send, 'gx', 0, 0, tiled=True)  8.92 us
    ppermute x3, starting transfers between devices, along_x(): lax.ppermute(values, 'gx', [(i, (i + shift) % count) for i in range(count)])  5.13 us
    pallas_call x1, Pallas kernels, per_device(): pl.pallas_call(closure_kernel, out_shape=(tile(count_x, 32, NY), lines, l...  2.45 us
    ppermute x1, starting transfers between devices, per_device(): lax.ppermute(last, 'gy', [(i, (i + 1) % count_y) for i in range(count_y)])  1.92 us
    ppermute x1, waiting for transfers between devices, per_device(): lax.ppermute(first, 'gy', [((i + 1) % count_y, i) for i in range(count_y)])  1.82 us
    ppermute x1, waiting for transfers between devices, per_device(): other = lax.ppermute(own, 'gx', [(i, i ^ 1) for i in range(count_x)])  1.18 us
    pallas_call x1, Pallas kernels, per_device(): pl.pallas_call(load_kernel, in_specs=[in_hbm] * 5, out_shape=(lines, tile...  1.11 us
  transfers between devices with their start and end apart: 6, of which 3 were waited for; matrix products, arithmetic and copies ran while one was open for 0% of the time, Pallas kernels for 1%

profile of v5, /device:TPU:32, one launch (start us, length us, event | category | flops | bytes accessed | tf_op | source)
XLA Modules:
  0.0 47.5 jit_solution(3971867320294653509)
XLA Ops:
  0.6 1.1 %shard_map.94 = (f32[32,8,128]{2,1,0:T(8,128)S(1)}, f32[8,128]{1,0:T(8,128)S(1)}, f32[8,128]{1,0:T(8,128)S(1)}, f32[64,128]{1,0:T(8,128)S(1)}, s32[32,128]{1,0:T...) custom-call(f32[256,128]{1,0:T(8,128)} %bitcast.10, f32[64,128]{1,0:T(8,128)} %bitcast.12, s32[32,128]{1,0:T(8,128)} %sea_hbm.1, ...), custom_call_target="tpu_custom_call" | custom-call | tf_op jit(solution)/shard_map/pallas_call | solution.py:702
  1.7 0.4 shard_map.95
  2.1 0.1 collective-permute-start
  2.3 1.2 %collective-permute-done.other_ref = f32[48,128]{1,0:T(8,128)S(1)} collective-permute-done((f32[48,128]{1,0:T(8,128)S(1)}, f32[48,128]{1,0:T(8,128)S(1)}, u32[]{:S(2)}, u32[]{:S(2)}) %collective-permute-start) | collective-permute-done | bytes 24608 | tf_op jit(solution)/shard_map/ppermute | solution.py:728
  3.5 0.0 copy-start
  3.5 1.6 %collective-permute-start.1 = (f32[48,128]{1,0:T(8,128)S(1)}, f32[48,128]{1,0:T(8,128)S(1)}, u32[]{:S(2)}, u32[]{:S(2)}) collective-permute-start(f32[48,128]{1,0:T(8,128)S(1)} %get-tuple-element.46), channel_id=1, source_target_pairs={{0,64},{32,96},{64,128},{96,160},{128,192},{160,224},{192,0},{224,... | collective-permute-start | bytes 73736 | tf_op jit(solution)/shard_map/ppermute | solution.py:682
  5.0 1.7 %collective-permute-start.2 = (f32[48,128]{1,0:T(8,128)S(1)}, f32[48,128]{1,0:T(8,128)S(1)}, u32[]{:S(2)}, u32[]{:S(2)}) collective-permute-start(f32[48,128]{1,0:T(8,128)S(1)} %get-tuple-element.47), channel_id=1, source_target_pairs={{0,192},{32,224},{64,0},{96,32},{128,64},{160,96},{192,128},{224,1... | collective-permute-start | bytes 73736 | tf_op jit(solution)/shard_map/ppermute | solution.py:682
  6.8 1.8 %collective-permute-start.3 = (f32[40,128]{1,0:T(8,128)S(1)}, f32[40,128]{1,0:T(8,128)S(1)}, u32[]{:S(2)}, u32[]{:S(2)}) collective-permute-start(f32[40,128]{1,0:T(8,128)S(1)} %get-tuple-element.45.chip_ref), channel_id=1, source_target_pairs={{0,128},{32,160},{64,192},{96,224},{128,0},{160,32},{192,64},{224,... | collective-permute-start | bytes 61448 | tf_op jit(solution)/shard_map/ppermute | solution.py:682
  8.6 1.9 %collective-permute-start.4 = (f32[8,128]{1,0:T(8,128)S(1)}, f32[8,128]{1,0:T(8,128)S(1)}, u32[]{:S(2)}, u32[]{:S(2)}) collective-permute-start(f32[8,128]{1,0:T(8,128)S(1)} %get-tuple-element.54), channel_id=1, source_target_pairs={{0,1},{1,2},{2,3},{3,4},{4,5},{5,6},{6,7},{7,8},{8,9},{9,10},{10,1... | collective-permute-start | bytes 12296 | tf_op jit(solution)/shard_map/ppermute | solution.py:735
  10.5 0.1 collective-permute-start.5
  10.6 0.0 copy-start.1
  10.6 0.0 copy-done
  10.6 0.7 %copy-done.1 = f32[64]{0:T(128)S(1)} copy-done((f32[64]{0:T(128)S(1)}, f32[64]{0:T(128)}, u32[]{:S(2)}) %copy-start.1) | copy-done | bytes 280
  11.3 0.3 shard_map.99
  11.6 0.5 %collective-permute-done.3.far_ref = f32[40,128]{1,0:T(8,128)S(1)} collective-permute-done((f32[40,128]{1,0:T(8,128)S(1)}, f32[40,128]{1,0:T(8,128)S(1)}, u32[]{:S(2)}, u32[]{:S(2)}) %collective-permute-start.3) | collective-permute-done | bytes 20512 | tf_op jit(solution)/shard_map/ppermute | solution.py:682
  12.1 0.0 collective-permute-done.1.before_ref
  12.1 0.0 collective-permute-done.2.after_ref
  12.1 0.2 shard_map.97
  12.3 0.0 collective-permute-done.4.low_ref
  12.3 1.8 %collective-permute-done.5.high_ref = f32[8,128]{1,0:T(8,128)S(1)} collective-permute-done((f32[8,128]{1,0:T(8,128)S(1)}, f32[8,128]{1,0:T(8,128)S(1)}, u32[]{:S(2)}, u32[]{:S(2)}) %collective-permute-start.5) | collective-permute-done | bytes 4128 | tf_op jit(solution)/shard_map/ppermute | solution.py:736
  14.1 0.2 shard_map.98
  14.3 2.5 %shard_map.100 = (f32[8,32,128]{2,1,0:T(8,128)S(1)}, f32[32,8,128]{2,1,0:T(8,128)S(1)}, f32[32,8,128]{2,1,0:T(8,128)S(1)}, f32[2,8,128]{2,1,0:T(8,128)S(1)}) custom-call(f32[48,128]{1,0:T(8,128)S(1)} %get-tuple-element.44.own_ref, f32[32,8,128]{2,1,0:T(8,128)S(1)} %get-tuple-element.39.fields_ref.lines_ref, ...), custom_call_target="tpu_custom_call" | custom-call | tf_op jit(solution)/shard_map/pallas_call | solution.py:757
  16.8 8.9 %all_to_all.10.second_ref = f32[8,32,128]{2,1,0:T(8,128)S(1)} all-to-all(f32[8,32,128]{2,1,0:T(8,128)S(1)} %get-tuple-element.65), channel_id=1, replica_groups=mesh['gx'=8,'gy'=32] {'gx'}, dimensions={0} | all-to-all | bytes 262144 | tf_op jit(solution)/shard_map/all_to_all | solution.py:763
  25.7 0.2 shard_map.101
  25.9 20.7 %all_to_all.11.refs_0_ = f32[32,8,128]{2,1,0:T(8,128)S(1)} all-to-all(f32[32,8,128]{2,1,0:T(8,128)S(1)} %get-tuple-element.68), channel_id=1, replica_groups=mesh['gx'=8,'gy'=32] {'gy'}, dimensions={0} | all-to-all | bytes 262144 | tf_op jit(solution)/shard_map/all_to_all | solution.py:769
  46.6 0.9 %shard_map.102 = (f32[256,128]{1,0:T(8,128)}, f32[256,128]{1,0:T(8,128)}, f32[10,64]{1,0:T(8,128)}) custom-call(f32[32,8,128]{2,1,0:T(8,128)S(1)} %all_to_all.11.refs_0_, f32[2,8,128]{2,1,0:T(8,128)S(1)} %get-tuple-element.69.refs_1_, f32[32,8,128]{2,1,0:T(8,128)S(1)} %get-tuple-element.70.refs_2_, f32[256,128]{1,0:T(8,128)S(1)} %get-tuple-element.71.refs_3_), custom_call_target="tpu_custom_call" | custom-call | tf_op jit(solution)/shard_map/pallas_call | solution.py:775
  (1 shorter events, 0.0 us)
Async XLA Ops:
  2.1 1.3 %collective-permute-start = (f32[48,128]{1,0:T(8,128)S(1)}, f32[48,128]{1,0:T(8,128)S(1)}, u32[]{:S(2)}, u32[]{:S(2)}) collective-permute-start(f32[48,128]{1,0:T(8,128)S(1)} %get-tuple-element.44.own_ref), channel_id=1, source_target_pairs={{0,32},{32,0},{64,96},{96,64},{128,160},{160,128},{192,224},{224,1... | collective-permute-start | bytes 73736 | tf_op jit(solution)/shard_map/ppermute | solution.py:728
  3.5 7.2 %copy-start = (f32[64,9]{0,1:T(8,128)S(1)}, f32[64,9]{0,1:T(8,128)}, u32[]{:S(2)}) copy-start(f32[64,9]{0,1:T(8,128)} %param.11) | copy-start | bytes 6916
  3.5 8.6 %collective-permute-start.1 = (f32[48,128]{1,0:T(8,128)S(1)}, f32[48,128]{1,0:T(8,128)S(1)}, u32[]{:S(2)}, u32[]{:S(2)}) collective-permute-start(f32[48,128]{1,0:T(8,128)S(1)} %get-tuple-element.46), channel_id=1, source_target_pairs={{0,64},{32,96},{64,128},{96,160},{128,192},{160,224},{192,0},{224,... | collective-permute-start | bytes 73736 | tf_op jit(solution)/shard_map/ppermute | solution.py:682
  5.0 7.0 %collective-permute-start.2 = (f32[48,128]{1,0:T(8,128)S(1)}, f32[48,128]{1,0:T(8,128)S(1)}, u32[]{:S(2)}, u32[]{:S(2)}) collective-permute-start(f32[48,128]{1,0:T(8,128)S(1)} %get-tuple-element.47), channel_id=1, source_target_pairs={{0,192},{32,224},{64,0},{96,32},{128,64},{160,96},{192,128},{224,1... | collective-permute-start | bytes 73736 | tf_op jit(solution)/shard_map/ppermute | solution.py:682
  6.8 5.3 %collective-permute-start.3 = (f32[40,128]{1,0:T(8,128)S(1)}, f32[40,128]{1,0:T(8,128)S(1)}, u32[]{:S(2)}, u32[]{:S(2)}) collective-permute-start(f32[40,128]{1,0:T(8,128)S(1)} %get-tuple-element.45.chip_ref), channel_id=1, source_target_pairs={{0,128},{32,160},{64,192},{96,224},{128,0},{160,32},{192,64},{224,... | collective-permute-start | bytes 61448 | tf_op jit(solution)/shard_map/ppermute | solution.py:682
  8.6 3.7 %collective-permute-start.4 = (f32[8,128]{1,0:T(8,128)S(1)}, f32[8,128]{1,0:T(8,128)S(1)}, u32[]{:S(2)}, u32[]{:S(2)}) collective-permute-start(f32[8,128]{1,0:T(8,128)S(1)} %get-tuple-element.54), channel_id=1, source_target_pairs={{0,1},{1,2},{2,3},{3,4},{4,5},{5,6},{6,7},{7,8},{8,9},{9,10},{10,1... | collective-permute-start | bytes 12296 | tf_op jit(solution)/shard_map/ppermute | solution.py:735
  10.5 3.6 %collective-permute-start.5 = (f32[8,128]{1,0:T(8,128)S(1)}, f32[8,128]{1,0:T(8,128)S(1)}, u32[]{:S(2)}, u32[]{:S(2)}) collective-permute-start(f32[8,128]{1,0:T(8,128)S(1)} %get-tuple-element.55), channel_id=1, source_target_pairs={{1,0},{2,1},{3,2},{4,3},{5,4},{6,5},{7,6},{8,7},{9,8},{10,9},{11,1... | collective-permute-start | bytes 12296 | tf_op jit(solution)/shard_map/ppermute | solution.py:736
  10.6 0.7 %copy-start.1 = (f32[64]{0:T(128)S(1)}, f32[64]{0:T(128)}, u32[]{:S(2)}) copy-start(f32[64]{0:T(128)} %param.12) | copy-start | bytes 772

commit v6 on v5

--- a/solution.py
+++ b/solution.py
@@ -14,7 +14,7 @@
 HID = 64
 NX = 32
 NY = 128
-XS = 8
+XS = 4
 ROWS = 8
 RIM = 64
 
@@ -453,16 +453,64 @@
     turn = 0.3 * (0.5 + 0.5 * places / total_y)
     moment = row < 4
     outw = outw_ref[...]
-    sharp, keepers, to_feats = [], [], []
-    sums = jnp.zeros((48, 256), F32)
+    sharp, keepers = [], []
+    waiting, partial_sums = [], []
+    rim_north = [jnp.zeros((ROWS, NY), F32)]
+    rim_south = [jnp.zeros((ROWS, NY), F32)]
+    to_east, to_west, kept = [], [], []
+
+    def ahead(x):
+        return jnp.dot(
+            forward_ref[:, 0:80],
+            feats[:, x * NY : (x + XS) * NY],
+            preferred_element_type=F32,
+        )
+
+    def finish(x):
+        stacked = waiting.pop()
+        back = jnp.dot(back_ref[...], stacked, preferred_element_type=F32)
+        back = back[0:16] + back[16:32]
+        partial_sums.append(
+            lax.dot_general(
+                feats[0:48, x * NY : (x + XS) * NY],
+                stacked,
+                (((1,), (1,)), ((), ())),
+                preferred_element_type=F32,
+            )
+        )
+
+        for i in range(XS):
+            lane = RIM + x + i
+            to_sx, to_sy, bend_x, bend_y, middle = keepers[x + i]
+            mine = back[:, i * NY : (i + 1) * NY]
+            half_x = 0.5 * (to_sx + mine[0:8])
+            half_y = 0.5 * (to_sy + mine[8:16])
+            to_north = bend_y + half_y
+            to_south = bend_y - half_y
+            rim_north[0] = jnp.where(lanes == lane, pltpu.roll(to_north, lane + 1, 1), rim_north[0])
+            rim_south[0] = jnp.where(lanes == lane, pltpu.roll(to_south, lane, 1), rim_south[0])
+            to_east.append(bend_x + half_x)
+            to_west.append(bend_x - half_x)
+            kept.append(
+                middle
+                + jnp.where(lanes == 0, 0.0, pltpu.roll(to_north, 1, 1))
+                + jnp.where(lanes == NY - 1, 0.0, pltpu.roll(to_south, NY - 1, 1))
+            )
+            done = x + i - 1
+            if done >= 0:
+                total = kept[done] + to_west[done + 1]
+                grad_ref[done] = total + to_east[done - 1] if done else total
+
+    before = ahead(0)
     out_sums = jnp.zeros((2 * HID, NY), F32)
     load = load_back = jnp.zeros((ROWS, NY), F32)
     for x in range(NX):
         if x % XS == 0:
-            place = slice(x * NY, (x + XS) * NY)
-            hidden = jnp.tanh(
-                jnp.dot(forward_ref[:, 0:80], feats[:, place], preferred_element_type=F32)
-            )
+            hidden = jnp.tanh(before)
+            if x + XS < NX:
+                before = ahead(x + XS)
+            if x:
+                finish(x - XS)
         unit = hidden[:, (x % XS) * NY : (x % XS + 1) * NY]
         weighed = unit * outw
         mixed = by_level(
@@ -508,47 +556,19 @@
         middle = g + jnp.where(moment, untwist, 0.0) - 2.0 * (bend_x + bend_y)
         keepers.append((-0.3 * u * g, -0.3 * v * g, bend_x, bend_y, middle))
         if x % XS == XS - 1:
-            stacked = jnp.concatenate(split(jnp.concatenate(sharp, 1)), 0)
+            waiting.append(jnp.concatenate(split(jnp.concatenate(sharp, 1)), 0))
             sharp = []
-            back = jnp.dot(back_ref[...], stacked, preferred_element_type=F32)
-            to_feats.append(back[0:16] + back[16:32])
-            sums = sums + lax.dot_general(
-                feats[0:48, place], stacked, (((1,), (1,)), ((), ())), preferred_element_type=F32
-            )
+    finish(NX - XS)
+    grad_ref[NX - 1] = kept[NX - 1] + to_east[NX - 2]
+    sums = sum(partial_sums)
 
     first_own = load_back * jnp.where(
         (row & 2) == 0, own_ref[16:24, :], pltpu.roll(own_ref[16:24, :], 2, 0)
     )
     last_own = load * recip_ref[NX - 1]
 
-    rim_north = jnp.zeros((ROWS, NY), F32)
-    rim_south = jnp.zeros((ROWS, NY), F32)
-    to_east, to_west, kept = [], [], []
-    for x in range(NX):
-        to_sx, to_sy, bend_x, bend_y, middle = keepers[x]
-        mine = to_feats[x // XS][:, (x % XS) * NY : (x % XS + 1) * NY]
-        half_x = 0.5 * (to_sx + mine[0:8])
-        half_y = 0.5 * (to_sy + mine[8:16])
-        to_north = bend_y + half_y
-        to_south = bend_y - half_y
-        rim_north = jnp.where(lanes == RIM + x, pltpu.roll(to_north, RIM + x + 1, 1), rim_north)
-        rim_south = jnp.where(lanes == RIM + x, pltpu.roll(to_south, RIM + x, 1), rim_south)
-        to_east.append(bend_x + half_x)
-        to_west.append(bend_x - half_x)
-        kept.append(
-            middle
-            + jnp.where(lanes == 0, 0.0, pltpu.roll(to_north, 1, 1))
-            + jnp.where(lanes == NY - 1, 0.0, pltpu.roll(to_south, NY - 1, 1))
-        )
-    for x in range(NX):
-        total = kept[x]
-        if x:
-            total = total + to_east[x - 1]
-        if x < NX - 1:
-            total = total + to_west[x + 1]
-        grad_ref[x] = total
-    rims_ref[0] = rim_north
-    rims_ref[1] = rim_south
+    rims_ref[0] = rim_north[0]
+    rims_ref[1] = rim_south[0]
     to_last = to_east[NX - 1]
     to_first = to_west[0]
 

time: 47.7 us -> 47.5 us (level)
  no operation moved by 1% of the time
where the time goes in v6:
time: 47.5 us; the launch traced here: 47.3 us
  blocking collectives  29.6 us (62%)
  starting transfers between devices  7.25 us (15%)
  Pallas kernels  5.56 us (12%)
  waiting for transfers between devices  3.49 us (7%)
  between operations  0.7 us (1%)
  local copies, waits for them, and re-layouts  0.66 us (1%)
    all_to_all x1, blocking collectives, per_device(): third = lax.all_to_all(send, 'gy', 0, 0, tiled=True)  20.7 us
    all_to_all x1, blocking collectives, per_device(): second = lax.all_to_all(send, 'gx', 0, 0, tiled=True)  8.92 us
    ppermute x3, starting transfers between devices, along_x(): lax.ppermute(values, 'gx', [(i, (i + shift) % count) for i in range(count)])  5.13 us
    pallas_call x1, Pallas kernels, per_device(): pl.pallas_call(closure_kernel, out_shape=(tile(count_x, 32, NY), lines, l...  2.23 us
    ppermute x1, starting transfers between devices, per_device(): lax.ppermute(last, 'gy', [(i, (i + 1) % count_y) for i in range(count_y)])  1.92 us
    ppermute x1, waiting for transfers between devices, per_device(): lax.ppermute(first, 'gy', [((i + 1) % count_y, i) for i in range(count_y)])  1.82 us
    ppermute x1, waiting for transfers between devices, per_device(): other = lax.ppermute(own, 'gx', [(i, i ^ 1) for i in range(count_x)])  1.18 us
    pallas_call x1, Pallas kernels, per_device(): pl.pallas_call(load_kernel, in_specs=[in_hbm] * 5, out_shape=(lines, tile...  1.11 us
  transfers between devices with their start and end apart: 6, of which 3 were waited for; matrix products, arithmetic and copies ran while one was open for 0% of the time, Pallas kernels for 1%

profile of v6, /device:TPU:32, one launch (start us, length us, event | category | flops | bytes accessed | tf_op | source)
XLA Modules:
  0.0 47.3 jit_solution(3430976552229987647)
XLA Ops:
  0.6 1.1 %shard_map.94 = (f32[32,8,128]{2,1,0:T(8,128)S(1)}, f32[8,128]{1,0:T(8,128)S(1)}, f32[8,128]{1,0:T(8,128)S(1)}, f32[64,128]{1,0:T(8,128)S(1)}, s32[32,128]{1,0:T...) custom-call(f32[256,128]{1,0:T(8,128)} %bitcast.10, f32[64,128]{1,0:T(8,128)} %bitcast.12, s32[32,128]{1,0:T(8,128)} %sea_hbm.1, ...), custom_call_target="tpu_custom_call" | custom-call | tf_op jit(solution)/shard_map/pallas_call | solution.py:722
  1.7 0.4 shard_map.95
  2.1 0.1 collective-permute-start
  2.3 1.2 %collective-permute-done.other_ref = f32[48,128]{1,0:T(8,128)S(1)} collective-permute-done((f32[48,128]{1,0:T(8,128)S(1)}, f32[48,128]{1,0:T(8,128)S(1)}, u32[]{:S(2)}, u32[]{:S(2)}) %collective-permute-start) | collective-permute-done | bytes 24608 | tf_op jit(solution)/shard_map/ppermute | solution.py:748
  3.5 0.0 copy-start
  3.5 1.6 %collective-permute-start.1 = (f32[48,128]{1,0:T(8,128)S(1)}, f32[48,128]{1,0:T(8,128)S(1)}, u32[]{:S(2)}, u32[]{:S(2)}) collective-permute-start(f32[48,128]{1,0:T(8,128)S(1)} %get-tuple-element.46), channel_id=1, source_target_pairs={{0,64},{32,96},{64,128},{96,160},{128,192},{160,224},{192,0},{224,... | collective-permute-start | bytes 73736 | tf_op jit(solution)/shard_map/ppermute | solution.py:702
  5.0 1.7 %collective-permute-start.2 = (f32[48,128]{1,0:T(8,128)S(1)}, f32[48,128]{1,0:T(8,128)S(1)}, u32[]{:S(2)}, u32[]{:S(2)}) collective-permute-start(f32[48,128]{1,0:T(8,128)S(1)} %get-tuple-element.47), channel_id=1, source_target_pairs={{0,192},{32,224},{64,0},{96,32},{128,64},{160,96},{192,128},{224,1... | collective-permute-start | bytes 73736 | tf_op jit(solution)/shard_map/ppermute | solution.py:702
  6.8 1.8 %collective-permute-start.3 = (f32[40,128]{1,0:T(8,128)S(1)}, f32[40,128]{1,0:T(8,128)S(1)}, u32[]{:S(2)}, u32[]{:S(2)}) collective-permute-start(f32[40,128]{1,0:T(8,128)S(1)} %get-tuple-element.45.chip_ref), channel_id=1, source_target_pairs={{0,128},{32,160},{64,192},{96,224},{128,0},{160,32},{192,64},{224,... | collective-permute-start | bytes 61448 | tf_op jit(solution)/shard_map/ppermute | solution.py:702
  8.6 1.9 %collective-permute-start.4 = (f32[8,128]{1,0:T(8,128)S(1)}, f32[8,128]{1,0:T(8,128)S(1)}, u32[]{:S(2)}, u32[]{:S(2)}) collective-permute-start(f32[8,128]{1,0:T(8,128)S(1)} %get-tuple-element.54), channel_id=1, source_target_pairs={{0,1},{1,2},{2,3},{3,4},{4,5},{5,6},{6,7},{7,8},{8,9},{9,10},{10,1... | collective-permute-start | bytes 12296 | tf_op jit(solution)/shard_map/ppermute | solution.py:755
  10.5 0.1 collective-permute-start.5
  10.6 0.0 copy-start.1
  10.6 0.0 copy-done
  10.6 0.7 %copy-done.1 = f32[64]{0:T(128)S(1)} copy-done((f32[64]{0:T(128)S(1)}, f32[64]{0:T(128)}, u32[]{:S(2)}) %copy-start.1) | copy-done | bytes 280
  11.3 0.3 shard_map.99
  11.6 0.5 %collective-permute-done.3.far_ref = f32[40,128]{1,0:T(8,128)S(1)} collective-permute-done((f32[40,128]{1,0:T(8,128)S(1)}, f32[40,128]{1,0:T(8,128)S(1)}, u32[]{:S(2)}, u32[]{:S(2)}) %collective-permute-start.3) | collective-permute-done | bytes 20512 | tf_op jit(solution)/shard_map/ppermute | solution.py:702
  12.1 0.0 collective-permute-done.1.before_ref
  12.1 0.0 collective-permute-done.2.after_ref
  12.1 0.2 shard_map.97
  12.3 0.0 collective-permute-done.4.low_ref
  12.3 1.8 %collective-permute-done.5.high_ref = f32[8,128]{1,0:T(8,128)S(1)} collective-permute-done((f32[8,128]{1,0:T(8,128)S(1)}, f32[8,128]{1,0:T(8,128)S(1)}, u32[]{:S(2)}, u32[]{:S(2)}) %collective-permute-start.5) | collective-permute-done | bytes 4128 | tf_op jit(solution)/shard_map/ppermute | solution.py:756
  14.1 0.2 shard_map.98
  14.3 2.2 %shard_map.100 = (f32[8,32,128]{2,1,0:T(8,128)S(1)}, f32[32,8,128]{2,1,0:T(8,128)S(1)}, f32[32,8,128]{2,1,0:T(8,128)S(1)}, f32[2,8,128]{2,1,0:T(8,128)S(1)}) custom-call(f32[48,128]{1,0:T(8,128)S(1)} %get-tuple-element.44.own_ref, f32[32,8,128]{2,1,0:T(8,128)S(1)} %get-tuple-element.39.fields_ref.lines_ref, ...), custom_call_target="tpu_custom_call" | custom-call | tf_op jit(solution)/shard_map/pallas_call | solution.py:777
  16.6 8.9 %all_to_all.10.second_ref = f32[8,32,128]{2,1,0:T(8,128)S(1)} all-to-all(f32[8,32,128]{2,1,0:T(8,128)S(1)} %get-tuple-element.65), channel_id=1, replica_groups=mesh['gx'=8,'gy'=32] {'gx'}, dimensions={0} | all-to-all | bytes 262144 | tf_op jit(solution)/shard_map/all_to_all | solution.py:783
  25.5 0.2 shard_map.101
  25.7 20.7 %all_to_all.11.refs_0_ = f32[32,8,128]{2,1,0:T(8,128)S(1)} all-to-all(f32[32,8,128]{2,1,0:T(8,128)S(1)} %get-tuple-element.68), channel_id=1, replica_groups=mesh['gx'=8,'gy'=32] {'gy'}, dimensions={0} | all-to-all | bytes 262144 | tf_op jit(solution)/shard_map/all_to_all | solution.py:789
  46.4 0.9 %shard_map.102 = (f32[256,128]{1,0:T(8,128)}, f32[256,128]{1,0:T(8,128)}, f32[10,64]{1,0:T(8,128)}) custom-call(f32[32,8,128]{2,1,0:T(8,128)S(1)} %all_to_all.11.refs_0_, f32[2,8,128]{2,1,0:T(8,128)S(1)} %get-tuple-element.69.refs_1_, f32[32,8,128]{2,1,0:T(8,128)S(1)} %get-tuple-element.70.refs_2_, f32[256,128]{1,0:T(8,128)S(1)} %get-tuple-element.71.refs_3_), custom_call_target="tpu_custom_call" | custom-call | tf_op jit(solution)/shard_map/pallas_call | solution.py:795
  (1 shorter events, 0.0 us)
Async XLA Ops:
  2.1 1.3 %collective-permute-start = (f32[48,128]{1,0:T(8,128)S(1)}, f32[48,128]{1,0:T(8,128)S(1)}, u32[]{:S(2)}, u32[]{:S(2)}) collective-permute-start(f32[48,128]{1,0:T(8,128)S(1)} %get-tuple-element.44.own_ref), channel_id=1, source_target_pairs={{0,32},{32,0},{64,96},{96,64},{128,160},{160,128},{192,224},{224,1... | collective-permute-start | bytes 73736 | tf_op jit(solution)/shard_map/ppermute | solution.py:748
  3.5 7.2 %copy-start = (f32[64,9]{0,1:T(8,128)S(1)}, f32[64,9]{0,1:T(8,128)}, u32[]{:S(2)}) copy-start(f32[64,9]{0,1:T(8,128)} %param.11) | copy-start | bytes 6916
  3.5 8.6 %collective-permute-start.1 = (f32[48,128]{1,0:T(8,128)S(1)}, f32[48,128]{1,0:T(8,128)S(1)}, u32[]{:S(2)}, u32[]{:S(2)}) collective-permute-start(f32[48,128]{1,0:T(8,128)S(1)} %get-tuple-element.46), channel_id=1, source_target_pairs={{0,64},{32,96},{64,128},{96,160},{128,192},{160,224},{192,0},{224,... | collective-permute-start | bytes 73736 | tf_op jit(solution)/shard_map/ppermute | solution.py:702
  5.0 7.0 %collective-permute-start.2 = (f32[48,128]{1,0:T(8,128)S(1)}, f32[48,128]{1,0:T(8,128)S(1)}, u32[]{:S(2)}, u32[]{:S(2)}) collective-permute-start(f32[48,128]{1,0:T(8,128)S(1)} %get-tuple-element.47), channel_id=1, source_target_pairs={{0,192},{32,224},{64,0},{96,32},{128,64},{160,96},{192,128},{224,1... | collective-permute-start | bytes 73736 | tf_op jit(solution)/shard_map/ppermute | solution.py:702
  6.8 5.3 %collective-permute-start.3 = (f32[40,128]{1,0:T(8,128)S(1)}, f32[40,128]{1,0:T(8,128)S(1)}, u32[]{:S(2)}, u32[]{:S(2)}) collective-permute-start(f32[40,128]{1,0:T(8,128)S(1)} %get-tuple-element.45.chip_ref), channel_id=1, source_target_pairs={{0,128},{32,160},{64,192},{96,224},{128,0},{160,32},{192,64},{224,... | collective-permute-start | bytes 61448 | tf_op jit(solution)/shard_map/ppermute | solution.py:702
  8.6 3.7 %collective-permute-start.4 = (f32[8,128]{1,0:T(8,128)S(1)}, f32[8,128]{1,0:T(8,128)S(1)}, u32[]{:S(2)}, u32[]{:S(2)}) collective-permute-start(f32[8,128]{1,0:T(8,128)S(1)} %get-tuple-element.54), channel_id=1, source_target_pairs={{0,1},{1,2},{2,3},{3,4},{4,5},{5,6},{6,7},{7,8},{8,9},{9,10},{10,1... | collective-permute-start | bytes 12296 | tf_op jit(solution)/shard_map/ppermute | solution.py:755
  10.5 3.6 %collective-permute-start.5 = (f32[8,128]{1,0:T(8,128)S(1)}, f32[8,128]{1,0:T(8,128)S(1)}, u32[]{:S(2)}, u32[]{:S(2)}) collective-permute-start(f32[8,128]{1,0:T(8,128)S(1)} %get-tuple-element.55), channel_id=1, source_target_pairs={{1,0},{2,1},{3,2},{4,3},{5,4},{6,5},{7,6},{8,7},{9,8},{10,9},{11,1... | collective-permute-start | bytes 12296 | tf_op jit(solution)/shard_map/ppermute | solution.py:756
  10.6 0.7 %copy-start.1 = (f32[64]{0:T(128)S(1)}, f32[64]{0:T(128)}, u32[]{:S(2)}) copy-start(f32[64]{0:T(128)} %param.12) | copy-start | bytes 772

commit v7 on v6

--- a/solution.py
+++ b/solution.py
@@ -664,17 +664,6 @@
     count_y = third_ref.shape[0]
     lanes = lanes8()
     zero = jnp.zeros((ROWS, NY), F32)
-    parts = [third_ref[j] for j in range(count_y)]
-    while len(parts) > 1:
-        parts = [a + b for a, b in zip(parts[::2], parts[1::2])]
-    total = parts[0] * factor
-    closure_ref[0:8, :] = total[:, 0:HID]
-    for n in range(2):
-        closure_ref[8 + n : 9 + n, :] = jnp.concatenate(
-            [total[2 * n : 2 * n + 1, 96:], total[2 * n + 1 : 2 * n + 2, 96:]], 1
-        )
-    copies.append(pltpu.make_async_copy(closure_ref, closure_hbm, sems.at[1]))
-    copies[1].start()
     south = jnp.where(me_y > 0, third_ref[jnp.maximum(me_y - 1, 0)], zero)
     north = jnp.where(me_y < count_y - 1, third_ref[jnp.minimum(me_y + 1, count_y - 1)], zero)
     for x in range(NX):
@@ -687,6 +676,17 @@
         value = value + jnp.where(lanes == NY - 1, pltpu.roll(north, NY - 1 - RIM - x, 1), 0.0)
         out_ref[pl.ds(x, ROWS, stride=NX), :] = value
     copies.append(pltpu.make_async_copy(out_ref, out_hbm, sems.at[2]))
+    copies[1].start()
+    parts = [third_ref[j] for j in range(count_y)]
+    while len(parts) > 1:
+        parts = [a + b for a, b in zip(parts[::2], parts[1::2])]
+    total = parts[0] * factor
+    closure_ref[0:8, :] = total[:, 0:HID]
+    for n in range(2):
+        closure_ref[8 + n : 9 + n, :] = jnp.concatenate(
+            [total[2 * n : 2 * n + 1, 96:], total[2 * n + 1 : 2 * n + 2, 96:]], 1
+        )
+    copies.append(pltpu.make_async_copy(closure_ref, closure_hbm, sems.at[1]))
     copies[2].start()
     for copy in copies:
         copy.wait()

time: 47.5 us -> 47.5 us (level)
  no operation moved by 1% of the time
where the time goes in v7:
time: 47.5 us; the launch traced here: 47.3 us
  blocking collectives  29.6 us (62%)
  starting transfers between devices  7.25 us (15%)
  Pallas kernels  5.55 us (12%)
  waiting for transfers between devices  3.49 us (7%)
  between operations  0.7 us (1%)
  local copies, waits for them, and re-layouts  0.66 us (1%)
    all_to_all x1, blocking collectives, per_device(): third = lax.all_to_all(send, 'gy', 0, 0, tiled=True)  20.7 us
    all_to_all x1, blocking collectives, per_device(): second = lax.all_to_all(send, 'gx', 0, 0, tiled=True)  8.92 us
    ppermute x3, starting transfers between devices, along_x(): lax.ppermute(values, 'gx', [(i, (i + shift) % count) for i in range(count)])  5.13 us
    pallas_call x1, Pallas kernels, per_device(): pl.pallas_call(closure_kernel, out_shape=(tile(count_x, 32, NY), lines, l...  2.23 us
    ppermute x1, starting transfers between devices, per_device(): lax.ppermute(last, 'gy', [(i, (i + 1) % count_y) for i in range(count_y)])  1.92 us
    ppermute x1, waiting for transfers between devices, per_device(): lax.ppermute(first, 'gy', [((i + 1) % count_y, i) for i in range(count_y)])  1.82 us
    ppermute x1, waiting for transfers between devices, per_device(): other = lax.ppermute(own, 'gx', [(i, i ^ 1) for i in range(count_x)])  1.18 us
    pallas_call x1, Pallas kernels, per_device(): pl.pallas_call(load_kernel, in_specs=[in_hbm] * 5, out_shape=(lines, tile...  1.11 us
  transfers between devices with their start and end apart: 6, of which 3 were waited for; matrix products, arithmetic and copies ran while one was open for 0% of the time, Pallas kernels for 1%

profile of v7, /device:TPU:32, one launch (start us, length us, event | category | flops | bytes accessed | tf_op | source)
XLA Modules:
  0.0 47.3 jit_solution(16230596102777989940)
XLA Ops:
  0.6 1.1 %shard_map.94 = (f32[32,8,128]{2,1,0:T(8,128)S(1)}, f32[8,128]{1,0:T(8,128)S(1)}, f32[8,128]{1,0:T(8,128)S(1)}, f32[64,128]{1,0:T(8,128)S(1)}, s32[32,128]{1,0:T...) custom-call(f32[256,128]{1,0:T(8,128)} %bitcast.10, f32[64,128]{1,0:T(8,128)} %bitcast.12, s32[32,128]{1,0:T(8,128)} %sea_hbm.1, ...), custom_call_target="tpu_custom_call" | custom-call | tf_op jit(solution)/shard_map/pallas_call | solution.py:722
  1.7 0.4 shard_map.95
  2.1 0.1 collective-permute-start
  2.3 1.2 %collective-permute-done.other_ref = f32[48,128]{1,0:T(8,128)S(1)} collective-permute-done((f32[48,128]{1,0:T(8,128)S(1)}, f32[48,128]{1,0:T(8,128)S(1)}, u32[]{:S(2)}, u32[]{:S(2)}) %collective-permute-start) | collective-permute-done | bytes 24608 | tf_op jit(solution)/shard_map/ppermute | solution.py:748
  3.5 0.0 copy-start
  3.5 1.6 %collective-permute-start.1 = (f32[48,128]{1,0:T(8,128)S(1)}, f32[48,128]{1,0:T(8,128)S(1)}, u32[]{:S(2)}, u32[]{:S(2)}) collective-permute-start(f32[48,128]{1,0:T(8,128)S(1)} %get-tuple-element.46), channel_id=1, source_target_pairs={{0,64},{32,96},{64,128},{96,160},{128,192},{160,224},{192,0},{224,... | collective-permute-start | bytes 73736 | tf_op jit(solution)/shard_map/ppermute | solution.py:702
  5.0 1.7 %collective-permute-start.2 = (f32[48,128]{1,0:T(8,128)S(1)}, f32[48,128]{1,0:T(8,128)S(1)}, u32[]{:S(2)}, u32[]{:S(2)}) collective-permute-start(f32[48,128]{1,0:T(8,128)S(1)} %get-tuple-element.47), channel_id=1, source_target_pairs={{0,192},{32,224},{64,0},{96,32},{128,64},{160,96},{192,128},{224,1... | collective-permute-start | bytes 73736 | tf_op jit(solution)/shard_map/ppermute | solution.py:702
  6.8 1.8 %collective-permute-start.3 = (f32[40,128]{1,0:T(8,128)S(1)}, f32[40,128]{1,0:T(8,128)S(1)}, u32[]{:S(2)}, u32[]{:S(2)}) collective-permute-start(f32[40,128]{1,0:T(8,128)S(1)} %get-tuple-element.45.chip_ref), channel_id=1, source_target_pairs={{0,128},{32,160},{64,192},{96,224},{128,0},{160,32},{192,64},{224,... | collective-permute-start | bytes 61448 | tf_op jit(solution)/shard_map/ppermute | solution.py:702
  8.6 1.9 %collective-permute-start.4 = (f32[8,128]{1,0:T(8,128)S(1)}, f32[8,128]{1,0:T(8,128)S(1)}, u32[]{:S(2)}, u32[]{:S(2)}) collective-permute-start(f32[8,128]{1,0:T(8,128)S(1)} %get-tuple-element.54), channel_id=1, source_target_pairs={{0,1},{1,2},{2,3},{3,4},{4,5},{5,6},{6,7},{7,8},{8,9},{9,10},{10,1... | collective-permute-start | bytes 12296 | tf_op jit(solution)/shard_map/ppermute | solution.py:755
  10.5 0.1 collective-permute-start.5
  10.6 0.0 copy-start.1
  10.6 0.0 copy-done
  10.6 0.7 %copy-done.1 = f32[64]{0:T(128)S(1)} copy-done((f32[64]{0:T(128)S(1)}, f32[64]{0:T(128)}, u32[]{:S(2)}) %copy-start.1) | copy-done | bytes 280
  11.3 0.3 shard_map.99
  11.6 0.5 %collective-permute-done.3.far_ref = f32[40,128]{1,0:T(8,128)S(1)} collective-permute-done((f32[40,128]{1,0:T(8,128)S(1)}, f32[40,128]{1,0:T(8,128)S(1)}, u32[]{:S(2)}, u32[]{:S(2)}) %collective-permute-start.3) | collective-permute-done | bytes 20512 | tf_op jit(solution)/shard_map/ppermute | solution.py:702
  12.1 0.0 collective-permute-done.1.before_ref
  12.1 0.0 collective-permute-done.2.after_ref
  12.1 0.2 shard_map.97
  12.3 0.0 collective-permute-done.4.low_ref
  12.3 1.8 %collective-permute-done.5.high_ref = f32[8,128]{1,0:T(8,128)S(1)} collective-permute-done((f32[8,128]{1,0:T(8,128)S(1)}, f32[8,128]{1,0:T(8,128)S(1)}, u32[]{:S(2)}, u32[]{:S(2)}) %collective-permute-start.5) | collective-permute-done | bytes 4128 | tf_op jit(solution)/shard_map/ppermute | solution.py:756
  14.1 0.2 shard_map.98
  14.3 2.2 %shard_map.100 = (f32[8,32,128]{2,1,0:T(8,128)S(1)}, f32[32,8,128]{2,1,0:T(8,128)S(1)}, f32[32,8,128]{2,1,0:T(8,128)S(1)}, f32[2,8,128]{2,1,0:T(8,128)S(1)}) custom-call(f32[48,128]{1,0:T(8,128)S(1)} %get-tuple-element.44.own_ref, f32[32,8,128]{2,1,0:T(8,128)S(1)} %get-tuple-element.39.fields_ref.lines_ref, ...), custom_call_target="tpu_custom_call" | custom-call | tf_op jit(solution)/shard_map/pallas_call | solution.py:777
  16.6 8.9 %all_to_all.10.second_ref = f32[8,32,128]{2,1,0:T(8,128)S(1)} all-to-all(f32[8,32,128]{2,1,0:T(8,128)S(1)} %get-tuple-element.65), channel_id=1, replica_groups=mesh['gx'=8,'gy'=32] {'gx'}, dimensions={0} | all-to-all | bytes 262144 | tf_op jit(solution)/shard_map/all_to_all | solution.py:783
  25.5 0.2 shard_map.101
  25.7 20.7 %all_to_all.11.refs_0_ = f32[32,8,128]{2,1,0:T(8,128)S(1)} all-to-all(f32[32,8,128]{2,1,0:T(8,128)S(1)} %get-tuple-element.68), channel_id=1, replica_groups=mesh['gx'=8,'gy'=32] {'gy'}, dimensions={0} | all-to-all | bytes 262144 | tf_op jit(solution)/shard_map/all_to_all | solution.py:789
  46.4 0.9 %shard_map.102 = (f32[256,128]{1,0:T(8,128)}, f32[256,128]{1,0:T(8,128)}, f32[10,64]{1,0:T(8,128)}) custom-call(f32[32,8,128]{2,1,0:T(8,128)S(1)} %all_to_all.11.refs_0_, f32[2,8,128]{2,1,0:T(8,128)S(1)} %get-tuple-element.69.refs_1_, f32[32,8,128]{2,1,0:T(8,128)S(1)} %get-tuple-element.70.refs_2_, f32[256,128]{1,0:T(8,128)S(1)} %get-tuple-element.71.refs_3_), custom_call_target="tpu_custom_call" | custom-call | tf_op jit(solution)/shard_map/pallas_call | solution.py:795
  (1 shorter events, 0.0 us)
Async XLA Ops:
  2.1 1.3 %collective-permute-start = (f32[48,128]{1,0:T(8,128)S(1)}, f32[48,128]{1,0:T(8,128)S(1)}, u32[]{:S(2)}, u32[]{:S(2)}) collective-permute-start(f32[48,128]{1,0:T(8,128)S(1)} %get-tuple-element.44.own_ref), channel_id=1, source_target_pairs={{0,32},{32,0},{64,96},{96,64},{128,160},{160,128},{192,224},{224,1... | collective-permute-start | bytes 73736 | tf_op jit(solution)/shard_map/ppermute | solution.py:748
  3.5 7.2 %copy-start = (f32[64,9]{0,1:T(8,128)S(1)}, f32[64,9]{0,1:T(8,128)}, u32[]{:S(2)}) copy-start(f32[64,9]{0,1:T(8,128)} %param.11) | copy-start | bytes 6916
  3.5 8.6 %collective-permute-start.1 = (f32[48,128]{1,0:T(8,128)S(1)}, f32[48,128]{1,0:T(8,128)S(1)}, u32[]{:S(2)}, u32[]{:S(2)}) collective-permute-start(f32[48,128]{1,0:T(8,128)S(1)} %get-tuple-element.46), channel_id=1, source_target_pairs={{0,64},{32,96},{64,128},{96,160},{128,192},{160,224},{192,0},{224,... | collective-permute-start | bytes 73736 | tf_op jit(solution)/shard_map/ppermute | solution.py:702
  5.0 7.0 %collective-permute-start.2 = (f32[48,128]{1,0:T(8,128)S(1)}, f32[48,128]{1,0:T(8,128)S(1)}, u32[]{:S(2)}, u32[]{:S(2)}) collective-permute-start(f32[48,128]{1,0:T(8,128)S(1)} %get-tuple-element.47), channel_id=1, source_target_pairs={{0,192},{32,224},{64,0},{96,32},{128,64},{160,96},{192,128},{224,1... | collective-permute-start | bytes 73736 | tf_op jit(solution)/shard_map/ppermute | solution.py:702
  6.8 5.3 %collective-permute-start.3 = (f32[40,128]{1,0:T(8,128)S(1)}, f32[40,128]{1,0:T(8,128)S(1)}, u32[]{:S(2)}, u32[]{:S(2)}) collective-permute-start(f32[40,128]{1,0:T(8,128)S(1)} %get-tuple-element.45.chip_ref), channel_id=1, source_target_pairs={{0,128},{32,160},{64,192},{96,224},{128,0},{160,32},{192,64},{224,... | collective-permute-start | bytes 61448 | tf_op jit(solution)/shard_map/ppermute | solution.py:702
  8.6 3.7 %collective-permute-start.4 = (f32[8,128]{1,0:T(8,128)S(1)}, f32[8,128]{1,0:T(8,128)S(1)}, u32[]{:S(2)}, u32[]{:S(2)}) collective-permute-start(f32[8,128]{1,0:T(8,128)S(1)} %get-tuple-element.54), channel_id=1, source_target_pairs={{0,1},{1,2},{2,3},{3,4},{4,5},{5,6},{6,7},{7,8},{8,9},{9,10},{10,1... | collective-permute-start | bytes 12296 | tf_op jit(solution)/shard_map/ppermute | solution.py:755
  10.5 3.6 %collective-permute-start.5 = (f32[8,128]{1,0:T(8,128)S(1)}, f32[8,128]{1,0:T(8,128)S(1)}, u32[]{:S(2)}, u32[]{:S(2)}) collective-permute-start(f32[8,128]{1,0:T(8,128)S(1)} %get-tuple-element.55), channel_id=1, source_target_pairs={{1,0},{2,1},{3,2},{4,3},{5,4},{6,5},{7,6},{8,7},{9,8},{10,9},{11,1... | collective-permute-start | bytes 12296 | tf_op jit(solution)/shard_map/ppermute | solution.py:756
  10.6 0.7 %copy-start.1 = (f32[64]{0:T(128)S(1)}, f32[64]{0:T(128)}, u32[]{:S(2)}) copy-start(f32[64]{0:T(128)} %param.12) | copy-start | bytes 772
